TPU v7x, 256 devices: a whole 4x4x8 slice. The times are simulated.
256 devices in a mesh: cache: 16 (over z, y_lo), seq: 8 (over x, core), head: 2 (over y_hi).
Axes of the slice: x: 4, y: 4 (y_hi: 2, y_lo: 2; y = y_hi * 2 + y_lo), z: 8, core: 2. Of those that a mesh axis runs over, the one named last changes fastest.
Arguments:
- hidden: bfloat16 [16, 1024, 4096], P('cache', 'seq', 'head'), may hold values from -6 to 6
- kv_weight: bfloat16 [4096, 2, 1024], P('cache', None, 'head'), may hold values from -0.09375 to 0.09375
- queries: bfloat16 [2, 16, 1024, 4096], P(None, 'cache', 'seq', 'head'), may hold values from -200 to 200, as said below
- kv_pool: bfloat16 [128, 128, 2, 1024], P('cache', None, None, 'head'), may hold values from -6 to 6
- hit_host: int32 [16, 11, 1], replicated, may hold values from 0 to 15; in each aligned block of 11 rows (0 to 10, 11 to 21, ..., all dimensions but the last counted through in order) at most 2 rows name the same one
- hit_page: int32 [16, 11], replicated, may hold values from 0 to 7
- hit_request: int32 [16, 11], replicated, may hold values from 0 to 3
- segment_ids: int32 [16, 1024], P('cache'), may hold values from 0 to 3, never falling along the last dimension, each value on 1 to 512 neighbouring positions
Outputs:
- attended: bfloat16 [2, 16, 1024, 4096], P(None, 'cache', 'seq', 'head')
- kv_new: bfloat16 [16, 1024, 2, 1024], P('cache', 'seq', None, 'head')
Inputs may be any that keep to these rules, and one draw needn't show every extreme that they name: queries are real-valued rows of order one to a few tens. `hit_host`: among the 11 hit slots of one span at most 2 name the same host, and some span has exactly 2 slots on one host. `segment_ids`: within a span the ids never fall; each of the 4 requests holds 1 to 512 tokens, one exactly that many.
All inputs are finite; a program needn't handle non-finite values.
Results may differ from a plain program's by a relative error of at most 0.012.
The roundings to bfloat16 on the way count: a program that leaves them out, or rounds other values in their place, can miss the bound.
Values may be sent and summed in bfloat16 or wider, within the bound.
No kernel may reach another device: no remote copies, remote signals or barrier semaphores. Data moves between devices by JAX's collectives and lax.ppermute only.
A program may use at most 128 MiB of HBM per device.

v0:
```python
import math

import jax
import jax.numpy as jnp
from jax import lax
from jax.sharding import PartitionSpec as P

HD = 128
CAP = 2


masked_score = -1e30
block_limit = 512


def on_device(hidden, kv_weight, queries, kv_pool, hit_host, hit_page, hit_request, segment_ids):
    features = lax.all_gather(hidden[0], "head", axis=1, tiled=True)
    tok_rows = features.shape[0]
    head_cols = kv_weight.shape[2]
    projected = jnp.einsum(
        "td,djk->tjk",
        features,
        lax.all_gather(kv_weight, "cache", axis=0, tiled=True),
        preferred_element_type=jnp.float32,
    )
    kv_local = projected.astype(jnp.bfloat16)
    host_count = lax.axis_size("cache")
    span_index = lax.axis_index("cache")
    seq_index = lax.axis_index("seq")
    owners = hit_host[:, :, 0]
    slot_count = owners.shape[1]
    slot_order = jnp.arange(slot_count)
    same_host = owners[:, :, None] == owners[:, None, :]
    before = (slot_order[:, None] < slot_order[None, :])[None]
    slot_rank = jnp.sum(same_host & before, axis=1)
    held_here = owners == span_index
    capacity_rows = jnp.arange(CAP)
    chosen = held_here[:, None, :] & (slot_rank[:, None, :] == capacity_rows[None, :, None])
    page_choice = jnp.sum(jnp.where(chosen, hit_page[:, None, :], 0), axis=2)
    filled = jnp.any(chosen, axis=2)
    my_owners = lax.dynamic_index_in_dim(owners, span_index, 0, keepdims=False)
    my_ranks = lax.dynamic_index_in_dim(slot_rank, span_index, 0, keepdims=False)
    received_slot = my_owners * CAP + my_ranks
    page_width = kv_pool.shape[1]
    pages = kv_pool[page_choice]
    packed = jnp.where(filled[:, :, None, None, None], pages, jnp.zeros_like(pages))
    arrived = lax.all_to_all(packed, "cache", split_axis=0, concat_axis=0, tiled=True)
    prefix = arrived.reshape(host_count * CAP, page_width, 2, head_cols)[received_slot]
    layers = queries.shape[0]
    query_cols = queries.shape[3]
    groups = head_cols // HD
    per_group = query_cols // head_cols
    query_heads = queries[:, 0].reshape(layers, tok_rows, groups, per_group, HD)
    my_segments = segment_ids[0]
    query_pos = seq_index * tok_rows + jnp.arange(tok_rows, dtype=jnp.int32)
    query_seg = lax.dynamic_slice_in_dim(my_segments, seq_index * tok_rows, tok_rows)
    scale = 1.0 / math.sqrt(HD)

    def attend(carry, block_keys, key_seg, key_pos):
        peak, total, weighted = carry
        allowed = (key_seg[None, :] == query_seg[:, None]) & (
            key_pos[None, :] <= query_pos[:, None]
        )
        allowed = allowed[None, :, None, None, :]
        count_keys = block_keys.shape[0]
        keys_block = block_keys[:, 0].reshape(count_keys, groups, HD)
        values_block = block_keys[:, 1].reshape(count_keys, groups, HD)
        scores = (
            jnp.einsum(
                "ltgqe,nge->ltgqn", query_heads, keys_block, preferred_element_type=jnp.float32
            )
            * scale
        )
        scores = jnp.where(allowed, scores, masked_score)
        new_peak = jnp.maximum(peak, jnp.max(scores, axis=-1))
        probs = jnp.where(allowed, jnp.exp(scores - new_peak[..., None]), 0.0)
        factor = jnp.exp(peak - new_peak)
        total = total * factor + jnp.sum(probs, axis=-1)
        weighted = weighted * factor[..., None] + jnp.einsum(
            "ltgqn,nge->ltgqe",
            probs.astype(jnp.bfloat16),
            values_block,
            preferred_element_type=jnp.float32,
        )
        return (new_peak, total, weighted)

    def attend_blocks(carry, all_keys, key_seg, key_pos):
        count_keys = all_keys.shape[0]
        for block_start in range(0, count_keys, block_limit):
            block_end = min(block_start + block_limit, count_keys)
            carry = attend(
                carry,
                all_keys[block_start:block_end],
                key_seg[block_start:block_end],
                key_pos[block_start:block_end],
            )
        return carry

    stat_shape = (layers, tok_rows, groups, per_group)
    initial = (
        jnp.full(stat_shape, masked_score, jnp.float32),
        jnp.zeros(stat_shape, jnp.float32),
        jnp.zeros(stat_shape + (HD,), jnp.float32),
    )
    my_requests = lax.dynamic_index_in_dim(hit_request, span_index, 0, keepdims=False)
    prefix_rows = prefix.reshape(-1, 2, head_cols)
    prefix_count = prefix_rows.shape[0]
    started = attend_blocks(
        initial,
        prefix_rows,
        jnp.repeat(my_requests, kv_pool.shape[1]),
        jnp.full((prefix_count,), -1, jnp.int32),
    )
    piece = lax.all_gather(kv_local, "seq", axis=0, tiled=True)
    count_keys = piece.shape[0]
    peak, total, weighted = attend_blocks(
        started, piece, my_segments, jnp.arange(count_keys, dtype=jnp.int32)
    )
    attended = (
        (weighted / total[..., None]).astype(jnp.bfloat16).reshape(layers, tok_rows, query_cols)
    )
    return (attended[:, None], kv_local[None])


def solution(mesh):
    return jax.shard_map(
        on_device,
        mesh=mesh,
        in_specs=(
            P("cache", "seq", "head"),
            P("cache", None, "head"),
            P(None, "cache", "seq", "head"),
            P("cache", None, None, "head"),
            P(),
            P(),
            P(),
            P("cache", None),
        ),
        out_specs=(P(None, "cache", "seq", "head"), P("cache", "seq", None, "head")),
        check_vma=False,
    )
```

profile of v0, /device:TPU:97, one launch (start us, length us, event | category | flops | bytes accessed | tf_op | source)
XLA Modules:
  0.0 431.7 jit_solution(11263969908555742284)
XLA Ops:
  7.2 0.7 all-gather.9.cloned.1.call-update
  8.0 1.9 copy.119
  9.9 0.7 copy.193
  10.6 0.8 copy.160
  11.3 0.7 broadcast_compare_fusion
  12.0 0.8 copy.98
  13.4 17.9 %gather_fusion = bf16[32,128,2,512]{3,2,1,0:T(2,128)(2,1)} fusion(bf16[8,128,2,512]{3,2,1,0:T(2,128)(2,1)S(1)} %copy-done, s32[1024]{0:T(1024)S(1)} %pad_clamp_fusion.1), kind=kCustom, calls=%fused_computation | custom fusion | bytes 16777344 | tf_op jit(solution)/shard_map/gather | solution.py:45
  31.3 7.7 %copy_select_fusion = bf16[16,2,128,2,512]{4,2,3,1,0:T(8,128)(2,1)} fusion(bf16[16,2,128,2,512]{4,3,2,1,0:T(2,128)(2,1)} %bitcast.201, pred[16,2]{1,0:T(8,128)(4,1)S(1)} %copy.97), kind=kLoop, calls=%fused_computation.6 | loop fusion | flops 4194304 | bytes 16777248 | tf_op jit(solution)/shard_map/jit(_where)/select_n | solution.py:46
  39.0 8.4 %all-to-all-start = ((bf16[16,2,128,2,512]{4,2,3,1,0:T(8,128)(2,1)}), bf16[16,2,128,2,512]{4,2,3,1,0:T(8,128)(2,1)}, u32[]{:S(2)}, u32[]{:S(2)}) async-start(bf16[16,2,128,2,512]{4,2,3,1,0:T(8,128)(2,1)} %copy_select_fusion), calls=%async_computation | async-start | bytes 16777216 | tf_op jit(solution)/shard_map/all_to_all | solution.py:47
  47.5 0.8 reshape_squeeze.34
  48.3 0.4 multiply_reduce_fusion
  48.7 0.7 constant_dynamic-slice_fusion.2
  49.6 304.2 %all-gather.5.cloned.1.call-done = bf16[4096,2,512]{2,0,1:T(8,128)(2,1)} async-done(((bf16[256,2,512]{2,0,1:T(8,128)(2,1)}), bf16[4096,2,512]{2,0,1:T(8,128)(2,1)}) %all-gather.5.cloned.1.call-update) | async-done | bytes 8388624 | tf_op jit(solution)/shard_map/all_gather | solution.py:23
  353.7 5.7 %convolution_convert_fusion = bf16[128,2,512]{2,0,1:T(8,128)(2,1)} fusion(bf16[4096,2,512]{2,0,1:T(8,128)(2,1)} %all-gather.5.cloned.1.call-done, bf16[1,128,4096]{2,1,0:T(8,128)(2,1)} %all-gather.9.cloned.1.call-done), kind=kOutput, calls=%fused_computation.49 | convolution fusion | flops 1073872896 | bytes 9699328 | tf_op jit(solution)/shard_map/td,djk->tjk/dot_general | solution.py:20
  359.7 0.8 compare_and_fusion.3
  360.6 1.9 copy.130
  362.5 5.9 %gather_fusion.1 = bf16[11,128,2,512]{3,1,2,0:T(8,128)(2,1)} fusion(bf16[32,128,2,512]{3,1,2,0:T(8,128)(2,1)} %bitcast.5, s32[1024]{0:T(1024)S(1)} %pad_clamp_fusion), kind=kCustom, calls=%fused_computation.1 | custom fusion | bytes 5767212 | tf_op jit(solution)/shard_map/gather | solution.py:48
  368.4 2.8 fusion.74
  371.4 0.8 fusion.78
  372.2 1.0 copy.117
  373.2 1.0 copy.105
  374.2 1.2 copy.114
  375.5 0.2 copy.102
  375.7 1.3 copy.107
  377.0 1.0 fusion.77
  378.0 2.1 copy.111
  380.1 1.3 copy.108
  381.4 3.9 fusion.12
  385.3 4.8 %fusion.1 = (f32[2,128,4,4]{1,3,0,2:T(4,128)S(1)}, f32[4,512,2,128,4]{3,1,4,2,0:T(8,128)}) fusion(pred[128,512]{0,1:T(8,128)(4,1)S(1)} %get-tuple-element.36, bf16[512,4,128,1,1]{0,2,4,3,1:T(8,128)(2,1)S(1)} %bitcast.210, bf16[2,128,4,4,128]{4,3,2,1,0:T(4,128)(2,1)S(1)} %reshape_squeeze.34), kind=kOutput, calls=%fused_computation.12 | convolution fusion | flops 543158272 | bytes 10043392 | tf_op jit(solution)/shard_map/ltgqe,nge->ltgqn/dot_general | solution.py:69
  390.1 4.8 %fusion = (f32[2,128,4,4]{1,3,0,2:T(4,128)S(1)}, f32[4,512,2,128,4]{3,1,4,2,0:T(8,128)}) fusion(pred[128,512]{0,1:T(8,128)(4,1)S(1)} %get-tuple-element.35, bf16[512,4,128,1,1]{0,2,4,3,1:T(8,128)(2,1)S(1)} %bitcast.208, bf16[2,128,4,4,128]{4,3,2,1,0:T(4,128)(2,1)S(1)} %reshape_squeeze.34), kind=kOutput, calls=%fused_computation.11 | convolution fusion | flops 543158272 | bytes 10043392 | tf_op jit(solution)/shard_map/ltgqe,nge->ltgqn/dot_general | solution.py:69
  394.9 1.7 fusion.75
  396.6 1.0 copy.154
  397.6 0.2 copy.157
  397.8 0.1 reshape_squeeze.42
  398.1 1.5 fusion.2
  399.7 1.5 fusion.3
  401.3 0.7 slice-done.5
  402.0 2.3 fusion.4
  404.3 2.1 fusion.21
  406.4 2.1 fusion.10
  408.5 2.1 fusion.15
  410.6 2.1 fusion.8
  412.7 2.1 fusion.17
  415.0 2.4 fusion.6
  417.4 2.2 fusion.19
  419.6 1.6 fusion.13
  421.3 2.5 fusion.31
  423.9 1.3 copy.129
  (74 shorter events, 1.8 us)
Async XLA Ops:
  7.2 6.2 %copy-start = (bf16[8,128,2,512]{3,2,1,0:T(2,128)(2,1)S(1)}, bf16[8,128,2,512]{3,2,1,0:T(2,128)(2,1)}, u32[]{:S(2)}) copy-start(bf16[8,128,2,512]{3,2,1,0:T(2,128)(2,1)} %param.11) | copy-start | bytes 6291460
  7.2 42.4 %all-gather.9.cloned.1.call-start = ((), (), s32[]{:S(2)}) async-start(), calls=%async_computation.3 | async-start | bytes 1572864 | tf_op jit(solution)/shard_map/all_gather | solution.py:17
  7.9 345.8 %all-gather.5.cloned.1.call-start = ((), (), s32[]{:S(2)}) async-start(), calls=%async_computation.1 | async-start | bytes 8912896 | tf_op jit(solution)/shard_map/all_gather | solution.py:23
  39.0 8.5 %copy-start.2 = (bf16[2,1,128,2048]{3,2,1,0:T(8,128)(2,1)S(1)}, bf16[2,1,128,2048]{3,2,1,0:T(8,128)(2,1)}, u32[]{:S(2)}) copy-start(bf16[2,1,128,2048]{3,2,1,0:T(8,128)(2,1)} %param.10) | copy-start | bytes 3145732
  39.0 9.2 %copy-start.7 = (s32[16,11,1]{0,2,1:T(1,128)S(1)}, s32[16,11,1]{0,2,1:T(1,128)}, u32[]{:S(2)}) copy-start(s32[16,11,1]{0,2,1:T(1,128)} %param.12) | copy-start | bytes 2116
  39.0 323.5 %all-to-all-start = ((bf16[16,2,128,2,512]{4,2,3,1,0:T(8,128)(2,1)}), bf16[16,2,128,2,512]{4,2,3,1,0:T(8,128)(2,1)}, u32[]{:S(2)}, u32[]{:S(2)}) async-start(bf16[16,2,128,2,512]{4,2,3,1,0:T(8,128)(2,1)} %copy_select_fusion), calls=%async_computation | async-start | bytes 16777216 | tf_op jit(solution)/shard_map/all_to_all | solution.py:47
  47.4 347.5 %all-gather.7.cloned.1.call-start = ((), (), s32[]{:S(2)}) async-start(), calls=%async_computation.2 | async-start | bytes 2359296 | tf_op jit(solution)/shard_map/all_gather | solution.py:114
  47.5 312.0 %copy-start.8 = (s32[1,1024]{1,0:T(1,128)S(1)}, s32[1,1024]{1,0:T(1,128)}, u32[]{:S(2)}) copy-start(s32[1,1024]{1,0:T(1,128)} %param.15) | copy-start | bytes 12292
  368.4 2.9 slice-start.6
  398.1 3.2 slice-start.4
  399.7 2.3 slice-start.5
  399.7 4.6 %copy-start.4 = (bf16[512,1,512]{0,2,1:T(8,128)(2,1)S(1)}, bf16[512,1,512]{0,2,1:T(8,128)(2,1)}, u32[]{:S(2)}) copy-start(bf16[512,1,512]{0,2,1:T(8,128)(2,1)} %copy.105) | copy-start | bytes 1572868
  410.6 2.1 copy-start.5
  410.6 4.2 slice-start.2
  412.7 2.3 slice-start.3
  414.8 2.5 copy-start.3
  415.0 4.6 %slice-start = ((s8[6291456]{0:T(1024)(128)(4,1)}), s8[4194304]{0:T(1024)(128)(4,1)S(1)}, s32[]{:S(2)}) async-start(s8[6291456]{0:T(1024)(128)(4,1)} %bitcast.195), calls=%async_computation.4 | async-start | bytes 8388608
  417.4 2.2 slice-start.1
  417.4 3.9 copy-start.6
  421.3 3.9 copy-start.1
Sparse Core Ops, SparseCore 0:
  9.8 29.7 all-gather.8
  42.0 311.6 all-gather.4
  359.6 32.1 all-gather.6
where the time goes:
time: 440 us; the launch traced here: 432 us
  waiting for transfers between devices  305 us (69%)
  local copies, waits for them, and re-layouts  50.4 us (11%)
  matrix products  33.3 us (8%)
  other arithmetic  20.4 us (5%)
  between operations  14.2 us (3%)
  starting transfers between devices  8.47 us (2%)
    all_gather x1, waiting for transfers between devices, on_device(): lax.all_gather(kv_weight, 'cache', axis=0, tiled=True)  304 us
    gather x1, local copies, waits for them, and re-layouts, on_device(): pages = kv_pool[page_choice]  17.9 us
    dot_general x5, matrix products, attend(): jnp.einsum('ltgqe,nge->ltgqn', query_heads, keys_block, preferred_element...  16.7 us
    dot_general x5, matrix products, attend(): jnp.einsum('ltgqn,nge->ltgqe', probs.astype(jnp.bfloat16), values_block,...  11 us
    reduce_sum x5, other arithmetic, attend(): total = total * factor + jnp.sum(probs, axis=-1)  10.4 us
  transfers between devices with their start and end apart: 4, of which 1 were waited for; matrix products, arithmetic and copies ran while one was open for 17% of the time, Pallas kernels for 0%

commit v1 on v0

v1 whole, which is shorter than its diff:
```python
import math

import jax
import jax.numpy as jnp
from jax import lax
from jax.experimental import pallas as pl
from jax.experimental.pallas import tpu as pltpu
from jax.sharding import PartitionSpec as P

HD = 128
CAP = 2
HEADS = 4
GROUP = 4
TOK = 128
LAYERS = 2
CHUNKS = LAYERS * GROUP
ROWS = CHUNKS * TOK
WIDTH = 1024
HITS = 11
HALF = 64
SPANS = 16
MASKED = -1e30
NEVER = 1e30
FACTOR = math.log2(math.e) / math.sqrt(HD)
VMEM_LIMIT = 16 * 1024 * 1024

CACHE_UP = [(i, (i + 2) % 16) for i in range(16)]
CACHE_DOWN = [(i, (i - 2) % 16) for i in range(16)]
CACHE_NEAR = [(i, i ^ 1) for i in range(16)]
CORE = [(i, i ^ 1) for i in range(8)]
XPAIR = [(i, i ^ 2) for i in range(8)]
XUP = [(i, (i + 2) % 8) for i in range(8)]
XDOWN = [(i, (i - 2) % 8) for i in range(8)]
XFAR = [(i, (i + 4) % 8) for i in range(8)]
HEAD = [(0, 1), (1, 0)]
ANY = pl.BlockSpec(memory_space=pl.ANY)
SMEM = pl.BlockSpec(memory_space=pltpu.SMEM)
VMEM = pl.BlockSpec(memory_space=pltpu.VMEM)


def params():
    return pltpu.CompilerParams(vmem_limit_bytes=VMEM_LIMIT)


def cost(flops, transferred, exps=0):
    return pl.CostEstimate(flops=flops, bytes_accessed=transferred, transcendentals=exps)


def bf16(*shape):
    return jax.ShapeDtypeStruct(shape, jnp.bfloat16)


def f32(*shape):
    return jax.ShapeDtypeStruct(shape, jnp.float32)


def pack_kernel(hosts, pages, pool, *refs):
    out = refs[-1]
    me = lax.axis_index("cache")

    def one_span(c, _):
        found, first, second = jnp.int32(0), jnp.int32(0), jnp.int32(0)
        for h in range(HITS):
            here = hosts[c, h] == me
            page = pages[c, h]
            first = jnp.where(here & (found == 0), page, first)
            second = jnp.where(here & (found == 1), page, second)
            found = found + here.astype(jnp.int32)
        out[c * CAP] = pool[first]
        out[c * CAP + 1] = pool[second]
        return 0

    lax.fori_loop(0, SPANS, one_span, 0)


def pack(hosts, pages, pool, *after):
    return pl.pallas_call(
        pack_kernel,
        name="pack",
        out_shape=bf16(SPANS * CAP, HALF, 2 * HD),
        in_specs=[SMEM, SMEM, VMEM] + [VMEM] * len(after),
        out_specs=VMEM,
        compiler_params=params(),
        cost_estimate=cost(0, 2 * 2**20),
    )(hosts, pages, pool, *after)


def unpack_kernel(hosts, arrived, after, out):
    me = lax.axis_index("cache")
    for h in range(HITS):
        host = hosts[me, h]
        place = host * CAP
        for other in range(h):
            place = place + (hosts[me, other] == host).astype(jnp.int32)
        out[h * HALF : (h + 1) * HALF] = arrived[place]


def unpack(hosts, arrived, after):
    return pl.pallas_call(
        unpack_kernel,
        name="unpack",
        out_shape=bf16(HITS * HALF, 2 * HD),
        in_specs=[SMEM, VMEM, VMEM],
        out_specs=VMEM,
        compiler_params=params(),
        cost_estimate=cost(0, 2**20),
    )(hosts, arrived, after)


def project_near_kernel(*refs):
    hidden, weights = refs[:8], refs[8:15]
    partial, far_hidden, hid, wts = refs[15:]
    head = lax.axis_index("head")
    quarter = lax.rem(lax.axis_index("seq"), 4)
    z = lax.axis_index("cache") // 2
    far = pl.multiple_of(lax.rem(z + 4, 8) * 512, 512)
    for i in range(8):
        half, rel = i // 4, i % 4
        tokens = pl.multiple_of(jnp.bitwise_xor(quarter, rel) * TOK, TOK)
        columns = pl.multiple_of(jnp.bitwise_xor(head, half) * 2048, 2048)
        hid[pl.ds(tokens, TOK), pl.ds(columns, 2048)] = hidden[i][...]
    for i, shift in enumerate((0, -1, 1, -2, 2, -3, 3)):
        row = pl.multiple_of(lax.rem(z + shift + 8, 8) * 512, 512)
        wts[pl.ds(row, 512)] = weights[i][...]
    wts[pl.ds(far, 512)] = jnp.zeros((512, 2 * HD), jnp.bfloat16)
    partial[...] = jnp.dot(hid[...], wts[...], preferred_element_type=jnp.float32)
    far_hidden[...] = hid[:, pl.ds(far, 512)]


def project_near(hidden, weights):
    return pl.pallas_call(
        project_near_kernel,
        name="project_near",
        out_shape=(f32(4 * TOK, 2 * HD), bf16(4 * TOK, 512)),
        in_specs=[VMEM] * 15,
        out_specs=(VMEM, VMEM),
        scratch_shapes=[
            pltpu.VMEM((4 * TOK, 4096), jnp.bfloat16),
            pltpu.VMEM((4096, 2 * HD), jnp.bfloat16),
        ],
        compiler_params=params(),
        cost_estimate=cost(2 * 512 * 3584 * 256, 6 * 2**20),
    )(*hidden, *weights)


def project_far_kernel(partial, far_hidden, weights, out):
    out[...] = (
        partial[...] + jnp.dot(far_hidden[...], weights[...], preferred_element_type=jnp.float32)
    ).astype(out.dtype)


def project_far(partial, far_hidden, weights):
    return pl.pallas_call(
        project_far_kernel,
        name="project_far",
        out_shape=bf16(4 * TOK, 2 * HD),
        in_specs=[VMEM] * 3,
        out_specs=VMEM,
        compiler_params=params(),
        cost_estimate=cost(2 * 512 * 512 * 256, 2**20),
    )(partial, far_hidden, weights)


def absorb(places, pieces, rows, limits, bias, state):
    peaks, totals, sums = state
    steps = [(g, part) for g in range(HEADS) for part in range(ROWS // WIDTH)]
    repeat = WIDTH // TOK
    wide = None if limits is None else [jnp.concatenate([limit] * repeat, axis=1) for limit in limits]
    if bias is not None:
        bias = jnp.concatenate([bias] * repeat, axis=1)
    flipped = [jnp.transpose(piece[:, HD:]) for piece in pieces]

    def raw(i):
        g, part = steps[i]
        place = places[g]
        return jnp.dot(
            pieces[g][:, :HD], rows[place, :, part * WIDTH : (part + 1) * WIDTH], preferred_element_type=jnp.float32
        )

    def soften(i, found):
        g, part = steps[i]
        place = places[g]
        where = slice(part * WIDTH, (part + 1) * WIDTH)
        scaled = found * FACTOR
        if bias is not None:
            scaled = scaled + bias
        halves = scaled.shape[0] // TOK
        largest = None
        for h in range(halves):
            block = jnp.max(scaled[h * TOK : (h + 1) * TOK].reshape(TOK // 8, 8, WIDTH), axis=0)
            if wide is not None:
                block = jnp.where(wide[h], block, MASKED)
            largest = block if largest is None else jnp.maximum(largest, block)
        before = peaks[place, 0:1, where]
        peak = jnp.maximum(before, jnp.max(largest, axis=0, keepdims=True))
        shrink = jnp.exp2(before - peak)
        probs = []
        for h in range(halves):
            level = peak if wide is None else jnp.where(wide[h], peak, NEVER)
            probs.append(jnp.exp2(scaled[h * TOK : (h + 1) * TOK] - level))
        total = totals[place, :, where] * shrink
        for block in probs:
            total = total + jnp.sum(block.reshape(TOK // 8, 8, WIDTH), axis=0)
        peaks[place, 0:1, where] = peak
        totals[place, :, where] = total
        return jnp.concatenate([block.astype(jnp.bfloat16) for block in probs], axis=0), shrink

    def add(i, probs, shrink):
        g, part = steps[i]
        place = places[g]
        where = slice(part * WIDTH, (part + 1) * WIDTH)
        sums[place, :, where] = sums[place, :, where] * shrink + jnp.dot(
            flipped[g], probs, preferred_element_type=jnp.float32
        )

    found, held = raw(0), None
    for i in range(len(steps)):
        following = raw(i + 1) if i + 1 < len(steps) else None
        if held is not None:
            add(i - 1, *held)
        held = soften(i, found)
        found = following
    add(len(steps) - 1, *held)


def relay_kernel(*refs):
    out = refs[-1]
    for i in range(4):
        out[i] = refs[i][...]


def relay(blocks, after):
    return pl.pallas_call(
        relay_kernel,
        name="relay",
        out_shape=bf16(4, *blocks[0].shape),
        in_specs=[VMEM] * 4 + [VMEM] * len(after),
        out_specs=VMEM,
        compiler_params=params(),
        cost_estimate=cost(0, 2**21),
    )(*blocks, *after)


def stage_kernel(hidden, own_cols, near_cols, queries, query_seg, key_seg, hosts, pool, sent, both, rows, bias):
    seq = lax.axis_index("seq")
    odd = lax.rem(lax.axis_index("cache"), 2)
    sent[...] = hidden[...]
    both[pl.ds(pl.multiple_of(odd * 256, 256), 256)] = own_cols[...]
    both[pl.ds(pl.multiple_of(256 - odd * 256, 256), 256)] = near_cols[...]
    for g in range(HEADS):
        for chunk in range(CHUNKS):
            column = (g * GROUP + chunk % GROUP) * HD
            rows[g, :, chunk * TOK : (chunk + 1) * TOK] = jnp.transpose(
                queries[chunk // GROUP, :, column : column + HD]
            )
    query_wide = jnp.broadcast_to(query_seg[...], (TOK, TOK))
    key_row = lax.broadcasted_iota(jnp.int32, (TOK, TOK), 0)
    query_lane = lax.broadcasted_iota(jnp.int32, (TOK, TOK), 1) + seq * TOK
    for block in range(8):
        key_wide = jnp.transpose(jnp.broadcast_to(key_seg[block : block + 1], (TOK, TOK)))
        allowed = (key_wide == query_wide) & (key_row + block * TOK <= query_lane)
        bias[block // 2, (block % 2) * TOK : (block % 2 + 1) * TOK] = jnp.where(allowed, 0.0, MASKED)


def stage(hidden, own_cols, near_cols, queries, query_seg, key_seg, hosts, pool):
    return pl.pallas_call(
        stage_kernel,
        name="stage",
        out_shape=(
            bf16(*hidden.shape),
            bf16(512, 2 * HD),
            bf16(HEADS, HD, ROWS),
            f32(4, 2 * TOK, TOK),
        ),
        in_specs=[VMEM] * 6 + [SMEM, VMEM],
        out_specs=(VMEM,) * 4,
        compiler_params=params(),
        cost_estimate=cost(0, 3 * 2**20),
    )(hidden, own_cols, near_cols, queries, query_seg, key_seg, hosts, pool)


def ring_place():
    seq = lax.axis_index("seq")
    x, core = seq // 2, lax.rem(seq, 2)
    places = [half * 2 + jnp.bitwise_xor(core, flip) for half in range(2) for flip in range(2)]
    return seq, x, places


def attend_new_kernel(segments, rows, bias, mine, theirs, after, own, peak, total, summed):
    seq, x, places = ring_place()
    refs = (mine, theirs)
    low = segments[seq * TOK]
    last = seq // 2
    first = jnp.int32(0)
    for k in range(4):
        first = first + (segments[k * 2 * TOK + 2 * TOK - 1] < low).astype(jnp.int32)
    part_rows = pl.ds(pl.multiple_of(lax.rem(seq, 4) * TOK, TOK), TOK)
    core = lax.rem(seq, 2)
    for g in range(HEADS):
        shift = lax.rem((x // 2) * 2 + g // 2 - x + 4, 4)
        flip = jnp.bitwise_xor(core, g % 2)
        block = jnp.where(flip == 0, mine[shift, part_rows, :], theirs[shift, part_rows, :])
        own[:, 0, g * HD : (g + 1) * HD] = block[:, :HD]
        own[:, 1, g * HD : (g + 1) * HD] = block[:, HD:]
    peak[...] = jnp.full(peak.shape, MASKED, jnp.float32)
    total[...] = jnp.zeros(total.shape, jnp.float32)
    summed[...] = jnp.zeros(summed.shape, jnp.float32)

    def one_pair(i, _):
        k = last - i
        where = pl.ds(pl.multiple_of(lax.rem(k, 2) * 2 * TOK, 2 * TOK), 2 * TOK)
        pieces = [
            refs[flip][lax.rem((k // 2) * 2 + half - x + 4, 4), where, :] for half in range(2) for flip in range(2)
        ]
        absorb(places, pieces, rows, None, bias[k], (peak, total, summed))
        return 0

    lax.fori_loop(0, last - first + 1, one_pair, 0)


def attend_new(segments, rows, bias, mine, theirs, after):
    return pl.pallas_call(
        attend_new_kernel,
        name="attend_new",
        out_shape=(
            bf16(TOK, 2, HEADS * HD),
            f32(HEADS, 8, ROWS),
            f32(HEADS, 8, ROWS),
            f32(HEADS, HD, ROWS),
        ),
        in_specs=[SMEM] + [VMEM] * 5,
        out_specs=(VMEM,) * 4,
        compiler_params=params(),
        cost_estimate=cost(2 * 10**9, 6 * 2**20, 3 * 10**6),
    )(segments, rows, bias, mine, theirs, after)


def attend_pages_kernel(
    requests, segments, query_seg, rows, peak_in, total_in, summed_in, mine, theirs, out, peak, total, summed, chosen
):
    seq, x, places = ring_place()
    span = lax.axis_index("cache")
    refs = (mine, theirs)
    low, high = segments[seq * TOK], segments[seq * TOK + TOK - 1]
    count = jnp.int32(0)
    for slot in range(HITS):
        chosen[count] = jnp.int32(slot)
        request = requests[span, slot]
        count = count + ((request >= low) & (request <= high)).astype(jnp.int32)
    peak[...] = peak_in[...]
    total[...] = total_in[...]
    summed[...] = summed_in[...]
    seg = query_seg[...]

    def one_pair(pair, _):
        slots = [chosen[2 * pair], chosen[jnp.minimum(2 * pair + 1, count - 1)]]
        second = jnp.where(2 * pair + 1 < count, requests[span, slots[1]], -1)
        limits = [seg == requests[span, slots[0]], seg == second]
        pieces = [
            jnp.concatenate(
                [
                    refs[flip][
                        lax.rem(2 * part + half - x + 4, 4), pl.ds(pl.multiple_of(slot * HALF, HALF), HALF), :
                    ]
                    for slot in slots
                    for part in range(2)
                ],
                axis=0,
            )
            for half in range(2)
            for flip in range(2)
        ]
        absorb(places, pieces, rows, limits, None, (peak, total, summed))
        return 0

    lax.fori_loop(0, (count + 1) // 2, one_pair, 0)
    for g in range(HEADS):
        for chunk in range(CHUNKS):
            where = slice(chunk * TOK, (chunk + 1) * TOK)
            value = summed[g, :, where] / jnp.sum(total[g, :, where], axis=0, keepdims=True)
            column = (g * GROUP + chunk % GROUP) * HD
            out[chunk // GROUP, :, column : column + HD] = jnp.transpose(value.astype(jnp.bfloat16))


def attend_pages(requests, segments, query_seg, rows, state, mine, theirs):
    return pl.pallas_call(
        attend_pages_kernel,
        name="attend_pages",
        out_shape=bf16(LAYERS, TOK, HEADS * GROUP * HD),
        in_specs=[SMEM, SMEM] + [VMEM] * 7,
        out_specs=VMEM,
        scratch_shapes=[
            pltpu.VMEM((HEADS, 8, ROWS), jnp.float32),
            pltpu.VMEM((HEADS, 8, ROWS), jnp.float32),
            pltpu.VMEM((HEADS, HD, ROWS), jnp.float32),
            pltpu.SMEM((HITS + 1,), jnp.int32),
        ],
        compiler_params=params(),
        cost_estimate=cost(3 * 10**9, 6 * 2**20, 5 * 10**6),
    )(requests, segments, query_seg, rows, *state, mine, theirs)


def seq_gather(block, *after):
    mine = relay(
        [
            block,
            lax.ppermute(block, "seq", XDOWN),
            lax.ppermute(block, "seq", XFAR),
            lax.ppermute(block, "seq", XUP),
        ],
        after,
    )
    return mine, lax.ppermute(mine, "seq", CORE)


def on_device(hidden, kv_weight, queries, kv_pool, hit_host, hit_page, hit_request, segment_ids):
    seq = lax.axis_index("seq")
    quarter = lax.rem(seq, 4)
    segments = segment_ids[0]
    query_seg = lax.dynamic_slice_in_dim(segments, seq * TOK, TOK).reshape(1, TOK)

    own_cols = lax.dynamic_slice_in_dim(kv_weight, quarter * HD, HD, 2).reshape(256, 2 * HD)
    near_cols = lax.ppermute(own_cols, "cache", CACHE_NEAR)
    hosts = hit_host[:, :, 0]
    pool = lax.dynamic_slice(
        kv_pool, (0, (seq // 4) * HALF, 0, quarter * HD), (kv_pool.shape[0], HALF, 2, HD)
    ).reshape(kv_pool.shape[0], HALF, 2 * HD)
    mine, both, rows, bias = stage(
        hidden[0], own_cols, near_cols, queries[:, 0], query_seg, segments.reshape(8, TOK), hosts, pool
    )
    ups, downs = [both], [both]
    for step in range(3):
        ups.append(lax.ppermute(ups[-1], "cache", CACHE_UP))
        downs.append(lax.ppermute(downs[-1], "cache", CACHE_DOWN))
    far = lax.ppermute(ups[3], "cache", CACHE_UP)
    weights = [both, ups[1], downs[1], ups[2], downs[2], ups[3], downs[3]]

    other = lax.ppermute(mine, "head", HEAD)
    hidden_rows = []
    for half in (mine, other):
        across = lax.ppermute(half, "seq", XPAIR)
        hidden_rows += [half, lax.ppermute(half, "seq", CORE), across, lax.ppermute(across, "seq", CORE)]


    partial, far_hidden = project_near(hidden_rows, weights)
    block = project_far(partial, far_hidden, far)
    packed = pack(hosts, hit_page, pool, block)
    arrived = lax.all_to_all(packed, "cache", split_axis=0, concat_axis=0, tiled=True)
    new_mine, new_theirs = seq_gather(block)
    prefix = unpack(hosts, arrived, new_theirs)
    own, *state = attend_new(segments, rows, bias, new_mine, new_theirs, prefix)
    page_mine, page_theirs = seq_gather(prefix, state[0])
    attended = attend_pages(hit_request, segments, query_seg, rows, state, page_mine, page_theirs)
    return attended[:, None], own[None]


def solution(mesh):
    return jax.shard_map(
        on_device,
        mesh=mesh,
        in_specs=(
            P("cache", "seq", "head"),
            P("cache", None, "head"),
            P(None, "cache", "seq", "head"),
            P("cache", None, None, "head"),
            P(),
            P(),
            P(),
            P("cache", None),
        ),
        out_specs=(P(None, "cache", "seq", "head"), P("cache", "seq", None, "head")),
        check_vma=False,
    )
```

time: 440 us -> 128 us (0.29); the launches traced: 432 us -> 128 us
  waiting for transfers between devices: 305 us -> 45.3 us
  starting transfers between devices: 8.47 us -> 48.3 us
  local copies, waits for them, and re-layouts: 50.4 us -> 14.6 us
  matrix products: 33.3 us -> 0 us
  other arithmetic: 20.4 us -> 0 us
  Pallas kernels: 0 us -> 19 us
  between operations: 14.2 us -> 0.81 us
    all_gather x3 -> x0, waiting for transfers between devices: 304 us -> none  [the longest x1 304 us: on_device(): lax.all_gather(kv_weight, 'cache', axis=0, tiled=True)]
    ppermute x0 -> x23, waiting for transfers between devices: none -> 45.3 us  [the longest x2 16.2 us: seq_gather(): lax.ppermute(block, 'seq', XUP)]
    ppermute x0 -> x23, starting transfers between devices: none -> 40.2 us  [the longest x2 9.49 us: seq_gather(): lax.ppermute(block, 'seq', XDOWN)]
    dot_general x11 -> x0, matrix products: 33.3 us -> none  [the longest x5 16.7 us: attend(): jnp.einsum('ltgqe,nge->ltgqn', query_heads, keys_block, preferred_element...]
    gather x2 -> x0, local copies, waits for them, and re-layouts: 23.8 us -> none  [the longest x1 17.9 us: on_device(): pages = kv_pool[page_choice]]
    pallas_call x0 -> x9, Pallas kernels: none -> 19 us  [the longest x1 8.87 us: attend_pages(): pl.pallas_call(attend_pages_kernel, name='attend_pages', out_shape=bf16(L...]
    slice x21 -> x0, local copies, waits for them, and re-layouts: 14.7 us -> none  [the longest x7 7.62 us: attend(): values_block = block_keys[:, 1].reshape(count_keys, groups, HD)]
    reduce_sum x7 -> x0, other arithmetic: 10.5 us -> none  [the longest x5 10.4 us: attend(): total = total * factor + jnp.sum(probs, axis=-1)]
  transfers between devices with their start and end apart: 4 -> 24, of which waited for: 1 -> 11; matrix products, arithmetic and copies ran while one was open for 17% -> 3% of each run, Pallas kernels for 0% -> 5%
where the time goes in v1:
time: 128 us
  starting transfers between devices  48.3 us (38%)
  waiting for transfers between devices  45.3 us (35%)
  Pallas kernels  19 us (15%)
  local copies, waits for them, and re-layouts  14.6 us (11%)
    ppermute x2, waiting for transfers between devices, seq_gather(): lax.ppermute(block, 'seq', XUP)  16.2 us
    unnamed x38, local copies, waits for them, and re-layouts  10.7 us
    ppermute x2, starting transfers between devices, seq_gather(): lax.ppermute(block, 'seq', XDOWN)  9.49 us
    pallas_call x1, Pallas kernels, attend_pages(): pl.pallas_call(attend_pages_kernel, name='attend_pages', out_shape=bf16(L...  8.87 us
    ppermute x3, starting transfers between devices, on_device(): ups.append(lax.ppermute(ups[-1], 'cache', CACHE_UP))  8.81 us
    all_to_all x1, starting transfers between devices, on_device(): lax.all_to_all(packed, 'cache', split_axis=0, concat_axis=0, tiled=True)  8.14 us
    ppermute x1, waiting for transfers between devices, on_device(): other = lax.ppermute(mine, 'head', HEAD)  7.95 us
    ppermute x3, waiting for transfers between devices, on_device(): ups.append(lax.ppermute(ups[-1], 'cache', CACHE_UP))  6.63 us
  transfers between devices with their start and end apart: 24, of which 11 were waited for; matrix products, arithmetic and copies ran while one was open for 3% of the time, Pallas kernels for 5%

profile of v1, /device:TPU:97, one launch (start us, length us, event | category | flops | bytes accessed | tf_op | source)
XLA Modules:
  0.0 128.0 jit_solution(7751537073046890609)
XLA Ops:
  0.7 1.2 constant_dynamic-slice_fusion.1
  1.8 1.4 %collective-permute-start = (bf16[256,256]{1,0:T(8,128)(2,1)S(1)}, bf16[256,256]{1,0:T(8,128)(2,1)}, u32[]{:S(2)}, u32[]{:S(2)}) collective-permute-start(bf16[256,256]{1,0:T(8,128)(2,1)S(1)} %bitcast.15), channel_id=1, source_target_pairs={{0,16},{16,0},{32,48},{48,32},{64,80},{80,64},{96,112},{112,96},{1... | collective-permute-start | bytes 393224 | tf_op jit(solution)/shard_map/ppermute | solution.py:423
  3.2 0.9 constant_dynamic-slice_fusion
  4.1 0.8 copy.10
  4.9 1.1 reshape.14.pool
  6.0 0.7 constant_dynamic-slice_fusion.2.query_seg
  6.7 1.0 copy-done.8
  7.7 0.7 copy-done.10
  8.4 1.4 %stage.1 = (bf16[128,2048]{1,0:T(8,128)(2,1)S(1)}, bf16[512,256]{1,0:T(8,128)(2,1)S(1)}, bf16[4,128,1024]{2,1,0:T(8,128)(2,1)S(1)}, f32[4,256,128]{2,1,0:T(8,128)S(1)}) custom-call(bf16[128,2048]{1,0:T(8,128)(2,1)S(1)} %bitcast.14, bf16[256,256]{1,0:T(8,128)(2,1)S(1)} %bitcast.16, bf16[256,256]{1,0:T(8,128)(2,1)} %collective-permute-done.near_cols, ...), custom_call_target="tpu_custom_call" | custom-call | bytes 3145728 | tf_op jit(solution)/shard_map/stage/pallas_call | solution.py:266
  9.8 1.0 copy-done.12
  10.8 0.8 copy-done.15
  11.6 2.6 %collective-permute-start.4 = (bf16[128,2048]{1,0:T(8,128)(2,1)S(1)}, bf16[128,2048]{1,0:T(8,128)(2,1)S(1)}, u32[]{:S(2)}, u32[]{:S(2)}) collective-permute-start(bf16[128,2048]{1,0:T(8,128)(2,1)S(1)} %get-tuple-element.14.refs_0_), channel_id=1, source_target_pairs={{0,1},{1,0},{2,3},{3,2},{4,5},{5,4},{6,7},{7,6},{8,9},{9,8},{10,11... | collective-permute-start | bytes 1572872 | tf_op jit(solution)/shard_map/ppermute | solution.py:438
  14.2 1.8 %collective-permute-start.1 = (bf16[128,2048]{1,0:T(8,128)(2,1)S(1)}, bf16[128,2048]{1,0:T(8,128)(2,1)S(1)}, u32[]{:S(2)}, u32[]{:S(2)}) collective-permute-start(bf16[128,2048]{1,0:T(8,128)(2,1)S(1)} %get-tuple-element.14.refs_0_), channel_id=1, source_target_pairs={{0,2},{2,0},{4,6},{6,4},{8,10},{10,8},{12,14},{14,12},{1,3},{3,1},... | collective-permute-start | bytes 1572872 | tf_op jit(solution)/shard_map/ppermute | solution.py:442
  16.0 1.2 collective-permute-start.2
  17.3 8.0 %collective-permute-done.4.refs_4_ = bf16[128,2048]{1,0:T(8,128)(2,1)S(1)} collective-permute-done((bf16[128,2048]{1,0:T(8,128)(2,1)S(1)}, bf16[128,2048]{1,0:T(8,128)(2,1)S(1)}, u32[]{:S(2)}, u32[]{:S(2)}) %collective-permute-start.4) | collective-permute-done | bytes 524320 | tf_op jit(solution)/shard_map/ppermute | solution.py:438
  25.2 1.2 collective-permute-start.6
  26.4 2.8 %collective-permute-start.8 = (bf16[512,256]{1,0:T(8,128)(2,1)S(1)}, bf16[512,256]{1,0:T(8,128)(2,1)S(1)}, u32[]{:S(2)}, u32[]{:S(2)}) collective-permute-start(bf16[512,256]{1,0:T(8,128)(2,1)S(1)} %get-tuple-element.15.refs_8_), channel_id=1, source_target_pairs={{0,32},{16,48},{32,64},{48,80},{64,96},{80,112},{96,128},{112,144}... | collective-permute-start | bytes 786440 | tf_op jit(solution)/shard_map/ppermute | solution.py:433
  29.3 3.3 %collective-permute-done.8.refs_9_ = bf16[512,256]{1,0:T(8,128)(2,1)S(1)} collective-permute-done((bf16[512,256]{1,0:T(8,128)(2,1)S(1)}, bf16[512,256]{1,0:T(8,128)(2,1)S(1)}, u32[]{:S(2)}, u32[]{:S(2)}) %collective-permute-start.8) | collective-permute-done | bytes 262176 | tf_op jit(solution)/shard_map/ppermute | solution.py:433
  32.6 3.1 %collective-permute-start.10 = (bf16[512,256]{1,0:T(8,128)(2,1)S(1)}, bf16[512,256]{1,0:T(8,128)(2,1)S(1)}, u32[]{:S(2)}, u32[]{:S(2)}) collective-permute-start(bf16[512,256]{1,0:T(8,128)(2,1)S(1)} %collective-permute-done.8.refs_9_), channel_id=1, source_target_pairs={{0,32},{16,48},{32,64},{48,80},{64,96},{80,112},{96,128},{112,144}... | collective-permute-start | bytes 786440 | tf_op jit(solution)/shard_map/ppermute | solution.py:433
  35.7 4.0 %collective-permute-start.5 = (bf16[128,2048]{1,0:T(8,128)(2,1)S(1)}, bf16[128,2048]{1,0:T(8,128)(2,1)S(1)}, u32[]{:S(2)}, u32[]{:S(2)}) collective-permute-start(bf16[128,2048]{1,0:T(8,128)(2,1)S(1)} %collective-permute-done.4.refs_4_), channel_id=1, source_target_pairs={{0,2},{2,0},{4,6},{6,4},{8,10},{10,8},{12,14},{14,12},{1,3},{3,1},... | collective-permute-start | bytes 1572872 | tf_op jit(solution)/shard_map/ppermute | solution.py:442
  39.8 0.7 collective-permute-done.6.refs_6_
  40.6 1.1 collective-permute-start.7
  41.6 2.8 %collective-permute-start.12 = (bf16[512,256]{1,0:T(8,128)(2,1)S(1)}, bf16[512,256]{1,0:T(8,128)(2,1)S(1)}, u32[]{:S(2)}, u32[]{:S(2)}) collective-permute-start(bf16[512,256]{1,0:T(8,128)(2,1)S(1)} %collective-permute-done.10.refs_11_), channel_id=1, source_target_pairs={{0,32},{16,48},{32,64},{48,80},{64,96},{80,112},{96,128},{112,144}... | collective-permute-start | bytes 786440 | tf_op jit(solution)/shard_map/ppermute | solution.py:433
  44.5 3.3 %collective-permute-done.12.refs_13_ = bf16[512,256]{1,0:T(8,128)(2,1)S(1)} collective-permute-done((bf16[512,256]{1,0:T(8,128)(2,1)S(1)}, bf16[512,256]{1,0:T(8,128)(2,1)S(1)}, u32[]{:S(2)}, u32[]{:S(2)}) %collective-permute-start.12) | collective-permute-done | bytes 262176 | tf_op jit(solution)/shard_map/ppermute | solution.py:433
  47.8 3.1 %collective-permute-start.14 = (bf16[512,256]{1,0:T(8,128)(2,1)S(1)}, bf16[512,256]{1,0:T(8,128)(2,1)S(1)}, u32[]{:S(2)}, u32[]{:S(2)}) collective-permute-start(bf16[512,256]{1,0:T(8,128)(2,1)S(1)} %collective-permute-done.12.refs_13_), channel_id=1, source_target_pairs={{0,32},{16,48},{32,64},{48,80},{64,96},{80,112},{96,128},{112,144}... | collective-permute-start | bytes 786440 | tf_op jit(solution)/shard_map/ppermute | solution.py:435
  50.9 1.7 %project_near.1 = (f32[512,256]{1,0:T(8,128)S(1)}, bf16[512,512]{1,0:T(8,128)(2,1)S(1)}) custom-call(bf16[128,2048]{1,0:T(8,128)(2,1)S(1)} %get-tuple-element.14.refs_0_, bf16[128,2048]{1,0:T(8,128)(2,1)S(1)} %collective-permute-done.1.refs_1_, bf16[128,2048]{1,0:T(8,128)(2,1)S(1)} %collective-permute-done.2.refs_2_, ...), custom_call_target="tpu_custom_call" | custom-call | flops 939524096 | bytes 6291456 | tf_op jit(solution)/shard_map/project_near/pallas_call | solution.py:131
  52.7 1.6 %collective-permute-done.14.weights = bf16[512,256]{1,0:T(8,128)(2,1)S(1)} collective-permute-done((bf16[512,256]{1,0:T(8,128)(2,1)S(1)}, bf16[512,256]{1,0:T(8,128)(2,1)S(1)}, u32[]{:S(2)}, u32[]{:S(2)}) %collective-permute-start.14) | collective-permute-done | bytes 262176 | tf_op jit(solution)/shard_map/ppermute | solution.py:435
  54.5 1.6 %pack.1 = bf16[32,64,256]{2,1,0:T(8,128)(2,1)S(1)} custom-call(s32[16,11]{1,0:T(8,128)S(1)} %bitcast.18, s32[16,11]{1,0:T(8,128)S(1)} %copy-done.9, bf16[8,64,256]{2,1,0:T(8,128)(2,1)S(1)} %reshape.14.pool, bf16[512,256]{1,0:T(8,128)(2,1)S(1)} %project_far.1.refs_0_), custom_call_target="tpu_custom_call" | custom-call | bytes 2097152 | tf_op jit(solution)/shard_map/pack/pallas_call | solution.py:77
  56.1 1.0 copy-done.1
  57.1 8.1 %all-to-all-start = ((bf16[32,64,256]{2,1,0:T(8,128)(2,1)}), bf16[32,64,256]{2,1,0:T(8,128)(2,1)S(1)}, u32[]{:S(2)}, u32[]{:S(2)}) async-start(bf16[32,64,256]{2,1,0:T(8,128)(2,1)} %copy-done.1), calls=%async_computation | async-start | bytes 2097152 | tf_op jit(solution)/shard_map/all_to_all | solution.py:448
  65.3 3.0 %collective-permute-start.15 = (bf16[512,256]{1,0:T(8,128)(2,1)S(1)}, bf16[512,256]{1,0:T(8,128)(2,1)S(1)}, u32[]{:S(2)}, u32[]{:S(2)}) collective-permute-start(bf16[512,256]{1,0:T(8,128)(2,1)S(1)} %project_far.1.refs_0_), channel_id=1, source_target_pairs={{0,12},{2,14},{4,0},{6,2},{8,4},{10,6},{12,8},{14,10},{1,13},{3,15... | collective-permute-start | bytes 786440 | tf_op jit(solution)/shard_map/ppermute | solution.py:407
  68.8 0.6 collective-permute-start.17
  69.4 5.9 %collective-permute-done.15.refs_1_ = bf16[512,256]{1,0:T(8,128)(2,1)S(1)} collective-permute-done((bf16[512,256]{1,0:T(8,128)(2,1)S(1)}, bf16[512,256]{1,0:T(8,128)(2,1)S(1)}, u32[]{:S(2)}, u32[]{:S(2)}) %collective-permute-start.15) | collective-permute-done | bytes 262176 | tf_op jit(solution)/shard_map/ppermute | solution.py:407
  75.3 6.0 %collective-permute-done.17.refs_3_ = bf16[512,256]{1,0:T(8,128)(2,1)S(1)} collective-permute-done((bf16[512,256]{1,0:T(8,128)(2,1)S(1)}, bf16[512,256]{1,0:T(8,128)(2,1)S(1)}, u32[]{:S(2)}, u32[]{:S(2)}) %collective-permute-start.17) | collective-permute-done | bytes 262176 | tf_op jit(solution)/shard_map/ppermute | solution.py:409
  81.4 2.9 %collective-permute-start.18 = (bf16[4,512,256]{2,1,0:T(8,128)(2,1)S(1)}, bf16[4,512,256]{2,1,0:T(8,128)(2,1)S(1)}, u32[]{:S(2)}, u32[]{:S(2)}) collective-permute-start(bf16[4,512,256]{2,1,0:T(8,128)(2,1)S(1)} %relay.2.mine), channel_id=1, source_target_pairs={{0,2},{2,0},{4,6},{6,4},{8,10},{10,8},{12,14},{14,12},{1,3},{3,1},... | collective-permute-start | bytes 3145736 | tf_op jit(solution)/shard_map/ppermute | solution.py:413
  84.3 1.0 copy-done.6
  85.3 1.3 %collective-permute-done.18.after.theirs = bf16[4,512,256]{2,1,0:T(8,128)(2,1)S(1)} collective-permute-done((bf16[4,512,256]{2,1,0:T(8,128)(2,1)S(1)}, bf16[4,512,256]{2,1,0:T(8,128)(2,1)S(1)}, u32[]{:S(2)}, u32[]{:S(2)}) %collective-permute-start.18) | collective-permute-done | bytes 1048608 | tf_op jit(solution)/shard_map/ppermute | solution.py:413
  86.6 1.0 copy-done.3
  87.6 1.2 copy-done.4
  88.8 0.8 unpack.1.after.refs_0_
  89.6 6.5 %collective-permute-start.19 = (bf16[704,256]{1,0:T(8,128)(2,1)S(1)}, bf16[704,256]{1,0:T(8,128)(2,1)S(1)}, u32[]{:S(2)}, u32[]{:S(2)}) collective-permute-start(bf16[704,256]{1,0:T(8,128)(2,1)S(1)} %unpack.1.after.refs_0_), channel_id=1, source_target_pairs={{0,12},{2,14},{4,0},{6,2},{8,4},{10,6},{12,8},{14,10},{1,13},{3,15... | collective-permute-start | bytes 1081352 | tf_op jit(solution)/shard_map/ppermute | solution.py:407
  96.7 1.2 copy-done.13
  97.9 1.0 copy-done.16
  99.0 4.2 %attend_new.1 = (bf16[128,2,512]{2,1,0:T(2,128)(2,1)}, f32[4,8,1024]{2,1,0:T(8,128)S(1)}, f32[4,8,1024]{2,1,0:T(8,128)S(1)}, f32[4,128,1024]{2,1,0:T(8,128)S(1)}) custom-call(s32[1024]{0:T(1024)S(1)} %bitcast.21, bf16[4,128,1024]{2,1,0:T(8,128)(2,1)S(1)} %copy-done.13, f32[4,256,128]{2,1,0:T(8,128)S(1)} %copy-done.16, bf16[4,512,256]{2,1,0:T(8,128)(2,1)S(1)} %copy-done.7, ...), custom_call_target="tpu_custom_call" | custom-call | flops 2000000000 | bytes 6291456 | tf_op jit(solution)/shard_map/attend_new/pallas_call | solution.py:322
  103.2 2.1 %collective-permute-done.20.refs_2_ = bf16[704,256]{1,0:T(8,128)(2,1)S(1)} collective-permute-done((bf16[704,256]{1,0:T(8,128)(2,1)S(1)}, bf16[704,256]{1,0:T(8,128)(2,1)S(1)}, u32[]{:S(2)}, u32[]{:S(2)}) %collective-permute-start.20) | collective-permute-done | bytes 360480 | tf_op jit(solution)/shard_map/ppermute | solution.py:408
  105.4 10.2 %collective-permute-done.21.refs_3_ = bf16[704,256]{1,0:T(8,128)(2,1)S(1)} collective-permute-done((bf16[704,256]{1,0:T(8,128)(2,1)S(1)}, bf16[704,256]{1,0:T(8,128)(2,1)S(1)}, u32[]{:S(2)}, u32[]{:S(2)}) %collective-permute-start.21) | collective-permute-done | bytes 360480 | tf_op jit(solution)/shard_map/ppermute | solution.py:409
  116.3 2.8 %collective-permute-done.22.theirs = bf16[4,704,256]{2,1,0:T(8,128)(2,1)S(1)} collective-permute-done((bf16[4,704,256]{2,1,0:T(8,128)(2,1)S(1)}, bf16[4,704,256]{2,1,0:T(8,128)(2,1)S(1)}, u32[]{:S(2)}, u32[]{:S(2)}) %collective-permute-start.22) | collective-permute-done | bytes 1441824 | tf_op jit(solution)/shard_map/ppermute | solution.py:413
  119.1 8.9 %attend_pages.1 = bf16[2,128,2048]{2,1,0:T(8,128)(2,1)} custom-call(s32[16,11]{1,0:T(8,128)S(1)} %copy-done.17, s32[1024]{0:T(1024)S(1)} %bitcast.22, s32[1,128]{1,0:T(1,128)S(1)} %constant_dynamic-slice_fusion.2.query_seg, bf16[4,128,1024]{2,1,0:T(8,128)(2,1)S(1)} %copy-done.14, f32[4,8,1024]{2,1,0:T(8,128)S(1)} %get-tuple-element.18.refs_4_.peak_in, ...), custom_call_target="tpu_custom_call" | custom-call | flops 3000000000 | bytes 6291456 | tf_op jit(solution)/shard_map/attend_pages/pallas_call | solution.py:386
  (51 shorter events, 2.5 us)
Async XLA Ops:
  0.6 2.6 %copy-start = (bf16[8,128,2,512]{3,2,1,0:T(2,128)(2,1)S(1)}, bf16[8,128,2,512]{3,2,1,0:T(2,128)(2,1)}, u32[]{:S(2)}) copy-start(bf16[8,128,2,512]{3,2,1,0:T(2,128)(2,1)} %param.11) | copy-start | bytes 6291460
  0.6 6.0 %copy-start.2 = (bf16[2,1,128,2048]{3,2,1,0:T(8,128)(2,1)S(1)}, bf16[2,1,128,2048]{3,2,1,0:T(8,128)(2,1)}, u32[]{:S(2)}) copy-start(bf16[2,1,128,2048]{3,2,1,0:T(8,128)(2,1)} %param.10) | copy-start | bytes 3145732
  1.8 4.8 %collective-permute-start = (bf16[256,256]{1,0:T(8,128)(2,1)S(1)}, bf16[256,256]{1,0:T(8,128)(2,1)}, u32[]{:S(2)}, u32[]{:S(2)}) collective-permute-start(bf16[256,256]{1,0:T(8,128)(2,1)S(1)} %bitcast.15), channel_id=1, source_target_pairs={{0,16},{16,0},{32,48},{48,32},{64,80},{80,64},{96,112},{112,96},{1... | collective-permute-start | bytes 393224 | tf_op jit(solution)/shard_map/ppermute | solution.py:423
  6.7 1.0 copy-start.8
  7.7 0.7 copy-start.10
  9.8 1.0 copy-start.12
  10.8 0.8 copy-start.15
  11.6 13.6 %collective-permute-start.4 = (bf16[128,2048]{1,0:T(8,128)(2,1)S(1)}, bf16[128,2048]{1,0:T(8,128)(2,1)S(1)}, u32[]{:S(2)}, u32[]{:S(2)}) collective-permute-start(bf16[128,2048]{1,0:T(8,128)(2,1)S(1)} %get-tuple-element.14.refs_0_), channel_id=1, source_target_pairs={{0,1},{1,0},{2,3},{3,2},{4,5},{5,4},{6,7},{7,6},{8,9},{9,8},{10,11... | collective-permute-start | bytes 1572872 | tf_op jit(solution)/shard_map/ppermute | solution.py:438
  14.2 21.5 %collective-permute-start.1 = (bf16[128,2048]{1,0:T(8,128)(2,1)S(1)}, bf16[128,2048]{1,0:T(8,128)(2,1)S(1)}, u32[]{:S(2)}, u32[]{:S(2)}) collective-permute-start(bf16[128,2048]{1,0:T(8,128)(2,1)S(1)} %get-tuple-element.14.refs_0_), channel_id=1, source_target_pairs={{0,2},{2,0},{4,6},{6,4},{8,10},{10,8},{12,14},{14,12},{1,3},{3,1},... | collective-permute-start | bytes 1572872 | tf_op jit(solution)/shard_map/ppermute | solution.py:442
  16.0 23.7 %collective-permute-start.2 = (bf16[128,2048]{1,0:T(8,128)(2,1)S(1)}, bf16[128,2048]{1,0:T(8,128)(2,1)S(1)}, u32[]{:S(2)}, u32[]{:S(2)}) collective-permute-start(bf16[128,2048]{1,0:T(8,128)(2,1)S(1)} %get-tuple-element.14.refs_0_), channel_id=1, source_target_pairs={{0,4},{2,6},{4,0},{6,2},{8,12},{10,14},{12,8},{14,10},{1,5},{3,7},... | collective-permute-start | bytes 1572872 | tf_op jit(solution)/shard_map/ppermute | solution.py:441
  25.2 15.4 %collective-permute-start.6 = (bf16[128,2048]{1,0:T(8,128)(2,1)S(1)}, bf16[128,2048]{1,0:T(8,128)(2,1)S(1)}, u32[]{:S(2)}, u32[]{:S(2)}) collective-permute-start(bf16[128,2048]{1,0:T(8,128)(2,1)S(1)} %collective-permute-done.4.refs_4_), channel_id=1, source_target_pairs={{0,4},{2,6},{4,0},{6,2},{8,12},{10,14},{12,8},{14,10},{1,5},{3,7},... | collective-permute-start | bytes 1572872 | tf_op jit(solution)/shard_map/ppermute | solution.py:441
  26.4 28.1 %copy-start.9 = (s32[16,11]{1,0:T(8,128)S(1)}, s32[16,11]{1,0:T(8,128)}, u32[]{:S(2)}) copy-start(s32[16,11]{1,0:T(8,128)} %pages.1) | copy-start | bytes 2116
  26.4 6.2 %collective-permute-start.8 = (bf16[512,256]{1,0:T(8,128)(2,1)S(1)}, bf16[512,256]{1,0:T(8,128)(2,1)S(1)}, u32[]{:S(2)}, u32[]{:S(2)}) collective-permute-start(bf16[512,256]{1,0:T(8,128)(2,1)S(1)} %get-tuple-element.15.refs_8_), channel_id=1, source_target_pairs={{0,32},{16,48},{32,64},{48,80},{64,96},{80,112},{96,128},{112,144}... | collective-permute-start | bytes 786440 | tf_op jit(solution)/shard_map/ppermute | solution.py:433
  29.3 6.4 %collective-permute-start.9 = (bf16[512,256]{1,0:T(8,128)(2,1)S(1)}, bf16[512,256]{1,0:T(8,128)(2,1)S(1)}, u32[]{:S(2)}, u32[]{:S(2)}) collective-permute-start(bf16[512,256]{1,0:T(8,128)(2,1)S(1)} %get-tuple-element.15.refs_8_), channel_id=1, source_target_pairs={{0,224},{16,240},{32,0},{48,16},{64,32},{80,48},{96,64},{112,80},{... | collective-permute-start | bytes 786440 | tf_op jit(solution)/shard_map/ppermute | solution.py:434
  32.6 9.0 %collective-permute-start.10 = (bf16[512,256]{1,0:T(8,128)(2,1)S(1)}, bf16[512,256]{1,0:T(8,128)(2,1)S(1)}, u32[]{:S(2)}, u32[]{:S(2)}) collective-permute-start(bf16[512,256]{1,0:T(8,128)(2,1)S(1)} %collective-permute-done.8.refs_9_), channel_id=1, source_target_pairs={{0,32},{16,48},{32,64},{48,80},{64,96},{80,112},{96,128},{112,144}... | collective-permute-start | bytes 786440 | tf_op jit(solution)/shard_map/ppermute | solution.py:433
  35.7 8.8 %collective-permute-start.11 = (bf16[512,256]{1,0:T(8,128)(2,1)S(1)}, bf16[512,256]{1,0:T(8,128)(2,1)S(1)}, u32[]{:S(2)}, u32[]{:S(2)}) collective-permute-start(bf16[512,256]{1,0:T(8,128)(2,1)S(1)} %collective-permute-done.9.refs_10_), channel_id=1, source_target_pairs={{0,224},{16,240},{32,0},{48,16},{64,32},{80,48},{96,64},{112,80},{... | collective-permute-start | bytes 786440 | tf_op jit(solution)/shard_map/ppermute | solution.py:434
  35.7 15.2 %collective-permute-start.5 = (bf16[128,2048]{1,0:T(8,128)(2,1)S(1)}, bf16[128,2048]{1,0:T(8,128)(2,1)S(1)}, u32[]{:S(2)}, u32[]{:S(2)}) collective-permute-start(bf16[128,2048]{1,0:T(8,128)(2,1)S(1)} %collective-permute-done.4.refs_4_), channel_id=1, source_target_pairs={{0,2},{2,0},{4,6},{6,4},{8,10},{10,8},{12,14},{14,12},{1,3},{3,1},... | collective-permute-start | bytes 1572872 | tf_op jit(solution)/shard_map/ppermute | solution.py:442
  39.7 11.2 %collective-permute-start.3 = (bf16[128,2048]{1,0:T(8,128)(2,1)S(1)}, bf16[128,2048]{1,0:T(8,128)(2,1)S(1)}, u32[]{:S(2)}, u32[]{:S(2)}) collective-permute-start(bf16[128,2048]{1,0:T(8,128)(2,1)S(1)} %collective-permute-done.2.refs_2_), channel_id=1, source_target_pairs={{0,2},{2,0},{4,6},{6,4},{8,10},{10,8},{12,14},{14,12},{1,3},{3,1},... | collective-permute-start | bytes 1572872 | tf_op jit(solution)/shard_map/ppermute | solution.py:442
  40.6 10.4 %collective-permute-start.7 = (bf16[128,2048]{1,0:T(8,128)(2,1)S(1)}, bf16[128,2048]{1,0:T(8,128)(2,1)S(1)}, u32[]{:S(2)}, u32[]{:S(2)}) collective-permute-start(bf16[128,2048]{1,0:T(8,128)(2,1)S(1)} %collective-permute-done.6.refs_6_), channel_id=1, source_target_pairs={{0,2},{2,0},{4,6},{6,4},{8,10},{10,8},{12,14},{14,12},{1,3},{3,1},... | collective-permute-start | bytes 1572872 | tf_op jit(solution)/shard_map/ppermute | solution.py:442
  41.6 6.2 %collective-permute-start.12 = (bf16[512,256]{1,0:T(8,128)(2,1)S(1)}, bf16[512,256]{1,0:T(8,128)(2,1)S(1)}, u32[]{:S(2)}, u32[]{:S(2)}) collective-permute-start(bf16[512,256]{1,0:T(8,128)(2,1)S(1)} %collective-permute-done.10.refs_11_), channel_id=1, source_target_pairs={{0,32},{16,48},{32,64},{48,80},{64,96},{80,112},{96,128},{112,144}... | collective-permute-start | bytes 786440 | tf_op jit(solution)/shard_map/ppermute | solution.py:433
  44.5 6.4 %collective-permute-start.13 = (bf16[512,256]{1,0:T(8,128)(2,1)S(1)}, bf16[512,256]{1,0:T(8,128)(2,1)S(1)}, u32[]{:S(2)}, u32[]{:S(2)}) collective-permute-start(bf16[512,256]{1,0:T(8,128)(2,1)S(1)} %collective-permute-done.11.refs_12_), channel_id=1, source_target_pairs={{0,224},{16,240},{32,0},{48,16},{64,32},{80,48},{96,64},{112,80},{... | collective-permute-start | bytes 786440 | tf_op jit(solution)/shard_map/ppermute | solution.py:434
  47.8 6.4 %collective-permute-start.14 = (bf16[512,256]{1,0:T(8,128)(2,1)S(1)}, bf16[512,256]{1,0:T(8,128)(2,1)S(1)}, u32[]{:S(2)}, u32[]{:S(2)}) collective-permute-start(bf16[512,256]{1,0:T(8,128)(2,1)S(1)} %collective-permute-done.12.refs_13_), channel_id=1, source_target_pairs={{0,32},{16,48},{32,64},{48,80},{64,96},{80,112},{96,128},{112,144}... | collective-permute-start | bytes 786440 | tf_op jit(solution)/shard_map/ppermute | solution.py:435
  56.1 1.0 copy-start.1
  57.1 30.5 %all-to-all-start = ((bf16[32,64,256]{2,1,0:T(8,128)(2,1)}), bf16[32,64,256]{2,1,0:T(8,128)(2,1)S(1)}, u32[]{:S(2)}, u32[]{:S(2)}) async-start(bf16[32,64,256]{2,1,0:T(8,128)(2,1)} %copy-done.1), calls=%async_computation | async-start | bytes 2097152 | tf_op jit(solution)/shard_map/all_to_all | solution.py:448
  65.2 31.5 %copy-start.11 = (s32[1,1024]{1,0:T(1,128)S(1)}, s32[1,1024]{1,0:T(1,128)}, u32[]{:S(2)}) copy-start(s32[1,1024]{1,0:T(1,128)} %param.15) | copy-start | bytes 12292
  65.3 10.1 %collective-permute-start.15 = (bf16[512,256]{1,0:T(8,128)(2,1)S(1)}, bf16[512,256]{1,0:T(8,128)(2,1)S(1)}, u32[]{:S(2)}, u32[]{:S(2)}) collective-permute-start(bf16[512,256]{1,0:T(8,128)(2,1)S(1)} %project_far.1.refs_0_), channel_id=1, source_target_pairs={{0,12},{2,14},{4,0},{6,2},{8,4},{10,6},{12,8},{14,10},{1,13},{3,15... | collective-permute-start | bytes 786440 | tf_op jit(solution)/shard_map/ppermute | solution.py:407
  68.3 7.1 %collective-permute-start.16 = (bf16[512,256]{1,0:T(8,128)(2,1)S(1)}, bf16[512,256]{1,0:T(8,128)(2,1)S(1)}, u32[]{:S(2)}, u32[]{:S(2)}) collective-permute-start(bf16[512,256]{1,0:T(8,128)(2,1)S(1)} %project_far.1.refs_0_), channel_id=1, source_target_pairs={{0,8},{2,10},{4,12},{6,14},{8,0},{10,2},{12,4},{14,6},{1,9},{3,11}... | collective-permute-start | bytes 786440 | tf_op jit(solution)/shard_map/ppermute | solution.py:408
  68.8 12.5 %collective-permute-start.17 = (bf16[512,256]{1,0:T(8,128)(2,1)S(1)}, bf16[512,256]{1,0:T(8,128)(2,1)S(1)}, u32[]{:S(2)}, u32[]{:S(2)}) collective-permute-start(bf16[512,256]{1,0:T(8,128)(2,1)S(1)} %project_far.1.refs_0_), channel_id=1, source_target_pairs={{0,4},{2,6},{4,8},{6,10},{8,12},{10,14},{12,0},{14,2},{1,5},{3,7},... | collective-permute-start | bytes 786440 | tf_op jit(solution)/shard_map/ppermute | solution.py:409
  81.4 5.2 %collective-permute-start.18 = (bf16[4,512,256]{2,1,0:T(8,128)(2,1)S(1)}, bf16[4,512,256]{2,1,0:T(8,128)(2,1)S(1)}, u32[]{:S(2)}, u32[]{:S(2)}) collective-permute-start(bf16[4,512,256]{2,1,0:T(8,128)(2,1)S(1)} %relay.2.mine), channel_id=1, source_target_pairs={{0,2},{2,0},{4,6},{6,4},{8,10},{10,8},{12,14},{14,12},{1,3},{3,1},... | collective-permute-start | bytes 3145736 | tf_op jit(solution)/shard_map/ppermute | solution.py:413
  84.3 1.0 copy-start.6
  86.6 1.0 copy-start.3
  87.6 1.2 copy-start.4
  88.8 7.9 %copy-start.5 = (bf16[4,512,256]{2,1,0:T(8,128)(2,1)S(1)}, bf16[4,512,256]{2,1,0:T(8,128)(2,1)}, u32[]{:S(2)}) copy-start(bf16[4,512,256]{2,1,0:T(8,128)(2,1)} %copy-done.3) | copy-start | bytes 3145732
  88.8 7.9 %copy-start.7 = (bf16[4,512,256]{2,1,0:T(8,128)(2,1)S(1)}, bf16[4,512,256]{2,1,0:T(8,128)(2,1)}, u32[]{:S(2)}) copy-start(bf16[4,512,256]{2,1,0:T(8,128)(2,1)} %copy-done.6) | copy-start | bytes 3145732
  89.6 13.7 %collective-permute-start.19 = (bf16[704,256]{1,0:T(8,128)(2,1)S(1)}, bf16[704,256]{1,0:T(8,128)(2,1)S(1)}, u32[]{:S(2)}, u32[]{:S(2)}) collective-permute-start(bf16[704,256]{1,0:T(8,128)(2,1)S(1)} %unpack.1.after.refs_0_), channel_id=1, source_target_pairs={{0,12},{2,14},{4,0},{6,2},{8,4},{10,6},{12,8},{14,10},{1,13},{3,15... | collective-permute-start | bytes 1081352 | tf_op jit(solution)/shard_map/ppermute | solution.py:407
  96.0 9.3 %collective-permute-start.20 = (bf16[704,256]{1,0:T(8,128)(2,1)S(1)}, bf16[704,256]{1,0:T(8,128)(2,1)S(1)}, u32[]{:S(2)}, u32[]{:S(2)}) collective-permute-start(bf16[704,256]{1,0:T(8,128)(2,1)S(1)} %unpack.1.after.refs_0_), channel_id=1, source_target_pairs={{0,8},{2,10},{4,12},{6,14},{8,0},{10,2},{12,4},{14,6},{1,9},{3,11}... | collective-permute-start | bytes 1081352 | tf_op jit(solution)/shard_map/ppermute | solution.py:408
  96.6 19.0 %collective-permute-start.21 = (bf16[704,256]{1,0:T(8,128)(2,1)S(1)}, bf16[704,256]{1,0:T(8,128)(2,1)S(1)}, u32[]{:S(2)}, u32[]{:S(2)}) collective-permute-start(bf16[704,256]{1,0:T(8,128)(2,1)S(1)} %unpack.1.after.refs_0_), channel_id=1, source_target_pairs={{0,4},{2,6},{4,8},{6,10},{8,12},{10,14},{12,0},{14,2},{1,5},{3,7},... | collective-permute-start | bytes 1081352 | tf_op jit(solution)/shard_map/ppermute | solution.py:409
  96.7 1.2 copy-start.13
  97.9 1.0 copy-start.16
  103.2 15.9 %copy-start.14 = (bf16[4,128,1024]{2,1,0:T(8,128)(2,1)S(1)}, bf16[4,128,1024]{2,1,0:T(8,128)(2,1)}, u32[]{:S(2)}) copy-start(bf16[4,128,1024]{2,1,0:T(8,128)(2,1)} %copy-done.12) | copy-start | bytes 3145732
  103.2 15.9 %copy-start.17 = (s32[16,11]{1,0:T(8,128)S(1)}, s32[16,11]{1,0:T(8,128)}, u32[]{:S(2)}) copy-start(s32[16,11]{1,0:T(8,128)} %requests.1) | copy-start | bytes 2116
  115.7 3.4 %collective-permute-start.22 = (bf16[4,704,256]{2,1,0:T(8,128)(2,1)S(1)}, bf16[4,704,256]{2,1,0:T(8,128)(2,1)S(1)}, u32[]{:S(2)}, u32[]{:S(2)}) collective-permute-start(bf16[4,704,256]{2,1,0:T(8,128)(2,1)S(1)} %relay.3.mine), channel_id=1, source_target_pairs={{0,2},{2,0},{4,6},{6,4},{8,10},{10,8},{12,14},{14,12},{1,3},{3,1},... | collective-permute-start | bytes 4325384 | tf_op jit(solution)/shard_map/ppermute | solution.py:413

commit v2 on v1

--- a/solution.py
+++ b/solution.py
@@ -33,6 +33,7 @@
 XDOWN = [(i, (i - 2) % 8) for i in range(8)]
 XFAR = [(i, (i + 4) % 8) for i in range(8)]
 HEAD = [(0, 1), (1, 0)]
+DIAGONAL = [(i, i ^ 5) for i in range(16)]
 ANY = pl.BlockSpec(memory_space=pl.ANY)
 SMEM = pl.BlockSpec(memory_space=pltpu.SMEM)
 VMEM = pl.BlockSpec(memory_space=pltpu.VMEM)
@@ -100,25 +101,25 @@
         unpack_kernel,
         name="unpack",
         out_shape=bf16(HITS * HALF, 2 * HD),
-        in_specs=[SMEM, VMEM, VMEM],
+        in_specs=[SMEM, VMEM, ANY],
         out_specs=VMEM,
         compiler_params=params(),
         cost_estimate=cost(0, 2**20),
     )(hosts, arrived, after)
 
 
-def project_near_kernel(*refs):
-    hidden, weights = refs[:8], refs[8:15]
-    partial, far_hidden, hid, wts = refs[15:]
+def project_near_kernel(mine, theirs, *refs):
+    weights = refs[:7]
+    partial, far_hidden, hid, wts = refs[-4:]
     head = lax.axis_index("head")
     quarter = lax.rem(lax.axis_index("seq"), 4)
     z = lax.axis_index("cache") // 2
     far = pl.multiple_of(lax.rem(z + 4, 8) * 512, 512)
-    for i in range(8):
-        half, rel = i // 4, i % 4
-        tokens = pl.multiple_of(jnp.bitwise_xor(quarter, rel) * TOK, TOK)
-        columns = pl.multiple_of(jnp.bitwise_xor(head, half) * 2048, 2048)
-        hid[pl.ds(tokens, TOK), pl.ds(columns, 2048)] = hidden[i][...]
+    for i in range(4):
+        columns = pl.multiple_of(jnp.bitwise_xor(head, i // 2) * 2048, 2048)
+        for flip, block in enumerate((mine, theirs)):
+            tokens = pl.multiple_of(jnp.bitwise_xor(quarter, 2 * (i % 2) + flip) * TOK, TOK)
+            hid[pl.ds(tokens, TOK), pl.ds(columns, 2048)] = block[i]
     for i, shift in enumerate((0, -1, 1, -2, 2, -3, 3)):
         row = pl.multiple_of(lax.rem(z + shift + 8, 8) * 512, 512)
         wts[pl.ds(row, 512)] = weights[i][...]
@@ -127,12 +128,12 @@
     far_hidden[...] = hid[:, pl.ds(far, 512)]
 
 
-def project_near(hidden, weights):
+def project_near(mine, theirs, weights):
     return pl.pallas_call(
         project_near_kernel,
         name="project_near",
         out_shape=(f32(4 * TOK, 2 * HD), bf16(4 * TOK, 512)),
-        in_specs=[VMEM] * 15,
+        in_specs=[VMEM] * 9,
         out_specs=(VMEM, VMEM),
         scratch_shapes=[
             pltpu.VMEM((4 * TOK, 4096), jnp.bfloat16),
@@ -140,7 +141,7 @@
         ],
         compiler_params=params(),
         cost_estimate=cost(2 * 512 * 3584 * 256, 6 * 2**20),
-    )(*hidden, *weights)
+    )(mine, theirs, *weights)
 
 
 def project_far_kernel(partial, far_hidden, weights, out):
@@ -241,12 +242,42 @@
     )(*blocks, *after)
 
 
-def stage_kernel(hidden, own_cols, near_cols, queries, query_seg, key_seg, hosts, pool, sent, both, rows, bias):
-    seq = lax.axis_index("seq")
+def stage_kernel(hidden, pool, sent):
+    sent[...] = hidden[...]
+
+
+def stage(hidden, pool):
+    return pl.pallas_call(
+        stage_kernel,
+        name="stage",
+        out_shape=bf16(*hidden.shape),
+        in_specs=[VMEM, VMEM],
+        out_specs=VMEM,
+        compiler_params=params(),
+        cost_estimate=cost(0, 2**20),
+    )(hidden, pool)
+
+
+def order_kernel(own_cols, near_cols, hosts, pool, both):
     odd = lax.rem(lax.axis_index("cache"), 2)
-    sent[...] = hidden[...]
     both[pl.ds(pl.multiple_of(odd * 256, 256), 256)] = own_cols[...]
     both[pl.ds(pl.multiple_of(256 - odd * 256, 256), 256)] = near_cols[...]
+
+
+def order(own_cols, near_cols, hosts, pool):
+    return pl.pallas_call(
+        order_kernel,
+        name="order",
+        out_shape=bf16(512, 2 * HD),
+        in_specs=[VMEM, VMEM, SMEM, VMEM],
+        out_specs=VMEM,
+        compiler_params=params(),
+        cost_estimate=cost(0, 2**19),
+    )(own_cols, near_cols, hosts, pool)
+
+
+def prepare_kernel(queries, query_seg, key_seg, after, rows, bias):
+    seq = lax.axis_index("seq")
     for g in range(HEADS):
         for chunk in range(CHUNKS):
             column = (g * GROUP + chunk % GROUP) * HD
@@ -262,21 +293,16 @@
         bias[block // 2, (block % 2) * TOK : (block % 2 + 1) * TOK] = jnp.where(allowed, 0.0, MASKED)
 
 
-def stage(hidden, own_cols, near_cols, queries, query_seg, key_seg, hosts, pool):
-    return pl.pallas_call(
-        stage_kernel,
-        name="stage",
-        out_shape=(
-            bf16(*hidden.shape),
-            bf16(512, 2 * HD),
-            bf16(HEADS, HD, ROWS),
-            f32(4, 2 * TOK, TOK),
-        ),
-        in_specs=[VMEM] * 6 + [SMEM, VMEM],
-        out_specs=(VMEM,) * 4,
+def prepare(queries, query_seg, key_seg, after):
+    return pl.pallas_call(
+        prepare_kernel,
+        name="prepare",
+        out_shape=(bf16(HEADS, HD, ROWS), f32(4, 2 * TOK, TOK)),
+        in_specs=[VMEM] * 4,
+        out_specs=(VMEM,) * 2,
         compiler_params=params(),
         cost_estimate=cost(0, 3 * 2**20),
-    )(hidden, own_cols, near_cols, queries, query_seg, key_seg, hosts, pool)
+    )(queries, query_seg, key_seg, after)
 
 
 def ring_place():
@@ -425,9 +451,8 @@
     pool = lax.dynamic_slice(
         kv_pool, (0, (seq // 4) * HALF, 0, quarter * HD), (kv_pool.shape[0], HALF, 2, HD)
     ).reshape(kv_pool.shape[0], HALF, 2 * HD)
-    mine, both, rows, bias = stage(
-        hidden[0], own_cols, near_cols, queries[:, 0], query_seg, segments.reshape(8, TOK), hosts, pool
-    )
+    sent = stage(hidden[0], pool)
+    both = order(own_cols, near_cols, hosts, pool)
     ups, downs = [both], [both]
     for step in range(3):
         ups.append(lax.ppermute(ups[-1], "cache", CACHE_UP))
@@ -435,18 +460,19 @@
     far = lax.ppermute(ups[3], "cache", CACHE_UP)
     weights = [both, ups[1], downs[1], ups[2], downs[2], ups[3], downs[3]]
 
-    other = lax.ppermute(mine, "head", HEAD)
-    hidden_rows = []
-    for half in (mine, other):
-        across = lax.ppermute(half, "seq", XPAIR)
-        hidden_rows += [half, lax.ppermute(half, "seq", CORE), across, lax.ppermute(across, "seq", CORE)]
-
-
-    partial, far_hidden = project_near(hidden_rows, weights)
+    across = lax.ppermute(hidden[0], "seq", XPAIR)
+    other = lax.ppermute(sent, "head", HEAD)
+    diagonal = lax.ppermute(sent, ("seq", "head"), DIAGONAL)
+    hidden_mine = relay([sent, across, other, diagonal], (ups[3], downs[3]))
+    hidden_theirs = lax.ppermute(hidden_mine, "seq", CORE)
+
+    partial, far_hidden = project_near(hidden_mine, hidden_theirs, weights)
     block = project_far(partial, far_hidden, far)
     packed = pack(hosts, hit_page, pool, block)
     arrived = lax.all_to_all(packed, "cache", split_axis=0, concat_axis=0, tiled=True)
     new_mine, new_theirs = seq_gather(block)
+    rows, bias = prepare(queries[:, 0], query_seg, segments.reshape(8, TOK), new_mine)
+
     prefix = unpack(hosts, arrived, new_theirs)
     own, *state = attend_new(segments, rows, bias, new_mine, new_theirs, prefix)
     page_mine, page_theirs = seq_gather(prefix, state[0])

time: 128 us -> 123 us (0.961); the launches traced: 128 us -> 121 us
  waiting for transfers between devices: 45.3 us -> 57.2 us
  starting transfers between devices: 48.3 us -> 37.9 us
  local copies, waits for them, and re-layouts: 14.6 us -> 6.48 us
    unnamed x38 -> x20, local copies, waits for them, and re-layouts: 10.7 us -> 4.98 us
    all_to_all x1, waiting for transfers between devices: 0.01 us -> 5.39 us  [on_device(): lax.all_to_all(packed, 'cache', split_axis=0, concat_axis=0, tiled=True)]
    ppermute x7 -> x4, starting transfers between devices: 12.1 us -> 7.31 us  [the longest x1 3.03 us: on_device(): hidden_theirs = lax.ppermute(hidden_mine, 'seq', CORE)]
    ppermute x2, starting transfers between devices: 9.49 us -> 5.11 us  [seq_gather(): lax.ppermute(block, 'seq', XDOWN)]
    ppermute x7 -> x4, waiting for transfers between devices: 8.7 us -> 12.4 us  [the longest x1 10.7 us: on_device(): other = lax.ppermute(sent, 'head', HEAD)]
    ppermute x2, waiting for transfers between devices: 2.14 us -> 5.56 us  [seq_gather(): lax.ppermute(block, 'seq', XFAR)]
    pallas_call x1, Pallas kernels: 8.87 us -> 5.51 us  [attend_pages(): pl.pallas_call(attend_pages_kernel, name='attend_pages', out_shape=bf16(L...]
    ppermute x3, waiting for transfers between devices: 6.63 us -> 3.32 us  [on_device(): ups.append(lax.ppermute(ups[-1], 'cache', CACHE_UP))]
  transfers between devices with their start and end apart: 24 -> 21, of which waited for: 11 -> 15; matrix products, arithmetic and copies ran while one was open for 3% -> 1% of each run, Pallas kernels for 5% -> 5%
where the time goes in v2:
time: 123 us; the launch traced here: 121 us
  waiting for transfers between devices  57.2 us (47%)
  starting transfers between devices  37.9 us (31%)
  Pallas kernels  18.3 us (15%)
  local copies, waits for them, and re-layouts  6.48 us (5%)
    ppermute x2, waiting for transfers between devices, seq_gather(): lax.ppermute(block, 'seq', XUP)  16.5 us
    ppermute x1, waiting for transfers between devices, on_device(): other = lax.ppermute(sent, 'head', HEAD)  10.7 us
    ppermute x3, starting transfers between devices, on_device(): ups.append(lax.ppermute(ups[-1], 'cache', CACHE_UP))  9.47 us
    all_to_all x1, starting transfers between devices, on_device(): lax.all_to_all(packed, 'cache', split_axis=0, concat_axis=0, tiled=True)  8.65 us
    ppermute x2, waiting for transfers between devices, seq_gather(): lax.ppermute(block, 'seq', XFAR)  5.56 us
    pallas_call x1, Pallas kernels, attend_pages(): pl.pallas_call(attend_pages_kernel, name='attend_pages', out_shape=bf16(L...  5.51 us
    all_to_all x1, waiting for transfers between devices, on_device(): lax.all_to_all(packed, 'cache', split_axis=0, concat_axis=0, tiled=True)  5.39 us
    ppermute x2, waiting for transfers between devices, seq_gather(): return (mine, lax.ppermute(mine, 'seq', CORE))  5.14 us
  transfers between devices with their start and end apart: 21, of which 15 were waited for; matrix products, arithmetic and copies ran while one was open for 1% of the time, Pallas kernels for 5%

profile of v2, /device:TPU:97, one launch (start us, length us, event | category | flops | bytes accessed | tf_op | source)
XLA Modules:
  0.0 120.7 jit_solution(1222285320413804465)
XLA Ops:
  0.7 1.2 constant_dynamic-slice_fusion
  1.8 1.4 %collective-permute-start.3 = (bf16[256,256]{1,0:T(8,128)(2,1)S(1)}, bf16[256,256]{1,0:T(8,128)(2,1)S(1)}, u32[]{:S(2)}, u32[]{:S(2)}) collective-permute-start(bf16[256,256]{1,0:T(8,128)(2,1)S(1)} %bitcast.14), channel_id=1, source_target_pairs={{0,16},{16,0},{32,48},{48,32},{64,80},{80,64},{96,112},{112,96},{1... | collective-permute-start | bytes 393224 | tf_op jit(solution)/shard_map/ppermute | solution.py:449
  3.6 0.8 copy.10
  4.4 1.9 %collective-permute-done.3.near_cols = bf16[256,256]{1,0:T(8,128)(2,1)S(1)} collective-permute-done((bf16[256,256]{1,0:T(8,128)(2,1)S(1)}, bf16[256,256]{1,0:T(8,128)(2,1)S(1)}, u32[]{:S(2)}, u32[]{:S(2)}) %collective-permute-start.3) | collective-permute-done | bytes 131104 | tf_op jit(solution)/shard_map/ppermute | solution.py:449
  6.3 0.7 order.1.refs_0_
  7.0 2.9 %collective-permute-start.4 = (bf16[512,256]{1,0:T(8,128)(2,1)S(1)}, bf16[512,256]{1,0:T(8,128)(2,1)S(1)}, u32[]{:S(2)}, u32[]{:S(2)}) collective-permute-start(bf16[512,256]{1,0:T(8,128)(2,1)S(1)} %order.1.refs_0_), channel_id=1, source_target_pairs={{0,32},{16,48},{32,64},{48,80},{64,96},{80,112},{96,128},{112,144}... | collective-permute-start | bytes 786440 | tf_op jit(solution)/shard_map/ppermute | solution.py:458
  10.0 3.0 %collective-permute-start.1 = (bf16[128,2048]{1,0:T(8,128)(2,1)S(1)}, bf16[128,2048]{1,0:T(8,128)(2,1)S(1)}, u32[]{:S(2)}, u32[]{:S(2)}) collective-permute-start(bf16[128,2048]{1,0:T(8,128)(2,1)S(1)} %stage.1.refs_0_), channel_id=1, source_target_pairs={{0,1},{1,0},{2,3},{3,2},{4,5},{5,4},{6,7},{7,6},{8,9},{9,8},{10,11... | collective-permute-start | bytes 1572872 | tf_op jit(solution)/shard_map/ppermute | solution.py:464
  13.0 1.0 collective-permute-start.2
  14.0 0.3 collective-permute-start
  14.3 3.1 %collective-permute-start.5 = (bf16[512,256]{1,0:T(8,128)(2,1)S(1)}, bf16[512,256]{1,0:T(8,128)(2,1)S(1)}, u32[]{:S(2)}, u32[]{:S(2)}) collective-permute-start(bf16[512,256]{1,0:T(8,128)(2,1)S(1)} %collective-permute-done.4.refs_1_), channel_id=1, source_target_pairs={{0,32},{16,48},{32,64},{48,80},{64,96},{80,112},{96,128},{112,144}... | collective-permute-start | bytes 786440 | tf_op jit(solution)/shard_map/ppermute | solution.py:458
  17.4 3.3 %collective-permute-done.5.refs_3_ = bf16[512,256]{1,0:T(8,128)(2,1)S(1)} collective-permute-done((bf16[512,256]{1,0:T(8,128)(2,1)S(1)}, bf16[512,256]{1,0:T(8,128)(2,1)S(1)}, u32[]{:S(2)}, u32[]{:S(2)}) %collective-permute-start.5) | collective-permute-done | bytes 262176 | tf_op jit(solution)/shard_map/ppermute | solution.py:458
  20.7 3.4 %collective-permute-start.6 = (bf16[512,256]{1,0:T(8,128)(2,1)S(1)}, bf16[512,256]{1,0:T(8,128)(2,1)S(1)}, u32[]{:S(2)}, u32[]{:S(2)}) collective-permute-start(bf16[512,256]{1,0:T(8,128)(2,1)S(1)} %collective-permute-done.5.refs_3_), channel_id=1, source_target_pairs={{0,32},{16,48},{32,64},{48,80},{64,96},{80,112},{96,128},{112,144}... | collective-permute-start | bytes 786440 | tf_op jit(solution)/shard_map/ppermute | solution.py:458
  24.1 10.7 %collective-permute-done.1.refs_2_ = bf16[128,2048]{1,0:T(8,128)(2,1)S(1)} collective-permute-done((bf16[128,2048]{1,0:T(8,128)(2,1)S(1)}, bf16[128,2048]{1,0:T(8,128)(2,1)S(1)}, u32[]{:S(2)}, u32[]{:S(2)}) %collective-permute-start.1) | collective-permute-done | bytes 524320 | tf_op jit(solution)/shard_map/ppermute | solution.py:464
  34.8 0.7 collective-permute-done.refs_1_
  35.6 3.0 %collective-permute-start.10 = (bf16[4,128,2048]{2,1,0:T(8,128)(2,1)S(1)}, bf16[4,128,2048]{2,1,0:T(8,128)(2,1)S(1)}, u32[]{:S(2)}, u32[]{:S(2)}) collective-permute-start(bf16[4,128,2048]{2,1,0:T(8,128)(2,1)S(1)} %relay.3.mine), channel_id=1, source_target_pairs={{0,2},{2,0},{4,6},{6,4},{8,10},{10,8},{12,14},{14,12},{1,3},{3,1},... | collective-permute-start | bytes 6291464 | tf_op jit(solution)/shard_map/ppermute | solution.py:467
  38.7 2.7 %collective-permute-start.11 = (bf16[512,256]{1,0:T(8,128)(2,1)S(1)}, bf16[512,256]{1,0:T(8,128)(2,1)S(1)}, u32[]{:S(2)}, u32[]{:S(2)}) collective-permute-start(bf16[512,256]{1,0:T(8,128)(2,1)S(1)} %collective-permute-done.6.refs_4_.refs_5_), channel_id=1, source_target_pairs={{0,32},{16,48},{32,64},{48,80},{64,96},{80,112},{96,128},{112,144}... | collective-permute-start | bytes 786440 | tf_op jit(solution)/shard_map/ppermute | solution.py:460
  41.4 1.1 collective-permute-done.10.theirs
  42.4 1.7 %project_near.1 = (f32[512,256]{1,0:T(8,128)S(1)}, bf16[512,512]{1,0:T(8,128)(2,1)S(1)}) custom-call(bf16[4,128,2048]{2,1,0:T(8,128)(2,1)S(1)} %relay.3.mine, bf16[4,128,2048]{2,1,0:T(8,128)(2,1)S(1)} %collective-permute-done.10.theirs, bf16[512,256]{1,0:T(8,128)(2,1)S(1)} %order.1.refs_0_, bf16[512,256]{1,0:T(8,128)(2,1)S(1)} %collective-permute-done.4.refs_1_, ...), custom_call_target="tpu_custom_call" | custom-call | flops 939524096 | bytes 6291456 | tf_op jit(solution)/shard_map/project_near/pallas_call | solution.py:132
  44.2 2.8 %collective-permute-done.11.weights = bf16[512,256]{1,0:T(8,128)(2,1)S(1)} collective-permute-done((bf16[512,256]{1,0:T(8,128)(2,1)S(1)}, bf16[512,256]{1,0:T(8,128)(2,1)S(1)}, u32[]{:S(2)}, u32[]{:S(2)}) %collective-permute-start.11) | collective-permute-done | bytes 262176 | tf_op jit(solution)/shard_map/ppermute | solution.py:460
  47.0 0.3 project_far.1.refs_0_
  47.3 2.5 %pack.1 = bf16[32,64,256]{2,1,0:T(8,128)(2,1)} custom-call(s32[16,11]{1,0:T(8,128)S(1)} %bitcast.19, s32[16,11]{1,0:T(8,128)S(1)} %copy-done.6, bf16[8,64,256]{2,1,0:T(8,128)(2,1)S(1)} %reshape.13.pool, bf16[512,256]{1,0:T(8,128)(2,1)S(1)} %project_far.1.refs_0_), custom_call_target="tpu_custom_call" | custom-call | bytes 2097152 | tf_op jit(solution)/shard_map/pack/pallas_call | solution.py:78
  49.8 8.7 %all-to-all-start = ((bf16[32,64,256]{2,1,0:T(8,128)(2,1)}), bf16[32,64,256]{2,1,0:T(8,128)(2,1)}, u32[]{:S(2)}, u32[]{:S(2)}) async-start(bf16[32,64,256]{2,1,0:T(8,128)(2,1)} %pack.1), calls=%async_computation | async-start | bytes 2097152 | tf_op jit(solution)/shard_map/all_to_all | solution.py:472
  58.4 2.6 %collective-permute-start.12 = (bf16[512,256]{1,0:T(8,128)(2,1)S(1)}, bf16[512,256]{1,0:T(8,128)(2,1)S(1)}, u32[]{:S(2)}, u32[]{:S(2)}) collective-permute-start(bf16[512,256]{1,0:T(8,128)(2,1)S(1)} %project_far.1.refs_0_), channel_id=1, source_target_pairs={{0,12},{2,14},{4,0},{6,2},{8,4},{10,6},{12,8},{14,10},{1,13},{3,15... | collective-permute-start | bytes 786440 | tf_op jit(solution)/shard_map/ppermute | solution.py:433
  61.0 0.5 collective-permute-start.13
  61.5 0.6 collective-permute-start.14
  62.1 3.8 %collective-permute-done.12.refs_1_ = bf16[512,256]{1,0:T(8,128)(2,1)S(1)} collective-permute-done((bf16[512,256]{1,0:T(8,128)(2,1)S(1)}, bf16[512,256]{1,0:T(8,128)(2,1)S(1)}, u32[]{:S(2)}, u32[]{:S(2)}) %collective-permute-start.12) | collective-permute-done | bytes 262176 | tf_op jit(solution)/shard_map/ppermute | solution.py:433
  65.9 2.8 %collective-permute-done.13.refs_2_ = bf16[512,256]{1,0:T(8,128)(2,1)S(1)} collective-permute-done((bf16[512,256]{1,0:T(8,128)(2,1)S(1)}, bf16[512,256]{1,0:T(8,128)(2,1)S(1)}, u32[]{:S(2)}, u32[]{:S(2)}) %collective-permute-start.13) | collective-permute-done | bytes 262176 | tf_op jit(solution)/shard_map/ppermute | solution.py:434
  68.8 7.7 %collective-permute-done.14.refs_3_ = bf16[512,256]{1,0:T(8,128)(2,1)S(1)} collective-permute-done((bf16[512,256]{1,0:T(8,128)(2,1)S(1)}, bf16[512,256]{1,0:T(8,128)(2,1)S(1)}, u32[]{:S(2)}, u32[]{:S(2)}) %collective-permute-start.14) | collective-permute-done | bytes 262176 | tf_op jit(solution)/shard_map/ppermute | solution.py:435
  76.5 0.5 collective-permute-start.15
  77.0 2.3 %collective-permute-done.15.after.theirs = bf16[4,512,256]{2,1,0:T(8,128)(2,1)S(1)} collective-permute-done((bf16[4,512,256]{2,1,0:T(8,128)(2,1)S(1)}, bf16[4,512,256]{2,1,0:T(8,128)(2,1)S(1)}, u32[]{:S(2)}, u32[]{:S(2)}) %collective-permute-start.15) | collective-permute-done | bytes 1048608 | tf_op jit(solution)/shard_map/ppermute | solution.py:439
  79.3 1.0 copy-done.2
  80.2 5.4 %all-to-all-done.arrived = bf16[32,64,256]{2,1,0:T(8,128)(2,1)} async-done(((bf16[32,64,256]{2,1,0:T(8,128)(2,1)}), bf16[32,64,256]{2,1,0:T(8,128)(2,1)}, u32[]{:S(2)}, u32[]{:S(2)}) %all-to-all-start) | async-done | bytes 1048608 | tf_op jit(solution)/shard_map/all_to_all | solution.py:472
  85.6 1.2 %copy-done.3 = bf16[4,512,256]{2,1,0:T(8,128)(2,1)S(1)} copy-done((bf16[4,512,256]{2,1,0:T(8,128)(2,1)S(1)}, bf16[4,512,256]{2,1,0:T(8,128)(2,1)}, u32[]{:S(2)}) %copy-start.3) | copy-done | bytes 1048600
  86.9 1.3 %unpack.1.after.refs_0_ = bf16[704,256]{1,0:T(8,128)(2,1)S(1)} custom-call(s32[16,11]{1,0:T(8,128)S(1)} %bitcast.20, bf16[32,64,256]{2,1,0:T(8,128)(2,1)} %all-to-all-done.arrived, bf16[4,512,256]{2,1,0:T(8,128)(2,1)S(1)} %copy-done.3), custom_call_target="tpu_custom_call" | custom-call | bytes 1048576 | tf_op jit(solution)/shard_map/unpack/pallas_call | solution.py:100
  88.2 2.6 %collective-permute-start.16 = (bf16[704,256]{1,0:T(8,128)(2,1)S(1)}, bf16[704,256]{1,0:T(8,128)(2,1)}, u32[]{:S(2)}, u32[]{:S(2)}) collective-permute-start(bf16[704,256]{1,0:T(8,128)(2,1)S(1)} %unpack.1.after.refs_0_), channel_id=1, source_target_pairs={{0,12},{2,14},{4,0},{6,2},{8,4},{10,6},{12,8},{14,10},{1,13},{3,15... | collective-permute-start | bytes 1081352 | tf_op jit(solution)/shard_map/ppermute | solution.py:433
  90.8 0.5 collective-permute-start.17
  91.3 0.6 collective-permute-start.18
  91.9 1.2 %copy-done.1 = bf16[2,1,128,2048]{3,2,1,0:T(8,128)(2,1)S(1)} copy-done((bf16[2,1,128,2048]{3,2,1,0:T(8,128)(2,1)S(1)}, bf16[2,1,128,2048]{3,2,1,0:T(8,128)(2,1)}, u32[]{:S(2)}) %copy-start.1) | copy-done | bytes 1048600
  93.1 0.5 prepare.1
  93.6 0.7 copy-done.4
  94.3 4.3 %attend_new.1 = (bf16[128,2,512]{2,1,0:T(2,128)(2,1)}, f32[4,8,1024]{2,1,0:T(8,128)S(1)}, f32[4,8,1024]{2,1,0:T(8,128)S(1)}, f32[4,128,1024]{2,1,0:T(8,128)S(1)}) custom-call(s32[1024]{0:T(1024)S(1)} %bitcast.22, bf16[4,128,1024]{2,1,0:T(8,128)(2,1)S(1)} %get-tuple-element.12.rows, f32[4,256,128]{2,1,0:T(8,128)S(1)} %get-tuple-element.13.bias, ...), custom_call_target="tpu_custom_call" | custom-call | flops 2000000000 | bytes 6291456 | tf_op jit(solution)/shard_map/attend_new/pallas_call | solution.py:348
  98.6 0.2 collective-permute-done.16.refs_1_
  98.8 2.7 %collective-permute-done.17.refs_2_ = bf16[704,256]{1,0:T(8,128)(2,1)} collective-permute-done((bf16[704,256]{1,0:T(8,128)(2,1)S(1)}, bf16[704,256]{1,0:T(8,128)(2,1)}, u32[]{:S(2)}, u32[]{:S(2)}) %collective-permute-start.17) | collective-permute-done | bytes 360480 | tf_op jit(solution)/shard_map/ppermute | solution.py:434
  101.6 8.9 %collective-permute-done.18.refs_3_ = bf16[704,256]{1,0:T(8,128)(2,1)} collective-permute-done((bf16[704,256]{1,0:T(8,128)(2,1)S(1)}, bf16[704,256]{1,0:T(8,128)(2,1)}, u32[]{:S(2)}, u32[]{:S(2)}) %collective-permute-start.18) | collective-permute-done | bytes 360480 | tf_op jit(solution)/shard_map/ppermute | solution.py:435
  110.4 1.3 %relay.5.mine = bf16[4,704,256]{2,1,0:T(8,128)(2,1)S(1)} custom-call(bf16[704,256]{1,0:T(8,128)(2,1)S(1)} %unpack.1.after.refs_0_, bf16[704,256]{1,0:T(8,128)(2,1)} %collective-permute-done.16.refs_1_, bf16[704,256]{1,0:T(8,128)(2,1)} %collective-permute-done.17.refs_2_, bf16[704,256]{1,0:T(8,128)(2,1)} %collective-permute-done.18.refs_3_, ...), custom_call_target="tpu_custom_call" | custom-call | bytes 2097152 | tf_op jit(solution)/shard_map/relay/pallas_call | solution.py:234
  111.7 0.6 collective-permute-start.19
  112.3 2.8 %collective-permute-done.19.theirs = bf16[4,704,256]{2,1,0:T(8,128)(2,1)S(1)} collective-permute-done((bf16[4,704,256]{2,1,0:T(8,128)(2,1)S(1)}, bf16[4,704,256]{2,1,0:T(8,128)(2,1)S(1)}, u32[]{:S(2)}, u32[]{:S(2)}) %collective-permute-start.19) | collective-permute-done | bytes 1441824 | tf_op jit(solution)/shard_map/ppermute | solution.py:439
  115.2 5.5 %attend_pages.1 = bf16[2,128,2048]{2,1,0:T(8,128)(2,1)} custom-call(s32[16,11]{1,0:T(8,128)S(1)} %copy-done.8, s32[1024]{0:T(1024)S(1)} %bitcast.23, s32[1,128]{1,0:T(1,128)S(1)} %constant_dynamic-slice_fusion.2.query_seg, bf16[4,128,1024]{2,1,0:T(8,128)(2,1)S(1)} %get-tuple-element.12.rows, f32[4,8,1024]{2,1,0:T(8,128)S(1)} %get-tuple-element.14.refs_4_.peak_in, ...), custom_call_target="tpu_custom_call" | custom-call | flops 3000000000 | bytes 6291456 | tf_op jit(solution)/shard_map/attend_pages/pallas_call | solution.py:412
  (30 shorter events, 0.7 us)
Async XLA Ops:
  0.6 2.6 %copy-start = (bf16[8,128,2,512]{3,2,1,0:T(2,128)(2,1)S(1)}, bf16[8,128,2,512]{3,2,1,0:T(2,128)(2,1)}, u32[]{:S(2)}) copy-start(bf16[8,128,2,512]{3,2,1,0:T(2,128)(2,1)} %param.11) | copy-start | bytes 6291460
  0.6 9.3 %copy-start.5 = (bf16[1,128,2048]{2,1,0:T(8,128)(2,1)S(1)}, bf16[1,128,2048]{2,1,0:T(8,128)(2,1)}, u32[]{:S(2)}) copy-start(bf16[1,128,2048]{2,1,0:T(8,128)(2,1)} %param.8) | copy-start | bytes 1572868
  1.8 4.5 %collective-permute-start.3 = (bf16[256,256]{1,0:T(8,128)(2,1)S(1)}, bf16[256,256]{1,0:T(8,128)(2,1)S(1)}, u32[]{:S(2)}, u32[]{:S(2)}) collective-permute-start(bf16[256,256]{1,0:T(8,128)(2,1)S(1)} %bitcast.14), channel_id=1, source_target_pairs={{0,16},{16,0},{32,48},{48,32},{64,80},{80,64},{96,112},{112,96},{1... | collective-permute-start | bytes 393224 | tf_op jit(solution)/shard_map/ppermute | solution.py:449
  7.0 7.3 %collective-permute-start.4 = (bf16[512,256]{1,0:T(8,128)(2,1)S(1)}, bf16[512,256]{1,0:T(8,128)(2,1)S(1)}, u32[]{:S(2)}, u32[]{:S(2)}) collective-permute-start(bf16[512,256]{1,0:T(8,128)(2,1)S(1)} %order.1.refs_0_), channel_id=1, source_target_pairs={{0,32},{16,48},{32,64},{48,80},{64,96},{80,112},{96,128},{112,144}... | collective-permute-start | bytes 786440 | tf_op jit(solution)/shard_map/ppermute | solution.py:458
  9.9 7.5 %collective-permute-start.7 = (bf16[512,256]{1,0:T(8,128)(2,1)S(1)}, bf16[512,256]{1,0:T(8,128)(2,1)S(1)}, u32[]{:S(2)}, u32[]{:S(2)}) collective-permute-start(bf16[512,256]{1,0:T(8,128)(2,1)S(1)} %order.1.refs_0_), channel_id=1, source_target_pairs={{0,224},{16,240},{32,0},{48,16},{64,32},{80,48},{96,64},{112,80},{... | collective-permute-start | bytes 786440 | tf_op jit(solution)/shard_map/ppermute | solution.py:459
  10.0 24.8 %collective-permute-start.1 = (bf16[128,2048]{1,0:T(8,128)(2,1)S(1)}, bf16[128,2048]{1,0:T(8,128)(2,1)S(1)}, u32[]{:S(2)}, u32[]{:S(2)}) collective-permute-start(bf16[128,2048]{1,0:T(8,128)(2,1)S(1)} %stage.1.refs_0_), channel_id=1, source_target_pairs={{0,1},{1,0},{2,3},{3,2},{4,5},{5,4},{6,7},{7,6},{8,9},{9,8},{10,11... | collective-permute-start | bytes 1572872 | tf_op jit(solution)/shard_map/ppermute | solution.py:464
  13.0 21.8 %collective-permute-start.2 = (bf16[128,2048]{1,0:T(8,128)(2,1)S(1)}, bf16[128,2048]{1,0:T(8,128)(2,1)S(1)}, u32[]{:S(2)}, u32[]{:S(2)}) collective-permute-start(bf16[128,2048]{1,0:T(8,128)(2,1)S(1)} %stage.1.refs_0_), channel_id=1, source_target_pairs={{0,5},{1,4},{2,7},{3,6},{4,1},{5,0},{6,3},{7,2},{8,13},{9,12},{10,... | collective-permute-start | bytes 1572872 | tf_op jit(solution)/shard_map/ppermute | solution.py:465
  14.0 21.5 %collective-permute-start = (bf16[128,2048]{1,0:T(8,128)(2,1)S(1)}, bf16[128,2048]{1,0:T(8,128)(2,1)S(1)}, u32[]{:S(2)}, u32[]{:S(2)}) collective-permute-start(bf16[128,2048]{1,0:T(8,128)(2,1)S(1)} %bitcast.17), channel_id=1, source_target_pairs={{0,4},{2,6},{4,0},{6,2},{8,12},{10,14},{12,8},{14,10},{1,5},{3,7},... | collective-permute-start | bytes 1572872 | tf_op jit(solution)/shard_map/ppermute | solution.py:463
  14.3 6.4 %collective-permute-start.5 = (bf16[512,256]{1,0:T(8,128)(2,1)S(1)}, bf16[512,256]{1,0:T(8,128)(2,1)S(1)}, u32[]{:S(2)}, u32[]{:S(2)}) collective-permute-start(bf16[512,256]{1,0:T(8,128)(2,1)S(1)} %collective-permute-done.4.refs_1_), channel_id=1, source_target_pairs={{0,32},{16,48},{32,64},{48,80},{64,96},{80,112},{96,128},{112,144}... | collective-permute-start | bytes 786440 | tf_op jit(solution)/shard_map/ppermute | solution.py:458
  17.4 6.7 %collective-permute-start.8 = (bf16[512,256]{1,0:T(8,128)(2,1)S(1)}, bf16[512,256]{1,0:T(8,128)(2,1)S(1)}, u32[]{:S(2)}, u32[]{:S(2)}) collective-permute-start(bf16[512,256]{1,0:T(8,128)(2,1)S(1)} %collective-permute-done.7.refs_2_), channel_id=1, source_target_pairs={{0,224},{16,240},{32,0},{48,16},{64,32},{80,48},{96,64},{112,80},{... | collective-permute-start | bytes 786440 | tf_op jit(solution)/shard_map/ppermute | solution.py:459
  20.7 14.8 %collective-permute-start.6 = (bf16[512,256]{1,0:T(8,128)(2,1)S(1)}, bf16[512,256]{1,0:T(8,128)(2,1)S(1)}, u32[]{:S(2)}, u32[]{:S(2)}) collective-permute-start(bf16[512,256]{1,0:T(8,128)(2,1)S(1)} %collective-permute-done.5.refs_3_), channel_id=1, source_target_pairs={{0,32},{16,48},{32,64},{48,80},{64,96},{80,112},{96,128},{112,144}... | collective-permute-start | bytes 786440 | tf_op jit(solution)/shard_map/ppermute | solution.py:458
  24.1 11.4 %collective-permute-start.9 = (bf16[512,256]{1,0:T(8,128)(2,1)S(1)}, bf16[512,256]{1,0:T(8,128)(2,1)S(1)}, u32[]{:S(2)}, u32[]{:S(2)}) collective-permute-start(bf16[512,256]{1,0:T(8,128)(2,1)S(1)} %collective-permute-done.8.refs_4_), channel_id=1, source_target_pairs={{0,224},{16,240},{32,0},{48,16},{64,32},{80,48},{96,64},{112,80},{... | collective-permute-start | bytes 786440 | tf_op jit(solution)/shard_map/ppermute | solution.py:459
  35.6 11.7 %copy-start.6 = (s32[16,11]{1,0:T(8,128)S(1)}, s32[16,11]{1,0:T(8,128)}, u32[]{:S(2)}) copy-start(s32[16,11]{1,0:T(8,128)} %pages.1) | copy-start | bytes 2116
  35.6 6.8 %collective-permute-start.10 = (bf16[4,128,2048]{2,1,0:T(8,128)(2,1)S(1)}, bf16[4,128,2048]{2,1,0:T(8,128)(2,1)S(1)}, u32[]{:S(2)}, u32[]{:S(2)}) collective-permute-start(bf16[4,128,2048]{2,1,0:T(8,128)(2,1)S(1)} %relay.3.mine), channel_id=1, source_target_pairs={{0,2},{2,0},{4,6},{6,4},{8,10},{10,8},{12,14},{14,12},{1,3},{3,1},... | collective-permute-start | bytes 6291464 | tf_op jit(solution)/shard_map/ppermute | solution.py:467
  38.7 8.3 %collective-permute-start.11 = (bf16[512,256]{1,0:T(8,128)(2,1)S(1)}, bf16[512,256]{1,0:T(8,128)(2,1)S(1)}, u32[]{:S(2)}, u32[]{:S(2)}) collective-permute-start(bf16[512,256]{1,0:T(8,128)(2,1)S(1)} %collective-permute-done.6.refs_4_.refs_5_), channel_id=1, source_target_pairs={{0,32},{16,48},{32,64},{48,80},{64,96},{80,112},{96,128},{112,144}... | collective-permute-start | bytes 786440 | tf_op jit(solution)/shard_map/ppermute | solution.py:460
  49.8 35.9 %all-to-all-start = ((bf16[32,64,256]{2,1,0:T(8,128)(2,1)}), bf16[32,64,256]{2,1,0:T(8,128)(2,1)}, u32[]{:S(2)}, u32[]{:S(2)}) async-start(bf16[32,64,256]{2,1,0:T(8,128)(2,1)} %pack.1), calls=%async_computation | async-start | bytes 2097152 | tf_op jit(solution)/shard_map/all_to_all | solution.py:472
  58.4 33.5 %copy-start.7 = (s32[1,1024]{1,0:T(1,128)S(1)}, s32[1,1024]{1,0:T(1,128)}, u32[]{:S(2)}) copy-start(s32[1,1024]{1,0:T(1,128)} %param.15) | copy-start | bytes 12292
  58.4 7.5 %collective-permute-start.12 = (bf16[512,256]{1,0:T(8,128)(2,1)S(1)}, bf16[512,256]{1,0:T(8,128)(2,1)S(1)}, u32[]{:S(2)}, u32[]{:S(2)}) collective-permute-start(bf16[512,256]{1,0:T(8,128)(2,1)S(1)} %project_far.1.refs_0_), channel_id=1, source_target_pairs={{0,12},{2,14},{4,0},{6,2},{8,4},{10,6},{12,8},{14,10},{1,13},{3,15... | collective-permute-start | bytes 786440 | tf_op jit(solution)/shard_map/ppermute | solution.py:433
  61.0 7.8 %collective-permute-start.13 = (bf16[512,256]{1,0:T(8,128)(2,1)S(1)}, bf16[512,256]{1,0:T(8,128)(2,1)S(1)}, u32[]{:S(2)}, u32[]{:S(2)}) collective-permute-start(bf16[512,256]{1,0:T(8,128)(2,1)S(1)} %project_far.1.refs_0_), channel_id=1, source_target_pairs={{0,8},{2,10},{4,12},{6,14},{8,0},{10,2},{12,4},{14,6},{1,9},{3,11}... | collective-permute-start | bytes 786440 | tf_op jit(solution)/shard_map/ppermute | solution.py:434
  61.5 14.9 %collective-permute-start.14 = (bf16[512,256]{1,0:T(8,128)(2,1)S(1)}, bf16[512,256]{1,0:T(8,128)(2,1)S(1)}, u32[]{:S(2)}, u32[]{:S(2)}) collective-permute-start(bf16[512,256]{1,0:T(8,128)(2,1)S(1)} %project_far.1.refs_0_), channel_id=1, source_target_pairs={{0,4},{2,6},{4,8},{6,10},{8,12},{10,14},{12,0},{14,2},{1,5},{3,7},... | collective-permute-start | bytes 786440 | tf_op jit(solution)/shard_map/ppermute | solution.py:435
  76.5 2.8 %collective-permute-start.15 = (bf16[4,512,256]{2,1,0:T(8,128)(2,1)S(1)}, bf16[4,512,256]{2,1,0:T(8,128)(2,1)S(1)}, u32[]{:S(2)}, u32[]{:S(2)}) collective-permute-start(bf16[4,512,256]{2,1,0:T(8,128)(2,1)S(1)} %relay.4.after.mine), channel_id=1, source_target_pairs={{0,2},{2,0},{4,6},{6,4},{8,10},{10,8},{12,14},{14,12},{1,3},{3,1},... | collective-permute-start | bytes 3145736 | tf_op jit(solution)/shard_map/ppermute | solution.py:439
  79.3 1.0 copy-start.2
  85.6 1.2 %copy-start.3 = (bf16[4,512,256]{2,1,0:T(8,128)(2,1)S(1)}, bf16[4,512,256]{2,1,0:T(8,128)(2,1)}, u32[]{:S(2)}) copy-start(bf16[4,512,256]{2,1,0:T(8,128)(2,1)} %copy-done.2) | copy-start | bytes 3145732
  88.2 10.6 %collective-permute-start.16 = (bf16[704,256]{1,0:T(8,128)(2,1)S(1)}, bf16[704,256]{1,0:T(8,128)(2,1)}, u32[]{:S(2)}, u32[]{:S(2)}) collective-permute-start(bf16[704,256]{1,0:T(8,128)(2,1)S(1)} %unpack.1.after.refs_0_), channel_id=1, source_target_pairs={{0,12},{2,14},{4,0},{6,2},{8,4},{10,6},{12,8},{14,10},{1,13},{3,15... | collective-permute-start | bytes 1081352 | tf_op jit(solution)/shard_map/ppermute | solution.py:433
  90.8 10.8 %collective-permute-start.17 = (bf16[704,256]{1,0:T(8,128)(2,1)S(1)}, bf16[704,256]{1,0:T(8,128)(2,1)}, u32[]{:S(2)}, u32[]{:S(2)}) collective-permute-start(bf16[704,256]{1,0:T(8,128)(2,1)S(1)} %unpack.1.after.refs_0_), channel_id=1, source_target_pairs={{0,8},{2,10},{4,12},{6,14},{8,0},{10,2},{12,4},{14,6},{1,9},{3,11}... | collective-permute-start | bytes 1081352 | tf_op jit(solution)/shard_map/ppermute | solution.py:434
  91.3 19.2 %collective-permute-start.18 = (bf16[704,256]{1,0:T(8,128)(2,1)S(1)}, bf16[704,256]{1,0:T(8,128)(2,1)}, u32[]{:S(2)}, u32[]{:S(2)}) collective-permute-start(bf16[704,256]{1,0:T(8,128)(2,1)S(1)} %unpack.1.after.refs_0_), channel_id=1, source_target_pairs={{0,4},{2,6},{4,8},{6,10},{8,12},{10,14},{12,0},{14,2},{1,5},{3,7},... | collective-permute-start | bytes 1081352 | tf_op jit(solution)/shard_map/ppermute | solution.py:435
  91.9 1.2 %copy-start.1 = (bf16[2,1,128,2048]{3,2,1,0:T(8,128)(2,1)S(1)}, bf16[2,1,128,2048]{3,2,1,0:T(8,128)(2,1)}, u32[]{:S(2)}) copy-start(bf16[2,1,128,2048]{3,2,1,0:T(8,128)(2,1)} %param.10) | copy-start | bytes 3145732
  93.1 1.2 %copy-start.4 = (bf16[4,512,256]{2,1,0:T(8,128)(2,1)S(1)}, bf16[4,512,256]{2,1,0:T(8,128)(2,1)}, u32[]{:S(2)}) copy-start(bf16[4,512,256]{2,1,0:T(8,128)(2,1)} %copy-done.2) | copy-start | bytes 3145732
  98.6 16.5 %copy-start.8 = (s32[16,11]{1,0:T(8,128)S(1)}, s32[16,11]{1,0:T(8,128)}, u32[]{:S(2)}) copy-start(s32[16,11]{1,0:T(8,128)} %requests.1) | copy-start | bytes 2116
  111.7 3.4 %collective-permute-start.19 = (bf16[4,704,256]{2,1,0:T(8,128)(2,1)S(1)}, bf16[4,704,256]{2,1,0:T(8,128)(2,1)S(1)}, u32[]{:S(2)}, u32[]{:S(2)}) collective-permute-start(bf16[4,704,256]{2,1,0:T(8,128)(2,1)S(1)} %relay.5.mine), channel_id=1, source_target_pairs={{0,2},{2,0},{4,6},{6,4},{8,10},{10,8},{12,14},{14,12},{1,3},{3,1},... | collective-permute-start | bytes 4325384 | tf_op jit(solution)/shard_map/ppermute | solution.py:439

commit v3 on v2

--- a/solution.py
+++ b/solution.py
@@ -224,22 +224,39 @@
     add(len(steps) - 1, *held)
 
 
+def hold_kernel(*refs):
+    pass
+
+
+def hold(array, *after):
+    return pl.pallas_call(
+        hold_kernel,
+        name="hold",
+        out_shape=bf16(*array.shape),
+        in_specs=[ANY] * (1 + len(after)),
+        out_specs=ANY,
+        input_output_aliases={0: 0},
+        compiler_params=params(),
+        cost_estimate=cost(0, 1),
+    )(array, *after)
+
+
 def relay_kernel(*refs):
     out = refs[-1]
     for i in range(4):
         out[i] = refs[i][...]
 
 
-def relay(blocks, after):
+def relay(blocks, after, late=()):
     return pl.pallas_call(
         relay_kernel,
         name="relay",
         out_shape=bf16(4, *blocks[0].shape),
-        in_specs=[VMEM] * 4 + [VMEM] * len(after),
+        in_specs=[VMEM] * 4 + [VMEM] * len(after) + [ANY] * len(late),
         out_specs=VMEM,
         compiler_params=params(),
         cost_estimate=cost(0, 2**21),
-    )(*blocks, *after)
+    )(*blocks, *after, *late)
 
 
 def stage_kernel(hidden, pool, sent):
@@ -312,7 +329,9 @@
     return seq, x, places
 
 
-def attend_new_kernel(segments, rows, bias, mine, theirs, after, own, peak, total, summed):
+def attend_new_kernel(segments, rows, bias, mine, far_theirs, after, own, peak, total, summed, theirs, sem):
+    copy = pltpu.make_async_copy(far_theirs, theirs, sem)
+    copy.start()
     seq, x, places = ring_place()
     refs = (mine, theirs)
     low = segments[seq * TOK]
@@ -322,6 +341,7 @@
         first = first + (segments[k * 2 * TOK + 2 * TOK - 1] < low).astype(jnp.int32)
     part_rows = pl.ds(pl.multiple_of(lax.rem(seq, 4) * TOK, TOK), TOK)
     core = lax.rem(seq, 2)
+    copy.wait()
     for g in range(HEADS):
         shift = lax.rem((x // 2) * 2 + g // 2 - x + 4, 4)
         flip = jnp.bitwise_xor(core, g % 2)
@@ -354,8 +374,9 @@
             f32(HEADS, 8, ROWS),
             f32(HEADS, HD, ROWS),
         ),
-        in_specs=[SMEM] + [VMEM] * 5,
+        in_specs=[SMEM] + [VMEM] * 3 + [ANY, VMEM],
         out_specs=(VMEM,) * 4,
+        scratch_shapes=[pltpu.VMEM((4, 4 * TOK, 2 * HD), jnp.bfloat16), pltpu.SemaphoreType.DMA],
         compiler_params=params(),
         cost_estimate=cost(2 * 10**9, 6 * 2**20, 3 * 10**6),
     )(segments, rows, bias, mine, theirs, after)
@@ -463,13 +484,13 @@
     across = lax.ppermute(hidden[0], "seq", XPAIR)
     other = lax.ppermute(sent, "head", HEAD)
     diagonal = lax.ppermute(sent, ("seq", "head"), DIAGONAL)
-    hidden_mine = relay([sent, across, other, diagonal], (ups[3], downs[3]))
+    packed = pack(hosts, hit_page, pool, ups[1])
+    hidden_mine = relay([sent, across, other, diagonal], (ups[3], downs[3]), (packed,))
     hidden_theirs = lax.ppermute(hidden_mine, "seq", CORE)
 
     partial, far_hidden = project_near(hidden_mine, hidden_theirs, weights)
     block = project_far(partial, far_hidden, far)
-    packed = pack(hosts, hit_page, pool, block)
-    arrived = lax.all_to_all(packed, "cache", split_axis=0, concat_axis=0, tiled=True)
+    arrived = lax.all_to_all(hold(packed, block), "cache", split_axis=0, concat_axis=0, tiled=True)
     new_mine, new_theirs = seq_gather(block)
     rows, bias = prepare(queries[:, 0], query_seg, segments.reshape(8, TOK), new_mine)
 

time: 123 us -> 121 us (0.984); the launches traced: 121 us -> 122 us
  Pallas kernels: 18.3 us -> 21.7 us
  waiting for transfers between devices: 57.2 us -> 54.6 us
    pallas_call x1, Pallas kernels: 5.51 us -> 8.83 us  [attend_pages(): pl.pallas_call(attend_pages_kernel, name='attend_pages', out_shape=bf16(L...]
    ppermute x1, waiting for transfers between devices: 10.7 us -> 8.2 us  [on_device(): other = lax.ppermute(sent, 'head', HEAD)]
  transfers between devices with their start and end apart: 21 -> 21, of which waited for: 15 -> 15; matrix products, arithmetic and copies ran while one was open for 1% -> 1% of each run, Pallas kernels for 5% -> 7%
where the time goes in v3:
time: 121 us; the launch traced here: 122 us
  waiting for transfers between devices  54.6 us (45%)
  starting transfers between devices  37.9 us (31%)
  Pallas kernels  21.7 us (18%)
  local copies, waits for them, and re-layouts  6.49 us (5%)
    ppermute x2, waiting for transfers between devices, seq_gather(): lax.ppermute(block, 'seq', XUP)  16.5 us
    ppermute x3, starting transfers between devices, on_device(): ups.append(lax.ppermute(ups[-1], 'cache', CACHE_UP))  9.47 us
    pallas_call x1, Pallas kernels, attend_pages(): pl.pallas_call(attend_pages_kernel, name='attend_pages', out_shape=bf16(L...  8.83 us
    all_to_all x1, starting transfers between devices, on_device(): lax.all_to_all(hold(packed, block), 'cache', split_axis=0, concat_axis=0,...  8.66 us
    ppermute x1, waiting for transfers between devices, on_device(): other = lax.ppermute(sent, 'head', HEAD)  8.2 us
    ppermute x2, waiting for transfers between devices, seq_gather(): lax.ppermute(block, 'seq', XFAR)  5.56 us
    all_to_all x1, waiting for transfers between devices, on_device(): lax.all_to_all(hold(packed, block), 'cache', split_axis=0, concat_axis=0,...  5.38 us
    ppermute x2, waiting for transfers between devices, seq_gather(): return (mine, lax.ppermute(mine, 'seq', CORE))  5.14 us
  transfers between devices with their start and end apart: 21, of which 15 were waited for; matrix products, arithmetic and copies ran while one was open for 1% of the time, Pallas kernels for 7%

profile of v3, /device:TPU:97, one launch (start us, length us, event | category | flops | bytes accessed | tf_op | source)
XLA Modules:
  0.0 121.6 jit_solution(11678334991984969847)
XLA Ops:
  0.7 1.2 constant_dynamic-slice_fusion
  1.9 1.4 %collective-permute-start.3 = (bf16[256,256]{1,0:T(8,128)(2,1)S(1)}, bf16[256,256]{1,0:T(8,128)(2,1)S(1)}, u32[]{:S(2)}, u32[]{:S(2)}) collective-permute-start(bf16[256,256]{1,0:T(8,128)(2,1)S(1)} %bitcast.14), channel_id=1, source_target_pairs={{0,16},{16,0},{32,48},{48,32},{64,80},{80,64},{96,112},{112,96},{1... | collective-permute-start | bytes 393224 | tf_op jit(solution)/shard_map/ppermute | solution.py:470
  3.2 0.2 constant_dynamic-slice_fusion.1
  3.6 0.8 copy.11
  4.4 1.9 %collective-permute-done.3.near_cols = bf16[256,256]{1,0:T(8,128)(2,1)S(1)} collective-permute-done((bf16[256,256]{1,0:T(8,128)(2,1)S(1)}, bf16[256,256]{1,0:T(8,128)(2,1)S(1)}, u32[]{:S(2)}, u32[]{:S(2)}) %collective-permute-start.3) | collective-permute-done | bytes 131104 | tf_op jit(solution)/shard_map/ppermute | solution.py:470
  6.3 0.7 order.1.refs_0_
  7.0 2.9 %collective-permute-start.4 = (bf16[512,256]{1,0:T(8,128)(2,1)S(1)}, bf16[512,256]{1,0:T(8,128)(2,1)S(1)}, u32[]{:S(2)}, u32[]{:S(2)}) collective-permute-start(bf16[512,256]{1,0:T(8,128)(2,1)S(1)} %order.1.refs_0_), channel_id=1, source_target_pairs={{0,32},{16,48},{32,64},{48,80},{64,96},{80,112},{96,128},{112,144}... | collective-permute-start | bytes 786440 | tf_op jit(solution)/shard_map/ppermute | solution.py:479
  10.0 3.0 %collective-permute-start.1 = (bf16[128,2048]{1,0:T(8,128)(2,1)S(1)}, bf16[128,2048]{1,0:T(8,128)(2,1)S(1)}, u32[]{:S(2)}, u32[]{:S(2)}) collective-permute-start(bf16[128,2048]{1,0:T(8,128)(2,1)S(1)} %stage.1.refs_0_), channel_id=1, source_target_pairs={{0,1},{1,0},{2,3},{3,2},{4,5},{5,4},{6,7},{7,6},{8,9},{9,8},{10,11... | collective-permute-start | bytes 1572872 | tf_op jit(solution)/shard_map/ppermute | solution.py:485
  13.0 1.0 collective-permute-start.2
  14.0 0.3 collective-permute-start
  14.3 3.1 %collective-permute-start.5 = (bf16[512,256]{1,0:T(8,128)(2,1)S(1)}, bf16[512,256]{1,0:T(8,128)(2,1)S(1)}, u32[]{:S(2)}, u32[]{:S(2)}) collective-permute-start(bf16[512,256]{1,0:T(8,128)(2,1)S(1)} %collective-permute-done.4.refs_0_.refs_1_), channel_id=1, source_target_pairs={{0,32},{16,48},{32,64},{48,80},{64,96},{80,112},{96,128},{112,144}... | collective-permute-start | bytes 786440 | tf_op jit(solution)/shard_map/ppermute | solution.py:479
  17.4 3.3 %collective-permute-done.5.refs_3_ = bf16[512,256]{1,0:T(8,128)(2,1)S(1)} collective-permute-done((bf16[512,256]{1,0:T(8,128)(2,1)S(1)}, bf16[512,256]{1,0:T(8,128)(2,1)S(1)}, u32[]{:S(2)}, u32[]{:S(2)}) %collective-permute-start.5) | collective-permute-done | bytes 262176 | tf_op jit(solution)/shard_map/ppermute | solution.py:479
  20.7 3.4 %collective-permute-start.6 = (bf16[512,256]{1,0:T(8,128)(2,1)S(1)}, bf16[512,256]{1,0:T(8,128)(2,1)S(1)}, u32[]{:S(2)}, u32[]{:S(2)}) collective-permute-start(bf16[512,256]{1,0:T(8,128)(2,1)S(1)} %collective-permute-done.5.refs_3_), channel_id=1, source_target_pairs={{0,32},{16,48},{32,64},{48,80},{64,96},{80,112},{96,128},{112,144}... | collective-permute-start | bytes 786440 | tf_op jit(solution)/shard_map/ppermute | solution.py:479
  24.1 2.5 %pack.1.refs_6_.refs_0_ = bf16[32,64,256]{2,1,0:T(8,128)(2,1)} custom-call(s32[16,11]{1,0:T(8,128)S(1)} %bitcast.19, s32[16,11]{1,0:T(8,128)S(1)} %copy-done.6, bf16[8,64,256]{2,1,0:T(8,128)(2,1)S(1)} %reshape.13.pool, bf16[512,256]{1,0:T(8,128)(2,1)S(1)} %collective-permute-done.4.refs_0_.refs_1_), custom_call_target="tpu_custom_call" | custom-call | bytes 2097152 | tf_op jit(solution)/shard_map/pack/pallas_call | solution.py:78
  26.6 8.2 %collective-permute-done.1.refs_2_ = bf16[128,2048]{1,0:T(8,128)(2,1)S(1)} collective-permute-done((bf16[128,2048]{1,0:T(8,128)(2,1)S(1)}, bf16[128,2048]{1,0:T(8,128)(2,1)S(1)}, u32[]{:S(2)}, u32[]{:S(2)}) %collective-permute-start.1) | collective-permute-done | bytes 524320 | tf_op jit(solution)/shard_map/ppermute | solution.py:485
  34.8 0.7 collective-permute-done.refs_1_
  35.6 3.0 %collective-permute-start.10 = (bf16[4,128,2048]{2,1,0:T(8,128)(2,1)S(1)}, bf16[4,128,2048]{2,1,0:T(8,128)(2,1)S(1)}, u32[]{:S(2)}, u32[]{:S(2)}) collective-permute-start(bf16[4,128,2048]{2,1,0:T(8,128)(2,1)S(1)} %relay.3.mine), channel_id=1, source_target_pairs={{0,2},{2,0},{4,6},{6,4},{8,10},{10,8},{12,14},{14,12},{1,3},{3,1},... | collective-permute-start | bytes 6291464 | tf_op jit(solution)/shard_map/ppermute | solution.py:489
  38.7 2.7 %collective-permute-start.11 = (bf16[512,256]{1,0:T(8,128)(2,1)S(1)}, bf16[512,256]{1,0:T(8,128)(2,1)S(1)}, u32[]{:S(2)}, u32[]{:S(2)}) collective-permute-start(bf16[512,256]{1,0:T(8,128)(2,1)S(1)} %collective-permute-done.6.refs_4_.refs_5_), channel_id=1, source_target_pairs={{0,32},{16,48},{32,64},{48,80},{64,96},{80,112},{96,128},{112,144}... | collective-permute-start | bytes 786440 | tf_op jit(solution)/shard_map/ppermute | solution.py:481
  41.4 1.1 collective-permute-done.10.theirs
  42.4 1.7 %project_near.1 = (f32[512,256]{1,0:T(8,128)S(1)}, bf16[512,512]{1,0:T(8,128)(2,1)S(1)}) custom-call(bf16[4,128,2048]{2,1,0:T(8,128)(2,1)S(1)} %relay.3.mine, bf16[4,128,2048]{2,1,0:T(8,128)(2,1)S(1)} %collective-permute-done.10.theirs, bf16[512,256]{1,0:T(8,128)(2,1)S(1)} %order.1.refs_0_, bf16[512,256]{1,0:T(8,128)(2,1)S(1)} %collective-permute-done.4.refs_0_.refs_1_, ...), custom_call_target="tpu_custom_call" | custom-call | flops 939524096 | bytes 6291456 | tf_op jit(solution)/shard_map/project_near/pallas_call | solution.py:132
  44.2 2.8 %collective-permute-done.11.weights = bf16[512,256]{1,0:T(8,128)(2,1)S(1)} collective-permute-done((bf16[512,256]{1,0:T(8,128)(2,1)S(1)}, bf16[512,256]{1,0:T(8,128)(2,1)S(1)}, u32[]{:S(2)}, u32[]{:S(2)}) %collective-permute-start.11) | collective-permute-done | bytes 262176 | tf_op jit(solution)/shard_map/ppermute | solution.py:481
  47.0 0.3 project_far.1.refs_0_.refs_1_
  47.3 8.7 %all-to-all-start = ((bf16[32,64,256]{2,1,0:T(8,128)(2,1)}), bf16[32,64,256]{2,1,0:T(8,128)(2,1)}, u32[]{:S(2)}, u32[]{:S(2)}) async-start(bf16[32,64,256]{2,1,0:T(8,128)(2,1)} %hold.1), calls=%async_computation | async-start | bytes 2097152 | tf_op jit(solution)/shard_map/all_to_all | solution.py:493
  56.0 2.6 %collective-permute-start.12 = (bf16[512,256]{1,0:T(8,128)(2,1)S(1)}, bf16[512,256]{1,0:T(8,128)(2,1)S(1)}, u32[]{:S(2)}, u32[]{:S(2)}) collective-permute-start(bf16[512,256]{1,0:T(8,128)(2,1)S(1)} %project_far.1.refs_0_.refs_1_), channel_id=1, source_target_pairs={{0,12},{2,14},{4,0},{6,2},{8,4},{10,6},{12,8},{14,10},{1,13},{3,15... | collective-permute-start | bytes 786440 | tf_op jit(solution)/shard_map/ppermute | solution.py:454
  58.5 0.5 collective-permute-start.13
  59.1 0.6 collective-permute-start.14
  59.7 3.9 %collective-permute-done.12.refs_1_ = bf16[512,256]{1,0:T(8,128)(2,1)S(1)} collective-permute-done((bf16[512,256]{1,0:T(8,128)(2,1)S(1)}, bf16[512,256]{1,0:T(8,128)(2,1)S(1)}, u32[]{:S(2)}, u32[]{:S(2)}) %collective-permute-start.12) | collective-permute-done | bytes 262176 | tf_op jit(solution)/shard_map/ppermute | solution.py:454
  63.5 2.8 %collective-permute-done.13.refs_2_ = bf16[512,256]{1,0:T(8,128)(2,1)S(1)} collective-permute-done((bf16[512,256]{1,0:T(8,128)(2,1)S(1)}, bf16[512,256]{1,0:T(8,128)(2,1)S(1)}, u32[]{:S(2)}, u32[]{:S(2)}) %collective-permute-start.13) | collective-permute-done | bytes 262176 | tf_op jit(solution)/shard_map/ppermute | solution.py:455
  66.3 7.7 %collective-permute-done.14.refs_3_ = bf16[512,256]{1,0:T(8,128)(2,1)S(1)} collective-permute-done((bf16[512,256]{1,0:T(8,128)(2,1)S(1)}, bf16[512,256]{1,0:T(8,128)(2,1)S(1)}, u32[]{:S(2)}, u32[]{:S(2)}) %collective-permute-start.14) | collective-permute-done | bytes 262176 | tf_op jit(solution)/shard_map/ppermute | solution.py:456
  74.1 0.5 collective-permute-start.15
  74.6 2.3 %collective-permute-done.15.after.far_theirs = bf16[4,512,256]{2,1,0:T(8,128)(2,1)S(1)} collective-permute-done((bf16[4,512,256]{2,1,0:T(8,128)(2,1)S(1)}, bf16[4,512,256]{2,1,0:T(8,128)(2,1)S(1)}, u32[]{:S(2)}, u32[]{:S(2)}) %collective-permute-start.15) | collective-permute-done | bytes 1048608 | tf_op jit(solution)/shard_map/ppermute | solution.py:460
  76.8 1.0 copy-done.2
  77.8 5.4 %all-to-all-done.arrived = bf16[32,64,256]{2,1,0:T(8,128)(2,1)} async-done(((bf16[32,64,256]{2,1,0:T(8,128)(2,1)}), bf16[32,64,256]{2,1,0:T(8,128)(2,1)}, u32[]{:S(2)}, u32[]{:S(2)}) %all-to-all-start) | async-done | bytes 1048608 | tf_op jit(solution)/shard_map/all_to_all | solution.py:493
  83.2 1.2 %copy-done.3 = bf16[4,512,256]{2,1,0:T(8,128)(2,1)S(1)} copy-done((bf16[4,512,256]{2,1,0:T(8,128)(2,1)S(1)}, bf16[4,512,256]{2,1,0:T(8,128)(2,1)}, u32[]{:S(2)}) %copy-start.3) | copy-done | bytes 1048600
  84.4 1.3 %unpack.1.after.refs_0_ = bf16[704,256]{1,0:T(8,128)(2,1)S(1)} custom-call(s32[16,11]{1,0:T(8,128)S(1)} %bitcast.20, bf16[32,64,256]{2,1,0:T(8,128)(2,1)} %all-to-all-done.arrived, bf16[4,512,256]{2,1,0:T(8,128)(2,1)S(1)} %copy-done.3), custom_call_target="tpu_custom_call" | custom-call | bytes 1048576 | tf_op jit(solution)/shard_map/unpack/pallas_call | solution.py:100
  85.8 2.6 %collective-permute-start.16 = (bf16[704,256]{1,0:T(8,128)(2,1)S(1)}, bf16[704,256]{1,0:T(8,128)(2,1)}, u32[]{:S(2)}, u32[]{:S(2)}) collective-permute-start(bf16[704,256]{1,0:T(8,128)(2,1)S(1)} %unpack.1.after.refs_0_), channel_id=1, source_target_pairs={{0,12},{2,14},{4,0},{6,2},{8,4},{10,6},{12,8},{14,10},{1,13},{3,15... | collective-permute-start | bytes 1081352 | tf_op jit(solution)/shard_map/ppermute | solution.py:454
  88.3 0.5 collective-permute-start.17
  88.8 0.6 collective-permute-start.18
  89.5 1.2 %copy-done.1 = bf16[2,1,128,2048]{3,2,1,0:T(8,128)(2,1)S(1)} copy-done((bf16[2,1,128,2048]{3,2,1,0:T(8,128)(2,1)S(1)}, bf16[2,1,128,2048]{3,2,1,0:T(8,128)(2,1)}, u32[]{:S(2)}) %copy-start.1) | copy-done | bytes 1048600
  90.7 0.5 prepare.1
  91.2 0.7 copy-done.4
  91.9 4.4 %attend_new.1 = (bf16[128,2,512]{2,1,0:T(2,128)(2,1)}, f32[4,8,1024]{2,1,0:T(8,128)S(1)}, f32[4,8,1024]{2,1,0:T(8,128)S(1)}, f32[4,128,1024]{2,1,0:T(8,128)S(1)}) custom-call(s32[1024]{0:T(1024)S(1)} %bitcast.22, bf16[4,128,1024]{2,1,0:T(8,128)(2,1)S(1)} %get-tuple-element.12.rows, f32[4,256,128]{2,1,0:T(8,128)S(1)} %get-tuple-element.13.bias, ...), custom_call_target="tpu_custom_call" | custom-call | flops 2000000000 | bytes 6291456 | tf_op jit(solution)/shard_map/attend_new/pallas_call | solution.py:368
  96.4 2.7 %collective-permute-done.17.refs_2_ = bf16[704,256]{1,0:T(8,128)(2,1)} collective-permute-done((bf16[704,256]{1,0:T(8,128)(2,1)S(1)}, bf16[704,256]{1,0:T(8,128)(2,1)}, u32[]{:S(2)}, u32[]{:S(2)}) %collective-permute-start.17) | collective-permute-done | bytes 360480 | tf_op jit(solution)/shard_map/ppermute | solution.py:455
  99.1 8.9 %collective-permute-done.18.refs_3_ = bf16[704,256]{1,0:T(8,128)(2,1)} collective-permute-done((bf16[704,256]{1,0:T(8,128)(2,1)S(1)}, bf16[704,256]{1,0:T(8,128)(2,1)}, u32[]{:S(2)}, u32[]{:S(2)}) %collective-permute-start.18) | collective-permute-done | bytes 360480 | tf_op jit(solution)/shard_map/ppermute | solution.py:456
  108.0 1.3 %relay.5.mine = bf16[4,704,256]{2,1,0:T(8,128)(2,1)S(1)} custom-call(bf16[704,256]{1,0:T(8,128)(2,1)S(1)} %unpack.1.after.refs_0_, bf16[704,256]{1,0:T(8,128)(2,1)} %collective-permute-done.16.refs_1_, bf16[704,256]{1,0:T(8,128)(2,1)} %collective-permute-done.17.refs_2_, bf16[704,256]{1,0:T(8,128)(2,1)} %collective-permute-done.18.refs_3_, ...), custom_call_target="tpu_custom_call" | custom-call | bytes 2097152 | tf_op jit(solution)/shard_map/relay/pallas_call | solution.py:251
  109.3 0.6 collective-permute-start.19
  109.9 2.8 %collective-permute-done.19.theirs = bf16[4,704,256]{2,1,0:T(8,128)(2,1)S(1)} collective-permute-done((bf16[4,704,256]{2,1,0:T(8,128)(2,1)S(1)}, bf16[4,704,256]{2,1,0:T(8,128)(2,1)S(1)}, u32[]{:S(2)}, u32[]{:S(2)}) %collective-permute-start.19) | collective-permute-done | bytes 1441824 | tf_op jit(solution)/shard_map/ppermute | solution.py:460
  112.7 8.8 %attend_pages.1 = bf16[2,128,2048]{2,1,0:T(8,128)(2,1)} custom-call(s32[16,11]{1,0:T(8,128)S(1)} %copy-done.8, s32[1024]{0:T(1024)S(1)} %bitcast.23, s32[1,128]{1,0:T(1,128)S(1)} %constant_dynamic-slice_fusion.2.query_seg, bf16[4,128,1024]{2,1,0:T(8,128)(2,1)S(1)} %get-tuple-element.12.rows, f32[4,8,1024]{2,1,0:T(8,128)S(1)} %get-tuple-element.14.refs_4_.peak_in, ...), custom_call_target="tpu_custom_call" | custom-call | flops 3000000000 | bytes 6291456 | tf_op jit(solution)/shard_map/attend_pages/pallas_call | solution.py:433
  (31 shorter events, 0.6 us)
Async XLA Ops:
  0.6 2.6 %copy-start = (bf16[8,128,2,512]{3,2,1,0:T(2,128)(2,1)S(1)}, bf16[8,128,2,512]{3,2,1,0:T(2,128)(2,1)}, u32[]{:S(2)}) copy-start(bf16[8,128,2,512]{3,2,1,0:T(2,128)(2,1)} %param.11) | copy-start | bytes 6291460
  0.6 9.3 %copy-start.5 = (bf16[1,128,2048]{2,1,0:T(8,128)(2,1)S(1)}, bf16[1,128,2048]{2,1,0:T(8,128)(2,1)}, u32[]{:S(2)}) copy-start(bf16[1,128,2048]{2,1,0:T(8,128)(2,1)} %param.8) | copy-start | bytes 1572868
  0.7 23.5 %copy-start.6 = (s32[16,11]{1,0:T(8,128)S(1)}, s32[16,11]{1,0:T(8,128)}, u32[]{:S(2)}) copy-start(s32[16,11]{1,0:T(8,128)} %pages.1) | copy-start | bytes 2116
  1.9 4.5 %collective-permute-start.3 = (bf16[256,256]{1,0:T(8,128)(2,1)S(1)}, bf16[256,256]{1,0:T(8,128)(2,1)S(1)}, u32[]{:S(2)}, u32[]{:S(2)}) collective-permute-start(bf16[256,256]{1,0:T(8,128)(2,1)S(1)} %bitcast.14), channel_id=1, source_target_pairs={{0,16},{16,0},{32,48},{48,32},{64,80},{80,64},{96,112},{112,96},{1... | collective-permute-start | bytes 393224 | tf_op jit(solution)/shard_map/ppermute | solution.py:470
  7.0 7.3 %collective-permute-start.4 = (bf16[512,256]{1,0:T(8,128)(2,1)S(1)}, bf16[512,256]{1,0:T(8,128)(2,1)S(1)}, u32[]{:S(2)}, u32[]{:S(2)}) collective-permute-start(bf16[512,256]{1,0:T(8,128)(2,1)S(1)} %order.1.refs_0_), channel_id=1, source_target_pairs={{0,32},{16,48},{32,64},{48,80},{64,96},{80,112},{96,128},{112,144}... | collective-permute-start | bytes 786440 | tf_op jit(solution)/shard_map/ppermute | solution.py:479
  9.9 7.5 %collective-permute-start.7 = (bf16[512,256]{1,0:T(8,128)(2,1)S(1)}, bf16[512,256]{1,0:T(8,128)(2,1)S(1)}, u32[]{:S(2)}, u32[]{:S(2)}) collective-permute-start(bf16[512,256]{1,0:T(8,128)(2,1)S(1)} %order.1.refs_0_), channel_id=1, source_target_pairs={{0,224},{16,240},{32,0},{48,16},{64,32},{80,48},{96,64},{112,80},{... | collective-permute-start | bytes 786440 | tf_op jit(solution)/shard_map/ppermute | solution.py:480
  10.0 24.8 %collective-permute-start.1 = (bf16[128,2048]{1,0:T(8,128)(2,1)S(1)}, bf16[128,2048]{1,0:T(8,128)(2,1)S(1)}, u32[]{:S(2)}, u32[]{:S(2)}) collective-permute-start(bf16[128,2048]{1,0:T(8,128)(2,1)S(1)} %stage.1.refs_0_), channel_id=1, source_target_pairs={{0,1},{1,0},{2,3},{3,2},{4,5},{5,4},{6,7},{7,6},{8,9},{9,8},{10,11... | collective-permute-start | bytes 1572872 | tf_op jit(solution)/shard_map/ppermute | solution.py:485
  13.0 21.8 %collective-permute-start.2 = (bf16[128,2048]{1,0:T(8,128)(2,1)S(1)}, bf16[128,2048]{1,0:T(8,128)(2,1)S(1)}, u32[]{:S(2)}, u32[]{:S(2)}) collective-permute-start(bf16[128,2048]{1,0:T(8,128)(2,1)S(1)} %stage.1.refs_0_), channel_id=1, source_target_pairs={{0,5},{1,4},{2,7},{3,6},{4,1},{5,0},{6,3},{7,2},{8,13},{9,12},{10,... | collective-permute-start | bytes 1572872 | tf_op jit(solution)/shard_map/ppermute | solution.py:486
  14.0 21.5 %collective-permute-start = (bf16[128,2048]{1,0:T(8,128)(2,1)S(1)}, bf16[128,2048]{1,0:T(8,128)(2,1)S(1)}, u32[]{:S(2)}, u32[]{:S(2)}) collective-permute-start(bf16[128,2048]{1,0:T(8,128)(2,1)S(1)} %bitcast.17), channel_id=1, source_target_pairs={{0,4},{2,6},{4,0},{6,2},{8,12},{10,14},{12,8},{14,10},{1,5},{3,7},... | collective-permute-start | bytes 1572872 | tf_op jit(solution)/shard_map/ppermute | solution.py:484
  14.3 6.4 %collective-permute-start.5 = (bf16[512,256]{1,0:T(8,128)(2,1)S(1)}, bf16[512,256]{1,0:T(8,128)(2,1)S(1)}, u32[]{:S(2)}, u32[]{:S(2)}) collective-permute-start(bf16[512,256]{1,0:T(8,128)(2,1)S(1)} %collective-permute-done.4.refs_0_.refs_1_), channel_id=1, source_target_pairs={{0,32},{16,48},{32,64},{48,80},{64,96},{80,112},{96,128},{112,144}... | collective-permute-start | bytes 786440 | tf_op jit(solution)/shard_map/ppermute | solution.py:479
  17.4 6.7 %collective-permute-start.8 = (bf16[512,256]{1,0:T(8,128)(2,1)S(1)}, bf16[512,256]{1,0:T(8,128)(2,1)S(1)}, u32[]{:S(2)}, u32[]{:S(2)}) collective-permute-start(bf16[512,256]{1,0:T(8,128)(2,1)S(1)} %collective-permute-done.7.refs_2_), channel_id=1, source_target_pairs={{0,224},{16,240},{32,0},{48,16},{64,32},{80,48},{96,64},{112,80},{... | collective-permute-start | bytes 786440 | tf_op jit(solution)/shard_map/ppermute | solution.py:480
  20.7 14.8 %collective-permute-start.6 = (bf16[512,256]{1,0:T(8,128)(2,1)S(1)}, bf16[512,256]{1,0:T(8,128)(2,1)S(1)}, u32[]{:S(2)}, u32[]{:S(2)}) collective-permute-start(bf16[512,256]{1,0:T(8,128)(2,1)S(1)} %collective-permute-done.5.refs_3_), channel_id=1, source_target_pairs={{0,32},{16,48},{32,64},{48,80},{64,96},{80,112},{96,128},{112,144}... | collective-permute-start | bytes 786440 | tf_op jit(solution)/shard_map/ppermute | solution.py:479
  24.1 11.4 %collective-permute-start.9 = (bf16[512,256]{1,0:T(8,128)(2,1)S(1)}, bf16[512,256]{1,0:T(8,128)(2,1)S(1)}, u32[]{:S(2)}, u32[]{:S(2)}) collective-permute-start(bf16[512,256]{1,0:T(8,128)(2,1)S(1)} %collective-permute-done.8.refs_4_), channel_id=1, source_target_pairs={{0,224},{16,240},{32,0},{48,16},{64,32},{80,48},{96,64},{112,80},{... | collective-permute-start | bytes 786440 | tf_op jit(solution)/shard_map/ppermute | solution.py:480
  35.6 6.8 %collective-permute-start.10 = (bf16[4,128,2048]{2,1,0:T(8,128)(2,1)S(1)}, bf16[4,128,2048]{2,1,0:T(8,128)(2,1)S(1)}, u32[]{:S(2)}, u32[]{:S(2)}) collective-permute-start(bf16[4,128,2048]{2,1,0:T(8,128)(2,1)S(1)} %relay.3.mine), channel_id=1, source_target_pairs={{0,2},{2,0},{4,6},{6,4},{8,10},{10,8},{12,14},{14,12},{1,3},{3,1},... | collective-permute-start | bytes 6291464 | tf_op jit(solution)/shard_map/ppermute | solution.py:489
  38.7 8.3 %collective-permute-start.11 = (bf16[512,256]{1,0:T(8,128)(2,1)S(1)}, bf16[512,256]{1,0:T(8,128)(2,1)S(1)}, u32[]{:S(2)}, u32[]{:S(2)}) collective-permute-start(bf16[512,256]{1,0:T(8,128)(2,1)S(1)} %collective-permute-done.6.refs_4_.refs_5_), channel_id=1, source_target_pairs={{0,32},{16,48},{32,64},{48,80},{64,96},{80,112},{96,128},{112,144}... | collective-permute-start | bytes 786440 | tf_op jit(solution)/shard_map/ppermute | solution.py:481
  47.3 35.9 %all-to-all-start = ((bf16[32,64,256]{2,1,0:T(8,128)(2,1)}), bf16[32,64,256]{2,1,0:T(8,128)(2,1)}, u32[]{:S(2)}, u32[]{:S(2)}) async-start(bf16[32,64,256]{2,1,0:T(8,128)(2,1)} %hold.1), calls=%async_computation | async-start | bytes 2097152 | tf_op jit(solution)/shard_map/all_to_all | solution.py:493
  56.0 33.5 %copy-start.7 = (s32[1,1024]{1,0:T(1,128)S(1)}, s32[1,1024]{1,0:T(1,128)}, u32[]{:S(2)}) copy-start(s32[1,1024]{1,0:T(1,128)} %param.15) | copy-start | bytes 12292
  56.0 7.5 %collective-permute-start.12 = (bf16[512,256]{1,0:T(8,128)(2,1)S(1)}, bf16[512,256]{1,0:T(8,128)(2,1)S(1)}, u32[]{:S(2)}, u32[]{:S(2)}) collective-permute-start(bf16[512,256]{1,0:T(8,128)(2,1)S(1)} %project_far.1.refs_0_.refs_1_), channel_id=1, source_target_pairs={{0,12},{2,14},{4,0},{6,2},{8,4},{10,6},{12,8},{14,10},{1,13},{3,15... | collective-permute-start | bytes 786440 | tf_op jit(solution)/shard_map/ppermute | solution.py:454
  58.5 7.8 %collective-permute-start.13 = (bf16[512,256]{1,0:T(8,128)(2,1)S(1)}, bf16[512,256]{1,0:T(8,128)(2,1)S(1)}, u32[]{:S(2)}, u32[]{:S(2)}) collective-permute-start(bf16[512,256]{1,0:T(8,128)(2,1)S(1)} %project_far.1.refs_0_.refs_1_), channel_id=1, source_target_pairs={{0,8},{2,10},{4,12},{6,14},{8,0},{10,2},{12,4},{14,6},{1,9},{3,11}... | collective-permute-start | bytes 786440 | tf_op jit(solution)/shard_map/ppermute | solution.py:455
  59.1 14.9 %collective-permute-start.14 = (bf16[512,256]{1,0:T(8,128)(2,1)S(1)}, bf16[512,256]{1,0:T(8,128)(2,1)S(1)}, u32[]{:S(2)}, u32[]{:S(2)}) collective-permute-start(bf16[512,256]{1,0:T(8,128)(2,1)S(1)} %project_far.1.refs_0_.refs_1_), channel_id=1, source_target_pairs={{0,4},{2,6},{4,8},{6,10},{8,12},{10,14},{12,0},{14,2},{1,5},{3,7},... | collective-permute-start | bytes 786440 | tf_op jit(solution)/shard_map/ppermute | solution.py:456
  74.1 2.8 %collective-permute-start.15 = (bf16[4,512,256]{2,1,0:T(8,128)(2,1)S(1)}, bf16[4,512,256]{2,1,0:T(8,128)(2,1)S(1)}, u32[]{:S(2)}, u32[]{:S(2)}) collective-permute-start(bf16[4,512,256]{2,1,0:T(8,128)(2,1)S(1)} %relay.4.after.mine), channel_id=1, source_target_pairs={{0,2},{2,0},{4,6},{6,4},{8,10},{10,8},{12,14},{14,12},{1,3},{3,1},... | collective-permute-start | bytes 3145736 | tf_op jit(solution)/shard_map/ppermute | solution.py:460
  76.8 1.0 copy-start.2
  83.2 1.2 %copy-start.3 = (bf16[4,512,256]{2,1,0:T(8,128)(2,1)S(1)}, bf16[4,512,256]{2,1,0:T(8,128)(2,1)}, u32[]{:S(2)}) copy-start(bf16[4,512,256]{2,1,0:T(8,128)(2,1)} %copy-done.2) | copy-start | bytes 3145732
  85.8 10.6 %collective-permute-start.16 = (bf16[704,256]{1,0:T(8,128)(2,1)S(1)}, bf16[704,256]{1,0:T(8,128)(2,1)}, u32[]{:S(2)}, u32[]{:S(2)}) collective-permute-start(bf16[704,256]{1,0:T(8,128)(2,1)S(1)} %unpack.1.after.refs_0_), channel_id=1, source_target_pairs={{0,12},{2,14},{4,0},{6,2},{8,4},{10,6},{12,8},{14,10},{1,13},{3,15... | collective-permute-start | bytes 1081352 | tf_op jit(solution)/shard_map/ppermute | solution.py:454
  88.3 10.8 %collective-permute-start.17 = (bf16[704,256]{1,0:T(8,128)(2,1)S(1)}, bf16[704,256]{1,0:T(8,128)(2,1)}, u32[]{:S(2)}, u32[]{:S(2)}) collective-permute-start(bf16[704,256]{1,0:T(8,128)(2,1)S(1)} %unpack.1.after.refs_0_), channel_id=1, source_target_pairs={{0,8},{2,10},{4,12},{6,14},{8,0},{10,2},{12,4},{14,6},{1,9},{3,11}... | collective-permute-start | bytes 1081352 | tf_op jit(solution)/shard_map/ppermute | solution.py:455
  88.8 19.1 %collective-permute-start.18 = (bf16[704,256]{1,0:T(8,128)(2,1)S(1)}, bf16[704,256]{1,0:T(8,128)(2,1)}, u32[]{:S(2)}, u32[]{:S(2)}) collective-permute-start(bf16[704,256]{1,0:T(8,128)(2,1)S(1)} %unpack.1.after.refs_0_), channel_id=1, source_target_pairs={{0,4},{2,6},{4,8},{6,10},{8,12},{10,14},{12,0},{14,2},{1,5},{3,7},... | collective-permute-start | bytes 1081352 | tf_op jit(solution)/shard_map/ppermute | solution.py:456
  89.5 1.2 %copy-start.1 = (bf16[2,1,128,2048]{3,2,1,0:T(8,128)(2,1)S(1)}, bf16[2,1,128,2048]{3,2,1,0:T(8,128)(2,1)}, u32[]{:S(2)}) copy-start(bf16[2,1,128,2048]{3,2,1,0:T(8,128)(2,1)} %param.10) | copy-start | bytes 3145732
  90.7 1.2 %copy-start.4 = (bf16[4,512,256]{2,1,0:T(8,128)(2,1)S(1)}, bf16[4,512,256]{2,1,0:T(8,128)(2,1)}, u32[]{:S(2)}) copy-start(bf16[4,512,256]{2,1,0:T(8,128)(2,1)} %copy-done.2) | copy-start | bytes 3145732
  96.3 16.4 %copy-start.8 = (s32[16,11]{1,0:T(8,128)S(1)}, s32[16,11]{1,0:T(8,128)}, u32[]{:S(2)}) copy-start(s32[16,11]{1,0:T(8,128)} %requests.1) | copy-start | bytes 2116
  109.3 3.4 %collective-permute-start.19 = (bf16[4,704,256]{2,1,0:T(8,128)(2,1)S(1)}, bf16[4,704,256]{2,1,0:T(8,128)(2,1)S(1)}, u32[]{:S(2)}, u32[]{:S(2)}) collective-permute-start(bf16[4,704,256]{2,1,0:T(8,128)(2,1)S(1)} %relay.5.mine), channel_id=1, source_target_pairs={{0,2},{2,0},{4,6},{6,4},{8,10},{10,8},{12,14},{14,12},{1,3},{3,1},... | collective-permute-start | bytes 4325384 | tf_op jit(solution)/shard_map/ppermute | solution.py:460

commit v4 on v3

--- a/solution.py
+++ b/solution.py
@@ -144,22 +144,24 @@
     )(mine, theirs, *weights)
 
 
-def project_far_kernel(partial, far_hidden, weights, out):
+def project_far_kernel(partial, far_hidden, weights_a, weights_b, out):
     out[...] = (
-        partial[...] + jnp.dot(far_hidden[...], weights[...], preferred_element_type=jnp.float32)
+        partial[...]
+        + jnp.dot(far_hidden[:, :256], weights_a[...], preferred_element_type=jnp.float32)
+        + jnp.dot(far_hidden[:, 256:], weights_b[...], preferred_element_type=jnp.float32)
     ).astype(out.dtype)
 
 
-def project_far(partial, far_hidden, weights):
+def project_far(partial, far_hidden, weights_a, weights_b):
     return pl.pallas_call(
         project_far_kernel,
         name="project_far",
         out_shape=bf16(4 * TOK, 2 * HD),
-        in_specs=[VMEM] * 3,
+        in_specs=[VMEM] * 4,
         out_specs=VMEM,
         compiler_params=params(),
         cost_estimate=cost(2 * 512 * 512 * 256, 2**20),
-    )(partial, far_hidden, weights)
+    )(partial, far_hidden, weights_a, weights_b)
 
 
 def absorb(places, pieces, rows, limits, bias, state):
@@ -247,16 +249,16 @@
         out[i] = refs[i][...]
 
 
-def relay(blocks, after, late=()):
+def relay(blocks, after):
     return pl.pallas_call(
         relay_kernel,
         name="relay",
         out_shape=bf16(4, *blocks[0].shape),
-        in_specs=[VMEM] * 4 + [VMEM] * len(after) + [ANY] * len(late),
+        in_specs=[VMEM] * (4 + len(after)),
         out_specs=VMEM,
         compiler_params=params(),
         cost_estimate=cost(0, 2**21),
-    )(*blocks, *after, *late)
+    )(*blocks, *after)
 
 
 def stage_kernel(hidden, pool, sent):
@@ -320,6 +322,25 @@
         compiler_params=params(),
         cost_estimate=cost(0, 3 * 2**20),
     )(queries, query_seg, key_seg, after)
+
+
+def bundle_kernel(sent, across, other, diagonal, up, down, packed, out, half_up, half_down):
+    for i, block in enumerate((sent, across, other, diagonal)):
+        out[i] = block[...]
+    half_up[...] = up[:256]
+    half_down[...] = down[256:]
+
+
+def bundle(blocks, up, down, packed):
+    return pl.pallas_call(
+        bundle_kernel,
+        name="bundle",
+        out_shape=(bf16(4, *blocks[0].shape), bf16(256, 2 * HD), bf16(256, 2 * HD)),
+        in_specs=[VMEM] * 6 + [ANY],
+        out_specs=(VMEM,) * 3,
+        compiler_params=params(),
+        cost_estimate=cost(0, 2**21),
+    )(*blocks, up, down, packed)
 
 
 def ring_place():
@@ -478,18 +499,19 @@
     for step in range(3):
         ups.append(lax.ppermute(ups[-1], "cache", CACHE_UP))
         downs.append(lax.ppermute(downs[-1], "cache", CACHE_DOWN))
-    far = lax.ppermute(ups[3], "cache", CACHE_UP)
     weights = [both, ups[1], downs[1], ups[2], downs[2], ups[3], downs[3]]
 
     across = lax.ppermute(hidden[0], "seq", XPAIR)
     other = lax.ppermute(sent, "head", HEAD)
     diagonal = lax.ppermute(sent, ("seq", "head"), DIAGONAL)
     packed = pack(hosts, hit_page, pool, ups[1])
-    hidden_mine = relay([sent, across, other, diagonal], (ups[3], downs[3]), (packed,))
+    hidden_mine, half_up, half_down = bundle([sent, across, other, diagonal], ups[3], downs[3], packed)
+    far_a = lax.ppermute(half_up, "cache", CACHE_UP)
+    far_b = lax.ppermute(half_down, "cache", CACHE_DOWN)
     hidden_theirs = lax.ppermute(hidden_mine, "seq", CORE)
 
     partial, far_hidden = project_near(hidden_mine, hidden_theirs, weights)
-    block = project_far(partial, far_hidden, far)
+    block = project_far(partial, far_hidden, far_a, far_b)
     arrived = lax.all_to_all(hold(packed, block), "cache", split_axis=0, concat_axis=0, tiled=True)
     new_mine, new_theirs = seq_gather(block)
     rows, bias = prepare(queries[:, 0], query_seg, segments.reshape(8, TOK), new_mine)

time: 121 us -> 116 us (0.959)
  the two profiles are of different devices: /device:TPU:97 before, /device:TPU:1 now
where the time goes in v4:
time: 116 us; the launch traced here: 117 us
  starting transfers between devices  45 us (39%)
  waiting for transfers between devices  40.9 us (35%)
  Pallas kernels  23.4 us (20%)
  local copies, waits for them, and re-layouts  6.49 us (6%)
    ppermute x3, starting transfers between devices, on_device(): downs.append(lax.ppermute(downs[-1], 'cache', CACHE_DOWN))  12.9 us
    ppermute x1, waiting for transfers between devices, on_device(): other = lax.ppermute(sent, 'head', HEAD)  11 us
    pallas_call x1, Pallas kernels, attend_pages(): pl.pallas_call(attend_pages_kernel, name='attend_pages', out_shape=bf16(L...  10.5 us
    ppermute x2, waiting for transfers between devices, seq_gather(): lax.ppermute(block, 'seq', XFAR)  9.94 us
    ppermute x2, starting transfers between devices, seq_gather(): return (mine, lax.ppermute(mine, 'seq', CORE))  7.16 us
    ppermute x2, waiting for transfers between devices, seq_gather(): return (mine, lax.ppermute(mine, 'seq', CORE))  5.14 us
    all_to_all x1, starting transfers between devices, on_device(): lax.all_to_all(hold(packed, block), 'cache', split_axis=0, concat_axis=0,...  4.99 us
    unnamed x20, local copies, waits for them, and re-layouts  4.99 us
  transfers between devices with their start and end apart: 22, of which 12 were waited for; matrix products, arithmetic and copies ran while one was open for 1% of the time, Pallas kernels for 8%

profile of v4, /device:TPU:1, one launch (start us, length us, event | category | flops | bytes accessed | tf_op | source)
XLA Modules:
  0.0 116.7 jit_solution(16420165324600741021)
XLA Ops:
  0.7 1.2 constant_dynamic-slice_fusion
  1.9 2.2 %collective-permute-start.3 = (bf16[256,256]{1,0:T(8,128)(2,1)S(1)}, bf16[256,256]{1,0:T(8,128)(2,1)S(1)}, u32[]{:S(2)}, u32[]{:S(2)}) collective-permute-start(bf16[256,256]{1,0:T(8,128)(2,1)S(1)} %bitcast.14), channel_id=1, source_target_pairs={{0,16},{16,0},{32,48},{48,32},{64,80},{80,64},{96,112},{112,96},{1... | collective-permute-start | bytes 393224 | tf_op jit(solution)/shard_map/ppermute | solution.py:491
  4.1 0.8 copy.11
  4.8 0.2 constant_dynamic-slice_fusion.1
  5.0 0.2 reshape.13.pool
  5.2 1.2 %collective-permute-done.3.near_cols = bf16[256,256]{1,0:T(8,128)(2,1)S(1)} collective-permute-done((bf16[256,256]{1,0:T(8,128)(2,1)S(1)}, bf16[256,256]{1,0:T(8,128)(2,1)S(1)}, u32[]{:S(2)}, u32[]{:S(2)}) %collective-permute-start.3) | collective-permute-done | bytes 131104 | tf_op jit(solution)/shard_map/ppermute | solution.py:491
  6.4 0.7 order.1.refs_0_
  7.1 6.4 %collective-permute-start.7 = (bf16[512,256]{1,0:T(8,128)(2,1)S(1)}, bf16[512,256]{1,0:T(8,128)(2,1)S(1)}, u32[]{:S(2)}, u32[]{:S(2)}) collective-permute-start(bf16[512,256]{1,0:T(8,128)(2,1)S(1)} %order.1.refs_0_), channel_id=1, source_target_pairs={{0,224},{16,240},{32,0},{48,16},{64,32},{80,48},{96,64},{112,80},{... | collective-permute-start | bytes 786440 | tf_op jit(solution)/shard_map/ppermute | solution.py:501
  13.5 3.9 %collective-permute-start.2 = (bf16[128,2048]{1,0:T(8,128)(2,1)S(1)}, bf16[128,2048]{1,0:T(8,128)(2,1)S(1)}, u32[]{:S(2)}, u32[]{:S(2)}) collective-permute-start(bf16[128,2048]{1,0:T(8,128)(2,1)S(1)} %stage.1.sent), channel_id=1, source_target_pairs={{0,5},{1,4},{2,7},{3,6},{4,1},{5,0},{6,3},{7,2},{8,13},{9,12},{10,... | collective-permute-start | bytes 1572872 | tf_op jit(solution)/shard_map/ppermute | solution.py:506
  17.5 0.3 collective-permute-start
  17.9 3.1 %collective-permute-start.8 = (bf16[512,256]{1,0:T(8,128)(2,1)S(1)}, bf16[512,256]{1,0:T(8,128)(2,1)S(1)}, u32[]{:S(2)}, u32[]{:S(2)}) collective-permute-start(bf16[512,256]{1,0:T(8,128)(2,1)S(1)} %collective-permute-done.7.refs_2_), channel_id=1, source_target_pairs={{0,224},{16,240},{32,0},{48,16},{64,32},{80,48},{96,64},{112,80},{... | collective-permute-start | bytes 786440 | tf_op jit(solution)/shard_map/ppermute | solution.py:501
  21.0 3.3 %collective-permute-done.8.refs_4_ = bf16[512,256]{1,0:T(8,128)(2,1)S(1)} collective-permute-done((bf16[512,256]{1,0:T(8,128)(2,1)S(1)}, bf16[512,256]{1,0:T(8,128)(2,1)S(1)}, u32[]{:S(2)}, u32[]{:S(2)}) %collective-permute-start.8) | collective-permute-done | bytes 262176 | tf_op jit(solution)/shard_map/ppermute | solution.py:501
  24.3 3.4 %collective-permute-start.9 = (bf16[512,256]{1,0:T(8,128)(2,1)S(1)}, bf16[512,256]{1,0:T(8,128)(2,1)S(1)}, u32[]{:S(2)}, u32[]{:S(2)}) collective-permute-start(bf16[512,256]{1,0:T(8,128)(2,1)S(1)} %collective-permute-done.8.refs_4_), channel_id=1, source_target_pairs={{0,224},{16,240},{32,0},{48,16},{64,32},{80,48},{96,64},{112,80},{... | collective-permute-start | bytes 786440 | tf_op jit(solution)/shard_map/ppermute | solution.py:501
  27.7 2.5 %pack.1.packed.refs_0_ = bf16[32,64,256]{2,1,0:T(8,128)(2,1)} custom-call(s32[16,11]{1,0:T(8,128)S(1)} %bitcast.19, s32[16,11]{1,0:T(8,128)S(1)} %copy-done.6, bf16[8,64,256]{2,1,0:T(8,128)(2,1)S(1)} %reshape.13.pool, bf16[512,256]{1,0:T(8,128)(2,1)S(1)} %collective-permute-done.4.refs_0_.refs_1_), custom_call_target="tpu_custom_call" | custom-call | bytes 2097152 | tf_op jit(solution)/shard_map/pack/pallas_call | solution.py:78
  30.2 11.0 %collective-permute-done.1.other = bf16[128,2048]{1,0:T(8,128)(2,1)S(1)} collective-permute-done((bf16[128,2048]{1,0:T(8,128)(2,1)S(1)}, bf16[128,2048]{1,0:T(8,128)(2,1)S(1)}, u32[]{:S(2)}, u32[]{:S(2)}) %collective-permute-start.1) | collective-permute-done | bytes 524320 | tf_op jit(solution)/shard_map/ppermute | solution.py:505
  41.1 0.2 bundle.1
  41.3 0.8 collective-permute-start.10
  42.1 2.7 %collective-permute-start.12 = (bf16[256,256]{1,0:T(8,128)(2,1)S(1)}, bf16[256,256]{1,0:T(8,128)(2,1)S(1)}, u32[]{:S(2)}, u32[]{:S(2)}) collective-permute-start(bf16[256,256]{1,0:T(8,128)(2,1)S(1)} %get-tuple-element.17), channel_id=1, source_target_pairs={{0,224},{16,240},{32,0},{48,16},{64,32},{80,48},{96,64},{112,80},{... | collective-permute-start | bytes 393224 | tf_op jit(solution)/shard_map/ppermute | solution.py:510
  44.8 1.1 collective-permute-done.10.theirs
  45.9 1.7 %project_near.1 = (f32[512,256]{1,0:T(8,128)S(1)}, bf16[512,512]{1,0:T(8,128)(2,1)S(1)}) custom-call(bf16[4,128,2048]{2,1,0:T(8,128)(2,1)S(1)} %get-tuple-element.13.mine, bf16[4,128,2048]{2,1,0:T(8,128)(2,1)S(1)} %collective-permute-done.10.theirs, bf16[512,256]{1,0:T(8,128)(2,1)S(1)} %order.1.refs_0_, ...), custom_call_target="tpu_custom_call" | custom-call | flops 939524096 | bytes 6291456 | tf_op jit(solution)/shard_map/project_near/pallas_call | solution.py:132
  47.6 0.8 collective-permute-done.11.weights_a
  48.4 0.3 project_far.1.refs_0_.refs_1_
  48.7 5.0 %all-to-all-start = ((bf16[32,64,256]{2,1,0:T(8,128)(2,1)}), bf16[32,64,256]{2,1,0:T(8,128)(2,1)}, u32[]{:S(2)}, u32[]{:S(2)}) async-start(bf16[32,64,256]{2,1,0:T(8,128)(2,1)} %hold.1), calls=%async_computation | async-start | bytes 2097152 | tf_op jit(solution)/shard_map/all_to_all | solution.py:515
  53.7 1.5 %collective-permute-start.15 = (bf16[512,256]{1,0:T(8,128)(2,1)S(1)}, bf16[512,256]{1,0:T(8,128)(2,1)S(1)}, u32[]{:S(2)}, u32[]{:S(2)}) collective-permute-start(bf16[512,256]{1,0:T(8,128)(2,1)S(1)} %project_far.1.refs_0_.refs_1_), channel_id=1, source_target_pairs={{0,4},{2,6},{4,8},{6,10},{8,12},{10,14},{12,0},{14,2},{1,5},{3,7},... | collective-permute-start | bytes 786440 | tf_op jit(solution)/shard_map/ppermute | solution.py:477
  55.2 2.5 %collective-permute-start.14 = (bf16[512,256]{1,0:T(8,128)(2,1)S(1)}, bf16[512,256]{1,0:T(8,128)(2,1)S(1)}, u32[]{:S(2)}, u32[]{:S(2)}) collective-permute-start(bf16[512,256]{1,0:T(8,128)(2,1)S(1)} %project_far.1.refs_0_.refs_1_), channel_id=1, source_target_pairs={{0,8},{2,10},{4,12},{6,14},{8,0},{10,2},{12,4},{14,6},{1,9},{3,11}... | collective-permute-start | bytes 786440 | tf_op jit(solution)/shard_map/ppermute | solution.py:476
  57.7 1.2 collective-permute-start.13
  58.8 2.9 %collective-permute-done.15.refs_3_ = bf16[512,256]{1,0:T(8,128)(2,1)S(1)} collective-permute-done((bf16[512,256]{1,0:T(8,128)(2,1)S(1)}, bf16[512,256]{1,0:T(8,128)(2,1)S(1)}, u32[]{:S(2)}, u32[]{:S(2)}) %collective-permute-start.15) | collective-permute-done | bytes 262176 | tf_op jit(solution)/shard_map/ppermute | solution.py:477
  61.7 6.6 %collective-permute-done.14.refs_2_ = bf16[512,256]{1,0:T(8,128)(2,1)S(1)} collective-permute-done((bf16[512,256]{1,0:T(8,128)(2,1)S(1)}, bf16[512,256]{1,0:T(8,128)(2,1)S(1)}, u32[]{:S(2)}, u32[]{:S(2)}) %collective-permute-start.14) | collective-permute-done | bytes 262176 | tf_op jit(solution)/shard_map/ppermute | solution.py:476
  68.3 0.1 relay.2.after.mine
  68.4 2.3 %collective-permute-start.16 = (bf16[4,512,256]{2,1,0:T(8,128)(2,1)S(1)}, bf16[4,512,256]{2,1,0:T(8,128)(2,1)S(1)}, u32[]{:S(2)}, u32[]{:S(2)}) collective-permute-start(bf16[4,512,256]{2,1,0:T(8,128)(2,1)S(1)} %relay.2.after.mine), channel_id=1, source_target_pairs={{0,2},{2,0},{4,6},{6,4},{8,10},{10,8},{12,14},{14,12},{1,3},{3,1},... | collective-permute-start | bytes 3145736 | tf_op jit(solution)/shard_map/ppermute | solution.py:481
  70.7 2.3 %collective-permute-done.16.after.far_theirs = bf16[4,512,256]{2,1,0:T(8,128)(2,1)S(1)} collective-permute-done((bf16[4,512,256]{2,1,0:T(8,128)(2,1)S(1)}, bf16[4,512,256]{2,1,0:T(8,128)(2,1)S(1)}, u32[]{:S(2)}, u32[]{:S(2)}) %collective-permute-start.16) | collective-permute-done | bytes 1048608 | tf_op jit(solution)/shard_map/ppermute | solution.py:481
  73.0 1.0 copy-done.2
  74.0 4.5 %all-to-all-done.arrived = bf16[32,64,256]{2,1,0:T(8,128)(2,1)} async-done(((bf16[32,64,256]{2,1,0:T(8,128)(2,1)}), bf16[32,64,256]{2,1,0:T(8,128)(2,1)}, u32[]{:S(2)}, u32[]{:S(2)}) %all-to-all-start) | async-done | bytes 1048608 | tf_op jit(solution)/shard_map/all_to_all | solution.py:515
  78.4 1.2 %copy-done.3 = bf16[4,512,256]{2,1,0:T(8,128)(2,1)S(1)} copy-done((bf16[4,512,256]{2,1,0:T(8,128)(2,1)S(1)}, bf16[4,512,256]{2,1,0:T(8,128)(2,1)}, u32[]{:S(2)}) %copy-start.3) | copy-done | bytes 1048600
  79.7 1.3 %unpack.1.after.refs_0_ = bf16[704,256]{1,0:T(8,128)(2,1)S(1)} custom-call(s32[16,11]{1,0:T(8,128)S(1)} %bitcast.20, bf16[32,64,256]{2,1,0:T(8,128)(2,1)} %all-to-all-done.arrived, bf16[4,512,256]{2,1,0:T(8,128)(2,1)S(1)} %copy-done.3), custom_call_target="tpu_custom_call" | custom-call | bytes 1048576 | tf_op jit(solution)/shard_map/unpack/pallas_call | solution.py:100
  81.0 1.3 %collective-permute-start.19 = (bf16[704,256]{1,0:T(8,128)(2,1)S(1)}, bf16[704,256]{1,0:T(8,128)(2,1)}, u32[]{:S(2)}, u32[]{:S(2)}) collective-permute-start(bf16[704,256]{1,0:T(8,128)(2,1)S(1)} %unpack.1.after.refs_0_), channel_id=1, source_target_pairs={{0,4},{2,6},{4,8},{6,10},{8,12},{10,14},{12,0},{14,2},{1,5},{3,7},... | collective-permute-start | bytes 1081352 | tf_op jit(solution)/shard_map/ppermute | solution.py:477
  82.3 2.5 %collective-permute-start.18 = (bf16[704,256]{1,0:T(8,128)(2,1)S(1)}, bf16[704,256]{1,0:T(8,128)(2,1)}, u32[]{:S(2)}, u32[]{:S(2)}) collective-permute-start(bf16[704,256]{1,0:T(8,128)(2,1)S(1)} %unpack.1.after.refs_0_), channel_id=1, source_target_pairs={{0,8},{2,10},{4,12},{6,14},{8,0},{10,2},{12,4},{14,6},{1,9},{3,11}... | collective-permute-start | bytes 1081352 | tf_op jit(solution)/shard_map/ppermute | solution.py:476
  84.7 1.1 collective-permute-start.17
  85.9 1.2 %copy-done.1 = bf16[2,1,128,2048]{3,2,1,0:T(8,128)(2,1)S(1)} copy-done((bf16[2,1,128,2048]{3,2,1,0:T(8,128)(2,1)S(1)}, bf16[2,1,128,2048]{3,2,1,0:T(8,128)(2,1)}, u32[]{:S(2)}) %copy-start.1) | copy-done | bytes 1048600
  87.1 0.5 prepare.1
  87.6 0.7 copy-done.4
  88.3 4.4 %attend_new.1 = (bf16[128,2,512]{2,1,0:T(2,128)(2,1)}, f32[4,8,1024]{2,1,0:T(8,128)S(1)}, f32[4,8,1024]{2,1,0:T(8,128)S(1)}, f32[4,128,1024]{2,1,0:T(8,128)S(1)}) custom-call(s32[1024]{0:T(1024)S(1)} %bitcast.22, bf16[4,128,1024]{2,1,0:T(8,128)(2,1)S(1)} %get-tuple-element.18.rows, f32[4,256,128]{2,1,0:T(8,128)S(1)} %get-tuple-element.19.bias, ...), custom_call_target="tpu_custom_call" | custom-call | flops 2000000000 | bytes 6291456 | tf_op jit(solution)/shard_map/attend_new/pallas_call | solution.py:389
  92.7 3.3 %collective-permute-done.18.refs_2_ = bf16[704,256]{1,0:T(8,128)(2,1)} collective-permute-done((bf16[704,256]{1,0:T(8,128)(2,1)S(1)}, bf16[704,256]{1,0:T(8,128)(2,1)}, u32[]{:S(2)}, u32[]{:S(2)}) %collective-permute-start.18) | collective-permute-done | bytes 360480 | tf_op jit(solution)/shard_map/ppermute | solution.py:476
  96.1 1.1 collective-permute-done.17.refs_1_
  97.2 1.3 %relay.3.mine = bf16[4,704,256]{2,1,0:T(8,128)(2,1)S(1)} custom-call(bf16[704,256]{1,0:T(8,128)(2,1)S(1)} %unpack.1.after.refs_0_, bf16[704,256]{1,0:T(8,128)(2,1)} %collective-permute-done.17.refs_1_, bf16[704,256]{1,0:T(8,128)(2,1)} %collective-permute-done.18.refs_2_, bf16[704,256]{1,0:T(8,128)(2,1)} %collective-permute-done.19.refs_3_, ...), custom_call_target="tpu_custom_call" | custom-call | bytes 2097152 | tf_op jit(solution)/shard_map/relay/pallas_call | solution.py:253
  98.5 4.8 %collective-permute-start.20 = (bf16[4,704,256]{2,1,0:T(8,128)(2,1)S(1)}, bf16[4,704,256]{2,1,0:T(8,128)(2,1)S(1)}, u32[]{:S(2)}, u32[]{:S(2)}) collective-permute-start(bf16[4,704,256]{2,1,0:T(8,128)(2,1)S(1)} %relay.3.mine), channel_id=1, source_target_pairs={{0,2},{2,0},{4,6},{6,4},{8,10},{10,8},{12,14},{14,12},{1,3},{3,1},... | collective-permute-start | bytes 4325384 | tf_op jit(solution)/shard_map/ppermute | solution.py:481
  103.3 2.8 %collective-permute-done.20.theirs = bf16[4,704,256]{2,1,0:T(8,128)(2,1)S(1)} collective-permute-done((bf16[4,704,256]{2,1,0:T(8,128)(2,1)S(1)}, bf16[4,704,256]{2,1,0:T(8,128)(2,1)S(1)}, u32[]{:S(2)}, u32[]{:S(2)}) %collective-permute-start.20) | collective-permute-done | bytes 1441824 | tf_op jit(solution)/shard_map/ppermute | solution.py:481
  106.2 10.5 %attend_pages.1 = bf16[2,128,2048]{2,1,0:T(8,128)(2,1)} custom-call(s32[16,11]{1,0:T(8,128)S(1)} %copy-done.8, s32[1024]{0:T(1024)S(1)} %bitcast.23, s32[1,128]{1,0:T(1,128)S(1)} %constant_dynamic-slice_fusion.2.query_seg, bf16[4,128,1024]{2,1,0:T(8,128)(2,1)S(1)} %get-tuple-element.18.rows, f32[4,8,1024]{2,1,0:T(8,128)S(1)} %get-tuple-element.20.refs_4_.peak_in, ...), custom_call_target="tpu_custom_call" | custom-call | flops 3000000000 | bytes 6291456 | tf_op jit(solution)/shard_map/attend_pages/pallas_call | solution.py:454
  (33 shorter events, 0.2 us)
Async XLA Ops:
  0.6 4.2 %copy-start = (bf16[8,128,2,512]{3,2,1,0:T(2,128)(2,1)S(1)}, bf16[8,128,2,512]{3,2,1,0:T(2,128)(2,1)}, u32[]{:S(2)}) copy-start(bf16[8,128,2,512]{3,2,1,0:T(2,128)(2,1)} %param.11) | copy-start | bytes 6291460
  0.6 12.9 %copy-start.5 = (bf16[1,128,2048]{2,1,0:T(8,128)(2,1)S(1)}, bf16[1,128,2048]{2,1,0:T(8,128)(2,1)}, u32[]{:S(2)}) copy-start(bf16[1,128,2048]{2,1,0:T(8,128)(2,1)} %param.8) | copy-start | bytes 1572868
  0.7 27.0 %copy-start.6 = (s32[16,11]{1,0:T(8,128)S(1)}, s32[16,11]{1,0:T(8,128)}, u32[]{:S(2)}) copy-start(s32[16,11]{1,0:T(8,128)} %pages.1) | copy-start | bytes 2116
  1.9 4.6 %collective-permute-start.3 = (bf16[256,256]{1,0:T(8,128)(2,1)S(1)}, bf16[256,256]{1,0:T(8,128)(2,1)S(1)}, u32[]{:S(2)}, u32[]{:S(2)}) collective-permute-start(bf16[256,256]{1,0:T(8,128)(2,1)S(1)} %bitcast.14), channel_id=1, source_target_pairs={{0,16},{16,0},{32,48},{48,32},{64,80},{80,64},{96,112},{112,96},{1... | collective-permute-start | bytes 393224 | tf_op jit(solution)/shard_map/ppermute | solution.py:491
  7.1 10.7 %collective-permute-start.7 = (bf16[512,256]{1,0:T(8,128)(2,1)S(1)}, bf16[512,256]{1,0:T(8,128)(2,1)S(1)}, u32[]{:S(2)}, u32[]{:S(2)}) collective-permute-start(bf16[512,256]{1,0:T(8,128)(2,1)S(1)} %order.1.refs_0_), channel_id=1, source_target_pairs={{0,224},{16,240},{32,0},{48,16},{64,32},{80,48},{96,64},{112,80},{... | collective-permute-start | bytes 786440 | tf_op jit(solution)/shard_map/ppermute | solution.py:501
  13.5 7.5 %collective-permute-start.4 = (bf16[512,256]{1,0:T(8,128)(2,1)S(1)}, bf16[512,256]{1,0:T(8,128)(2,1)S(1)}, u32[]{:S(2)}, u32[]{:S(2)}) collective-permute-start(bf16[512,256]{1,0:T(8,128)(2,1)S(1)} %order.1.refs_0_), channel_id=1, source_target_pairs={{0,32},{16,48},{32,64},{48,80},{64,96},{80,112},{96,128},{112,144}... | collective-permute-start | bytes 786440 | tf_op jit(solution)/shard_map/ppermute | solution.py:500
  13.5 16.6 %collective-permute-start.2 = (bf16[128,2048]{1,0:T(8,128)(2,1)S(1)}, bf16[128,2048]{1,0:T(8,128)(2,1)S(1)}, u32[]{:S(2)}, u32[]{:S(2)}) collective-permute-start(bf16[128,2048]{1,0:T(8,128)(2,1)S(1)} %stage.1.sent), channel_id=1, source_target_pairs={{0,5},{1,4},{2,7},{3,6},{4,1},{5,0},{6,3},{7,2},{8,13},{9,12},{10,... | collective-permute-start | bytes 1572872 | tf_op jit(solution)/shard_map/ppermute | solution.py:506
  17.5 23.6 %collective-permute-start.1 = (bf16[128,2048]{1,0:T(8,128)(2,1)S(1)}, bf16[128,2048]{1,0:T(8,128)(2,1)S(1)}, u32[]{:S(2)}, u32[]{:S(2)}) collective-permute-start(bf16[128,2048]{1,0:T(8,128)(2,1)S(1)} %stage.1.sent), channel_id=1, source_target_pairs={{0,1},{1,0},{2,3},{3,2},{4,5},{5,4},{6,7},{7,6},{8,9},{9,8},{10,11... | collective-permute-start | bytes 1572872 | tf_op jit(solution)/shard_map/ppermute | solution.py:505
  17.5 23.6 %collective-permute-start = (bf16[128,2048]{1,0:T(8,128)(2,1)S(1)}, bf16[128,2048]{1,0:T(8,128)(2,1)S(1)}, u32[]{:S(2)}, u32[]{:S(2)}) collective-permute-start(bf16[128,2048]{1,0:T(8,128)(2,1)S(1)} %bitcast.17), channel_id=1, source_target_pairs={{0,4},{2,6},{4,0},{6,2},{8,12},{10,14},{12,8},{14,10},{1,5},{3,7},... | collective-permute-start | bytes 1572872 | tf_op jit(solution)/shard_map/ppermute | solution.py:504
  17.9 6.4 %collective-permute-start.8 = (bf16[512,256]{1,0:T(8,128)(2,1)S(1)}, bf16[512,256]{1,0:T(8,128)(2,1)S(1)}, u32[]{:S(2)}, u32[]{:S(2)}) collective-permute-start(bf16[512,256]{1,0:T(8,128)(2,1)S(1)} %collective-permute-done.7.refs_2_), channel_id=1, source_target_pairs={{0,224},{16,240},{32,0},{48,16},{64,32},{80,48},{96,64},{112,80},{... | collective-permute-start | bytes 786440 | tf_op jit(solution)/shard_map/ppermute | solution.py:501
  21.0 6.7 %collective-permute-start.5 = (bf16[512,256]{1,0:T(8,128)(2,1)S(1)}, bf16[512,256]{1,0:T(8,128)(2,1)S(1)}, u32[]{:S(2)}, u32[]{:S(2)}) collective-permute-start(bf16[512,256]{1,0:T(8,128)(2,1)S(1)} %collective-permute-done.4.refs_0_.refs_1_), channel_id=1, source_target_pairs={{0,32},{16,48},{32,64},{48,80},{64,96},{80,112},{96,128},{112,144}... | collective-permute-start | bytes 786440 | tf_op jit(solution)/shard_map/ppermute | solution.py:500
  24.3 16.8 %collective-permute-start.9 = (bf16[512,256]{1,0:T(8,128)(2,1)S(1)}, bf16[512,256]{1,0:T(8,128)(2,1)S(1)}, u32[]{:S(2)}, u32[]{:S(2)}) collective-permute-start(bf16[512,256]{1,0:T(8,128)(2,1)S(1)} %collective-permute-done.8.refs_4_), channel_id=1, source_target_pairs={{0,224},{16,240},{32,0},{48,16},{64,32},{80,48},{96,64},{112,80},{... | collective-permute-start | bytes 786440 | tf_op jit(solution)/shard_map/ppermute | solution.py:501
  27.7 13.4 %collective-permute-start.6 = (bf16[512,256]{1,0:T(8,128)(2,1)S(1)}, bf16[512,256]{1,0:T(8,128)(2,1)S(1)}, u32[]{:S(2)}, u32[]{:S(2)}) collective-permute-start(bf16[512,256]{1,0:T(8,128)(2,1)S(1)} %collective-permute-done.5.refs_3_), channel_id=1, source_target_pairs={{0,32},{16,48},{32,64},{48,80},{64,96},{80,112},{96,128},{112,144}... | collective-permute-start | bytes 786440 | tf_op jit(solution)/shard_map/ppermute | solution.py:500
  41.3 4.6 %collective-permute-start.10 = (bf16[4,128,2048]{2,1,0:T(8,128)(2,1)S(1)}, bf16[4,128,2048]{2,1,0:T(8,128)(2,1)S(1)}, u32[]{:S(2)}, u32[]{:S(2)}) collective-permute-start(bf16[4,128,2048]{2,1,0:T(8,128)(2,1)S(1)} %get-tuple-element.13.mine), channel_id=1, source_target_pairs={{0,2},{2,0},{4,6},{6,4},{8,10},{10,8},{12,14},{14,12},{1,3},{3,1},... | collective-permute-start | bytes 6291464 | tf_op jit(solution)/shard_map/ppermute | solution.py:511
  42.1 6.3 %collective-permute-start.11 = (bf16[256,256]{1,0:T(8,128)(2,1)S(1)}, bf16[256,256]{1,0:T(8,128)(2,1)S(1)}, u32[]{:S(2)}, u32[]{:S(2)}) collective-permute-start(bf16[256,256]{1,0:T(8,128)(2,1)S(1)} %get-tuple-element.16), channel_id=1, source_target_pairs={{0,32},{16,48},{32,64},{48,80},{64,96},{80,112},{96,128},{112,144}... | collective-permute-start | bytes 393224 | tf_op jit(solution)/shard_map/ppermute | solution.py:509
  42.1 6.3 %collective-permute-start.12 = (bf16[256,256]{1,0:T(8,128)(2,1)S(1)}, bf16[256,256]{1,0:T(8,128)(2,1)S(1)}, u32[]{:S(2)}, u32[]{:S(2)}) collective-permute-start(bf16[256,256]{1,0:T(8,128)(2,1)S(1)} %get-tuple-element.17), channel_id=1, source_target_pairs={{0,224},{16,240},{32,0},{48,16},{64,32},{80,48},{96,64},{112,80},{... | collective-permute-start | bytes 393224 | tf_op jit(solution)/shard_map/ppermute | solution.py:510
  48.7 29.7 %all-to-all-start = ((bf16[32,64,256]{2,1,0:T(8,128)(2,1)}), bf16[32,64,256]{2,1,0:T(8,128)(2,1)}, u32[]{:S(2)}, u32[]{:S(2)}) async-start(bf16[32,64,256]{2,1,0:T(8,128)(2,1)} %hold.1), calls=%async_computation | async-start | bytes 2097152 | tf_op jit(solution)/shard_map/all_to_all | solution.py:515
  53.7 32.2 %copy-start.7 = (s32[1,1024]{1,0:T(1,128)S(1)}, s32[1,1024]{1,0:T(1,128)}, u32[]{:S(2)}) copy-start(s32[1,1024]{1,0:T(1,128)} %param.15) | copy-start | bytes 12292
  53.7 8.0 %collective-permute-start.15 = (bf16[512,256]{1,0:T(8,128)(2,1)S(1)}, bf16[512,256]{1,0:T(8,128)(2,1)S(1)}, u32[]{:S(2)}, u32[]{:S(2)}) collective-permute-start(bf16[512,256]{1,0:T(8,128)(2,1)S(1)} %project_far.1.refs_0_.refs_1_), channel_id=1, source_target_pairs={{0,4},{2,6},{4,8},{6,10},{8,12},{10,14},{12,0},{14,2},{1,5},{3,7},... | collective-permute-start | bytes 786440 | tf_op jit(solution)/shard_map/ppermute | solution.py:477
  55.2 13.1 %collective-permute-start.14 = (bf16[512,256]{1,0:T(8,128)(2,1)S(1)}, bf16[512,256]{1,0:T(8,128)(2,1)S(1)}, u32[]{:S(2)}, u32[]{:S(2)}) collective-permute-start(bf16[512,256]{1,0:T(8,128)(2,1)S(1)} %project_far.1.refs_0_.refs_1_), channel_id=1, source_target_pairs={{0,8},{2,10},{4,12},{6,14},{8,0},{10,2},{12,4},{14,6},{1,9},{3,11}... | collective-permute-start | bytes 786440 | tf_op jit(solution)/shard_map/ppermute | solution.py:476
  57.7 10.6 %collective-permute-start.13 = (bf16[512,256]{1,0:T(8,128)(2,1)S(1)}, bf16[512,256]{1,0:T(8,128)(2,1)S(1)}, u32[]{:S(2)}, u32[]{:S(2)}) collective-permute-start(bf16[512,256]{1,0:T(8,128)(2,1)S(1)} %project_far.1.refs_0_.refs_1_), channel_id=1, source_target_pairs={{0,12},{2,14},{4,0},{6,2},{8,4},{10,6},{12,8},{14,10},{1,13},{3,15... | collective-permute-start | bytes 786440 | tf_op jit(solution)/shard_map/ppermute | solution.py:475
  68.4 4.6 %collective-permute-start.16 = (bf16[4,512,256]{2,1,0:T(8,128)(2,1)S(1)}, bf16[4,512,256]{2,1,0:T(8,128)(2,1)S(1)}, u32[]{:S(2)}, u32[]{:S(2)}) collective-permute-start(bf16[4,512,256]{2,1,0:T(8,128)(2,1)S(1)} %relay.2.after.mine), channel_id=1, source_target_pairs={{0,2},{2,0},{4,6},{6,4},{8,10},{10,8},{12,14},{14,12},{1,3},{3,1},... | collective-permute-start | bytes 3145736 | tf_op jit(solution)/shard_map/ppermute | solution.py:481
  73.0 1.0 copy-start.2
  78.4 1.2 %copy-start.3 = (bf16[4,512,256]{2,1,0:T(8,128)(2,1)S(1)}, bf16[4,512,256]{2,1,0:T(8,128)(2,1)}, u32[]{:S(2)}) copy-start(bf16[4,512,256]{2,1,0:T(8,128)(2,1)} %copy-done.2) | copy-start | bytes 3145732
  81.0 11.7 %collective-permute-start.19 = (bf16[704,256]{1,0:T(8,128)(2,1)S(1)}, bf16[704,256]{1,0:T(8,128)(2,1)}, u32[]{:S(2)}, u32[]{:S(2)}) collective-permute-start(bf16[704,256]{1,0:T(8,128)(2,1)S(1)} %unpack.1.after.refs_0_), channel_id=1, source_target_pairs={{0,4},{2,6},{4,8},{6,10},{8,12},{10,14},{12,0},{14,2},{1,5},{3,7},... | collective-permute-start | bytes 1081352 | tf_op jit(solution)/shard_map/ppermute | solution.py:477
  82.3 13.8 %collective-permute-start.18 = (bf16[704,256]{1,0:T(8,128)(2,1)S(1)}, bf16[704,256]{1,0:T(8,128)(2,1)}, u32[]{:S(2)}, u32[]{:S(2)}) collective-permute-start(bf16[704,256]{1,0:T(8,128)(2,1)S(1)} %unpack.1.after.refs_0_), channel_id=1, source_target_pairs={{0,8},{2,10},{4,12},{6,14},{8,0},{10,2},{12,4},{14,6},{1,9},{3,11}... | collective-permute-start | bytes 1081352 | tf_op jit(solution)/shard_map/ppermute | solution.py:476
  84.7 12.4 %collective-permute-start.17 = (bf16[704,256]{1,0:T(8,128)(2,1)S(1)}, bf16[704,256]{1,0:T(8,128)(2,1)}, u32[]{:S(2)}, u32[]{:S(2)}) collective-permute-start(bf16[704,256]{1,0:T(8,128)(2,1)S(1)} %unpack.1.after.refs_0_), channel_id=1, source_target_pairs={{0,12},{2,14},{4,0},{6,2},{8,4},{10,6},{12,8},{14,10},{1,13},{3,15... | collective-permute-start | bytes 1081352 | tf_op jit(solution)/shard_map/ppermute | solution.py:475
  85.9 1.2 %copy-start.1 = (bf16[2,1,128,2048]{3,2,1,0:T(8,128)(2,1)S(1)}, bf16[2,1,128,2048]{3,2,1,0:T(8,128)(2,1)}, u32[]{:S(2)}) copy-start(bf16[2,1,128,2048]{3,2,1,0:T(8,128)(2,1)} %param.10) | copy-start | bytes 3145732
  87.1 1.2 %copy-start.4 = (bf16[4,512,256]{2,1,0:T(8,128)(2,1)S(1)}, bf16[4,512,256]{2,1,0:T(8,128)(2,1)}, u32[]{:S(2)}) copy-start(bf16[4,512,256]{2,1,0:T(8,128)(2,1)} %copy-done.2) | copy-start | bytes 3145732
  92.7 13.5 %copy-start.8 = (s32[16,11]{1,0:T(8,128)S(1)}, s32[16,11]{1,0:T(8,128)}, u32[]{:S(2)}) copy-start(s32[16,11]{1,0:T(8,128)} %requests.1) | copy-start | bytes 2116
  98.5 7.7 %collective-permute-start.20 = (bf16[4,704,256]{2,1,0:T(8,128)(2,1)S(1)}, bf16[4,704,256]{2,1,0:T(8,128)(2,1)S(1)}, u32[]{:S(2)}, u32[]{:S(2)}) collective-permute-start(bf16[4,704,256]{2,1,0:T(8,128)(2,1)S(1)} %relay.3.mine), channel_id=1, source_target_pairs={{0,2},{2,0},{4,6},{6,4},{8,10},{10,8},{12,14},{14,12},{1,3},{3,1},... | collective-permute-start | bytes 4325384 | tf_op jit(solution)/shard_map/ppermute | solution.py:481
